TPU v7x, 32 devices: a whole 2x2x4 slice. The times are simulated.
32 devices in a mesh: seq: 4 (over y, x), ctx: 8 (over z, core).
Axes of the slice: x: 2, y: 2, z: 4, core: 2. Of those that a mesh axis runs over, the one named last changes fastest.
Arguments:
- tokens: bfloat16 [4096, 1024], P(('seq', 'ctx')), may hold values from -6 to 6
- cotangent: bfloat16 [4096, 1024], P(('seq', 'ctx')), may hold values from -6 to 6
- gain_input: bfloat16 [1024], P('seq'), may hold values from 0.5 to 1.5
- w_query: bfloat16 [1024, 512], P('seq'), may hold values from -0.1875 to 0.1875
- key_weight: bfloat16 [1024, 128], P('seq'), may hold values from -0.1875 to 0.1875
- value_weight: bfloat16 [1024, 128], P('seq'), may hold values from -0.1875 to 0.1875
- w_mixin: bfloat16 [1024, 3352], P('seq'), may hold values from -0.1875 to 0.1875
- conv_taps: bfloat16 [4, 1792], P(None, 'seq'), may hold values from -3 to 3
- conv_bias: bfloat16 [1792], P('seq'), may hold values from -3 to 3
- step_offset: float32 [24], replicated, may hold values from -1 to 1
- decay_rate: float32 [24], replicated, may hold values from 0.0001953125 to 0.06
- skip_gain: float32 [24], replicated, may hold values from 0.5 to 1.5
- gain_mixer: bfloat16 [1536], P('seq'), may hold values from 0.5 to 1.5
- w_mixout: bfloat16 [1536, 1024], P('seq'), may hold values from -0.15625 to 0.15625
- w_attnout: bfloat16 [512, 1024], P('seq'), may hold values from -2 to 2
- gain_feed: bfloat16 [1024], P('seq'), may hold values from 0.5 to 1.5
- w_gate: bfloat16 [1024, 2048], P('seq'), may hold values from -0.1875 to 0.1875
- w_up: bfloat16 [1024, 2048], P('seq'), may hold values from -0.1875 to 0.1875
- w_down: bfloat16 [2048, 1024], P('seq'), may hold values from -0.125 to 0.125
Outputs:
- layer_out: bfloat16 [4096, 1024], P(('seq', 'ctx'))
- grad_tokens: float32 [4096, 1024], P(('seq', 'ctx'))
- grad_normin: float32 [1024], P('seq')
- grad_query: float32 [1024, 512], P('seq')
- grad_key: float32 [1024, 128], P('seq')
- grad_value: float32 [1024, 128], P('seq')
- grad_mixin: float32 [1024, 3352], P('seq')
- grad_taps: float32 [4, 1792], P(None, 'seq')
- grad_convbias: float32 [1792], P('seq')
- grad_offset: float32 [24], replicated
- grad_rate: float32 [24], replicated
- grad_skip: float32 [24], replicated
- grad_normmix: float32 [1536], P('seq')
- grad_mixout: float32 [1536, 1024], P('seq')
- grad_attnout: float32 [512, 1024], P('seq')
- grad_normffn: float32 [1024], P('seq')
- grad_gate: float32 [1024, 2048], P('seq')
- grad_up: float32 [1024, 2048], P('seq')
- grad_down: float32 [2048, 1024], P('seq')
All inputs are finite; a program needn't handle non-finite values.
Results may differ from a plain program's by a relative error of at most 0.017.
Values may be sent and summed in bfloat16 or wider, within the bound.
No kernel may reach another device: no remote copies, remote signals or barrier semaphores. Data moves between devices by JAX's collectives and lax.ppermute only.
A program may use at most 256 MiB of HBM per device.

v0:
```python
import jax
import jax.numpy as jnp
from jax import lax
from jax.sharding import PartitionSpec as P

QUERY_HEADS = 8
VALUE_HEADS = 2
HEAD_SIZE = 64
MH = 24
MP = 64
NS = 128
KC = 4


norm_epsilon = 1e-06
rope_base = 100000000000.0
highest = lax.Precision.HIGHEST


def from_behind(value, axis, steps):
    count = lax.axis_size(axis)
    initial, last = (max(0, -steps), min(count, count - steps))
    return lax.ppermute(value, axis, [(source, source + steps) for source in range(initial, last)])


def entering(value, axis, join, neutral):
    place = lax.axis_index(axis)
    gathered = jax.tree.map(
        lambda a, kind: lax.all_gather(a.astype(kind), axis), value, (jnp.bfloat16, jnp.bfloat16)
    )
    state = jax.tree.map(lambda a, e: jnp.zeros_like(a) + jnp.asarray(e, a.dtype), value, neutral)

    def one(turn, state):
        return join(
            state,
            jax.tree.map(
                lambda a, own: lax.dynamic_index_in_dim(a, turn, 0, False).astype(own.dtype),
                gathered,
                value,
            ),
        )

    return lax.fori_loop(0, place, one, state)


def entering_2(value, axis, join, neutral):
    count = lax.axis_size(axis)
    place = lax.axis_index(axis)
    ahead = count - 1 - place
    gathered = jax.tree.map(
        lambda a, kind: lax.all_gather(a.astype(kind), axis),
        value,
        jax.tree.map(lambda a: jnp.bfloat16 if a.dtype == jnp.float32 else a.dtype, value),
    )
    state = jax.tree.map(lambda a, e: jnp.zeros_like(a) + jnp.asarray(e, a.dtype), value, neutral)

    def one(turn, state):
        source = count - 1 - turn
        return join(
            state,
            jax.tree.map(
                lambda a, own: lax.dynamic_index_in_dim(a, source, 0, False).astype(own.dtype),
                gathered,
                value,
            ),
        )

    return lax.fori_loop(0, ahead, one, state)


def rms_scale(signal, gain_vec):
    return (
        signal
        * lax.rsqrt(jnp.mean(signal * signal, axis=-1, keepdims=True) + norm_epsilon)
        * gain_vec
    )


def rotary_apply(head_rows, token_positions):
    half_dim = head_rows.shape[-1] // 2
    frequency = rope_base ** (
        -(jnp.arange(half_dim, dtype=jnp.float32) * 2.0 / head_rows.shape[-1])
    )
    angles = token_positions.astype(jnp.float32)[:, None] * frequency[None, :]
    cosine = jnp.cos(angles)[:, None, :]
    sine_part = jnp.sin(angles)[:, None, :]
    lower_half = head_rows[..., :half_dim]
    upper_half = head_rows[..., half_dim:]
    return jnp.concatenate(
        [
            lower_half * cosine - upper_half * sine_part,
            upper_half * cosine + lower_half * sine_part,
        ],
        axis=-1,
    )


def conv_mix(extended, taps, shift):
    sequence_length = extended.shape[0] - taps.shape[0] + 1
    summed = shift[None, :] + jnp.zeros((sequence_length, taps.shape[1]), jnp.float32)
    for tap_index in range(taps.shape[0]):
        summed = (
            summed + taps[tap_index][None, :] * extended[tap_index : tap_index + sequence_length]
        )
    return jax.nn.silu(summed)


def ssm_part(mixed, raw_steps, offset, rates, skip_gain, inner_width):
    head_count = raw_steps.shape[1]
    state_size = (mixed.shape[1] - inner_width) // 2
    sequence_length = mixed.shape[0]
    head_input = mixed[:, :inner_width].reshape(
        sequence_length, head_count, inner_width // head_count
    )
    state_in = mixed[:, inner_width : inner_width + state_size]
    state_out = mixed[:, inner_width + state_size :]
    step_sizes = jax.nn.softplus(raw_steps + offset[None, :])
    log_decay = -step_sizes * rates[None, :]
    cumulated = jnp.cumsum(log_decay, axis=0)
    causal = (
        jnp.arange(sequence_length, dtype=jnp.int32)[:, None]
        >= jnp.arange(sequence_length, dtype=jnp.int32)[None, :]
    )
    log_gaps = cumulated.T[:, :, None] - cumulated.T[:, None, :]
    weights = jnp.where(causal[None], jnp.exp(jnp.where(causal[None], log_gaps, 0.0)), 0.0)
    intersection = jnp.dot(state_out, state_in.T, precision=highest)
    mixing = weights * intersection[None] * step_sizes.T[:, None, :]
    within = jnp.einsum("hts,shp->thp", mixing, head_input, precision=highest)
    out_zero = within + skip_gain[None, :, None] * head_input
    tail_weight = jnp.exp(cumulated[-1][None, :] - cumulated) * step_sizes
    local_state = jnp.einsum("sh,shp,sn->hpn", tail_weight, head_input, state_in, precision=highest)
    return (out_zero, local_state, jnp.exp(cumulated[-1]), state_out, cumulated)


def finish(out_zero, state_out, cumulated, start_state, gate_z, gain_vec):
    across = (
        jnp.einsum("tn,hpn->thp", state_out, start_state, precision=highest)
        * jnp.exp(cumulated)[:, :, None]
    )
    whole = out_zero + across
    gated = whole.reshape(whole.shape[0], -1) * jax.nn.silu(gate_z)
    return rms_scale(gated, gain_vec)


def chain(earlier, later):
    return (earlier[0] * later[0], later[0][:, None, None] * earlier[1] + later[1])


def attend(query_rows, kv_rows, query_pos):
    total_keys = kv_rows.shape[0]
    block = min(512, total_keys)
    kv_heads = query_rows.shape[0]
    head_dim = query_rows.shape[2]
    scale = head_dim ** (-0.5)

    def block_scores(block_index):
        kv_piece = lax.dynamic_slice_in_dim(kv_rows, block_index * block, block, 0).reshape(
            block, 2, kv_heads, head_dim
        )
        scores = (
            jnp.einsum(
                "hrd,khd->hrk", query_rows, kv_piece[:, 0], preferred_element_type=jnp.float32
            )
            * scale
        )
        allowed = (block_index * block + jnp.arange(block, dtype=jnp.int32))[None, :] <= query_pos[
            :, None
        ]
        return (kv_piece, scores, allowed)

    def total_step(carry, block_index):
        running_max, denominator = carry
        kv_piece, scores, allowed = block_scores(block_index)
        masked = jnp.where(allowed[None], scores, -1e30)
        new_max = jnp.maximum(running_max, jnp.max(masked, axis=-1))
        expanded = jnp.where(allowed[None], jnp.exp(masked - new_max[..., None]), 0.0)
        denominator = denominator * jnp.exp(running_max - new_max) + jnp.sum(expanded, axis=-1)
        return ((new_max, denominator), None)

    rows_all = query_rows.shape[1]
    block_ids = jnp.arange(total_keys // block, dtype=jnp.int32)
    initial = (
        jnp.full((kv_heads, rows_all), -1e30, jnp.float32),
        jnp.zeros((kv_heads, rows_all), jnp.float32),
    )
    totals, unused = lax.scan(total_step, initial, block_ids)
    log_total = totals[0] + jnp.log(totals[1])

    def value_step(accumulated, block_index):
        kv_piece, scores, allowed = block_scores(block_index)
        prob_low = jnp.where(
            allowed[None],
            jnp.exp(jnp.where(allowed[None], scores, 0.0) - log_total[..., None]),
            0.0,
        ).astype(jnp.bfloat16)
        accumulated = accumulated + jnp.einsum(
            "hrk,khd->hrd", prob_low, kv_piece[:, 1], preferred_element_type=jnp.float32
        )
        return (accumulated, None)

    out_full, unused = lax.scan(value_step, jnp.zeros(query_rows.shape, jnp.float32), block_ids)
    return (out_full, log_total)


def attend_back(query_rows, kv_rows, grad_out, out_full, log_total, query_pos):
    total_keys = kv_rows.shape[0]
    block = min(512, total_keys)
    kv_heads = query_rows.shape[0]
    head_dim = query_rows.shape[2]
    scale = head_dim ** (-0.5)
    grad_wide = grad_out.astype(jnp.float32)
    row_delta = jnp.sum(grad_wide * out_full, axis=-1)

    def step(query_grads_rows, block_index):
        kv_piece = lax.dynamic_slice_in_dim(kv_rows, block_index * block, block, 0).reshape(
            block, 2, kv_heads, head_dim
        )
        key_row_block = kv_piece[:, 0]
        value_rows = kv_piece[:, 1]
        scores = (
            jnp.einsum(
                "hrd,khd->hrk", query_rows, key_row_block, preferred_element_type=jnp.float32
            )
            * scale
        )
        allowed = (block_index * block + jnp.arange(block, dtype=jnp.int32))[None, :] <= query_pos[
            :, None
        ]
        attn_prob = jnp.where(
            allowed[None],
            jnp.exp(jnp.where(allowed[None], scores, 0.0) - log_total[..., None]),
            0.0,
        )
        grad_prob = jnp.einsum(
            "hrd,khd->hrk", grad_out, value_rows, preferred_element_type=jnp.float32
        )
        grad_score = (attn_prob * (grad_prob - row_delta[..., None])).astype(jnp.bfloat16)
        query_grads_rows = (
            query_grads_rows
            + jnp.einsum(
                "hrk,khd->hrd", grad_score, key_row_block, preferred_element_type=jnp.float32
            )
            * scale
        )
        grad_keys = (
            jnp.einsum("hrk,hrd->khd", grad_score, query_rows, preferred_element_type=jnp.float32)
            * scale
        )
        grad_values = jnp.einsum(
            "hrk,hrd->khd",
            attn_prob.astype(jnp.bfloat16),
            grad_out,
            preferred_element_type=jnp.float32,
        )
        return (
            query_grads_rows,
            jnp.stack([grad_keys, grad_values], axis=1).reshape(block, 2 * kv_heads * head_dim),
        )

    query_grads_rows, key_value_grad = lax.scan(
        step,
        jnp.zeros(query_rows.shape, jnp.float32),
        jnp.arange(total_keys // block, dtype=jnp.int32),
    )
    return (query_grads_rows, key_value_grad.reshape(total_keys, 2 * kv_heads * head_dim))


def body(
    tokens,
    cotangent,
    gain_input,
    w_query,
    key_weight,
    value_weight,
    w_mixin,
    conv_taps,
    conv_bias,
    step_offset,
    decay_rate,
    skip_gain,
    gain_mixer,
    w_mixout,
    w_attnout,
    gain_feed,
    w_gate,
    w_up,
    w_down,
):
    single_float = jnp.float32
    brain_float_half = jnp.bfloat16
    count_rows = tokens.shape[0]
    sequence_group = QUERY_HEADS // VALUE_HEADS
    inner_width = MH * MP
    conv_width = inner_width + 2 * NS
    first_row = lax.axis_index("ctx") * count_rows
    token_positions = first_row + jnp.arange(count_rows, dtype=jnp.int32)
    query_pos = first_row + jnp.arange(sequence_group * count_rows, dtype=jnp.int32) % count_rows
    mixer_full = (
        lax.all_gather(gain_input, "seq", axis=0, tiled=True),
        lax.all_gather(w_query, "seq", axis=0, tiled=True),
        lax.all_gather(key_weight, "seq", axis=0, tiled=True),
        lax.all_gather(value_weight, "seq", axis=0, tiled=True),
        lax.all_gather(w_mixin, "seq", axis=0, tiled=True),
        lax.all_gather(conv_taps, "seq", axis=1, tiled=True),
        lax.all_gather(conv_bias, "seq", axis=0, tiled=True),
        lax.all_gather(gain_mixer, "seq", axis=0, tiled=True),
        lax.all_gather(w_mixout, "seq", axis=0, tiled=True),
        lax.all_gather(w_attnout, "seq", axis=0, tiled=True),
    )
    feed_full = (
        lax.all_gather(gain_feed, "seq", axis=0, tiled=True),
        lax.all_gather(w_gate, "seq", axis=0, tiled=True),
        lax.all_gather(w_up, "seq", axis=0, tiled=True),
        lax.all_gather(w_down, "seq", axis=0, tiled=True),
    )
    (
        full_gin,
        full_query,
        key_full_matrix,
        full_value,
        full_mixin,
        full_taps,
        full_cbias,
        full_gmix,
        full_mixout,
        full_attnout,
    ) = mixer_full
    full_gfeed, full_gate, full_up, full_down = feed_full
    inputs = tokens.astype(single_float)
    gin_f = full_gin.astype(single_float)
    normed_batch = rms_scale(inputs, gin_f).astype(brain_float_half)
    q_pre = jnp.dot(normed_batch, full_query, preferred_element_type=single_float).reshape(
        count_rows, QUERY_HEADS, HEAD_SIZE
    )
    key_prerotary = jnp.dot(
        normed_batch, key_full_matrix, preferred_element_type=single_float
    ).reshape(count_rows, VALUE_HEADS, HEAD_SIZE)
    value_prerotary = jnp.dot(normed_batch, full_value, preferred_element_type=single_float)
    mix_pre = jnp.dot(normed_batch, full_mixin, preferred_element_type=single_float)
    query_lowered = rotary_apply(q_pre, token_positions).astype(brain_float_half)
    key_lowered = rotary_apply(key_prerotary, token_positions).astype(brain_float_half)
    key_value_local = jnp.concatenate(
        [
            key_lowered.reshape(count_rows, VALUE_HEADS * HEAD_SIZE),
            value_prerotary.astype(brain_float_half),
        ],
        axis=1,
    )
    kv_all = lax.all_gather(key_value_local, "ctx", axis=0, tiled=True)
    gate_z = mix_pre[:, :inner_width]
    conv_low = mix_pre[:, inner_width : inner_width + conv_width].astype(brain_float_half)
    raw_steps = mix_pre[:, inner_width + conv_width :]
    edge = from_behind(conv_low[count_rows - (KC - 1) :], "ctx", 1)
    extended = jnp.concatenate([edge, conv_low], axis=0).astype(single_float)
    taps_f = full_taps.astype(single_float)
    cbias_f = full_cbias.astype(single_float)
    gmix_f = full_gmix.astype(single_float)
    mixed = conv_mix(extended, taps_f, cbias_f)
    out_zero, local_state, decay, state_out, cumulated = ssm_part(
        mixed, raw_steps, step_offset, decay_rate, skip_gain, inner_width
    )
    decay_prefix, start_state = entering(
        (decay, local_state), "ctx", chain, (jnp.ones_like(decay), jnp.zeros_like(local_state))
    )
    mix_b = finish(out_zero, state_out, cumulated, start_state, gate_z, gmix_f).astype(
        brain_float_half
    )
    query_rows = (
        query_lowered.reshape(count_rows, VALUE_HEADS, sequence_group, HEAD_SIZE)
        .transpose(1, 2, 0, 3)
        .reshape(VALUE_HEADS, sequence_group * count_rows, HEAD_SIZE)
    )
    out_full, log_total = attend(query_rows, kv_all, query_pos)
    attn_b = (
        out_full.astype(brain_float_half)
        .reshape(VALUE_HEADS, sequence_group, count_rows, HEAD_SIZE)
        .transpose(2, 0, 1, 3)
        .reshape(count_rows, QUERY_HEADS * HEAD_SIZE)
    )
    residual = (
        inputs
        + jnp.dot(attn_b, full_attnout, preferred_element_type=single_float)
        + jnp.dot(mix_b, full_mixout, preferred_element_type=single_float)
    )
    gfeed_f = full_gfeed.astype(single_float)
    feed_b = rms_scale(residual, gfeed_f).astype(brain_float_half)
    gate = jnp.dot(feed_b, full_gate, preferred_element_type=single_float)
    up_part = jnp.dot(feed_b, full_up, preferred_element_type=single_float)
    hidden_b = (jax.nn.silu(gate) * up_part).astype(brain_float_half)
    layer_out = (
        residual + jnp.dot(hidden_b, full_down, preferred_element_type=single_float)
    ).astype(brain_float_half)
    gathered = (
        lax.all_gather(gain_input, "seq", axis=0, tiled=True),
        lax.all_gather(w_query, "seq", axis=0, tiled=True),
        lax.all_gather(key_weight, "seq", axis=0, tiled=True),
        lax.all_gather(value_weight, "seq", axis=0, tiled=True),
        lax.all_gather(w_mixin, "seq", axis=0, tiled=True),
        lax.all_gather(conv_taps, "seq", axis=1, tiled=True),
        lax.all_gather(conv_bias, "seq", axis=0, tiled=True),
        lax.all_gather(gain_mixer, "seq", axis=0, tiled=True),
        lax.all_gather(w_mixout, "seq", axis=0, tiled=True),
        lax.all_gather(w_attnout, "seq", axis=0, tiled=True),
        lax.all_gather(gain_feed, "seq", axis=0, tiled=True),
        lax.all_gather(w_gate, "seq", axis=0, tiled=True),
        lax.all_gather(w_up, "seq", axis=0, tiled=True),
        lax.all_gather(w_down, "seq", axis=0, tiled=True),
    )
    (
        full_gin,
        full_query,
        key_full_matrix,
        full_value,
        full_mixin,
        full_taps,
        full_cbias,
        full_gmix,
        full_mixout,
        full_attnout,
        full_gfeed,
        full_gate,
        full_up,
        full_down,
    ) = gathered
    gin_f = full_gin.astype(single_float)
    taps_f = full_taps.astype(single_float)
    cbias_f = full_cbias.astype(single_float)
    gmix_f = full_gmix.astype(single_float)
    gfeed_f = full_gfeed.astype(single_float)
    grad_down = jnp.dot(hidden_b.T, cotangent, preferred_element_type=single_float)
    grad_hidden = jnp.dot(cotangent, full_down.T, preferred_element_type=single_float)
    unused, pull_gate = jax.vjp(lambda gate_in, up_in: jax.nn.silu(gate_in) * up_in, gate, up_part)
    d_gate, d_up = pull_gate(grad_hidden)
    d_gate_b = d_gate.astype(brain_float_half)
    d_up_b = d_up.astype(brain_float_half)
    grad_gate = jnp.dot(feed_b.T, d_gate_b, preferred_element_type=single_float)
    grad_upw = jnp.dot(feed_b.T, d_up_b, preferred_element_type=single_float)
    d_feed = jnp.dot(d_gate_b, full_gate.T, preferred_element_type=single_float) + jnp.dot(
        d_up_b, full_up.T, preferred_element_type=single_float
    )
    unused, pull_feed = jax.vjp(rms_scale, residual, gfeed_f)
    d_res_norm, d_gfeed = pull_feed(d_feed)
    grad_res = cotangent.astype(single_float) + d_res_norm
    res_b = grad_res.astype(brain_float_half)
    grad_attnout = jnp.dot(attn_b.T, res_b, preferred_element_type=single_float)
    grad_mixout = jnp.dot(mix_b.T, res_b, preferred_element_type=single_float)
    attention_grad_bias = jnp.dot(
        res_b, full_attnout.T, preferred_element_type=single_float
    ).astype(brain_float_half)
    d_mix = jnp.dot(res_b, full_mixout.T, preferred_element_type=single_float)
    grad_out = (
        attention_grad_bias.reshape(count_rows, VALUE_HEADS, sequence_group, HEAD_SIZE)
        .transpose(1, 2, 0, 3)
        .reshape(VALUE_HEADS, sequence_group * count_rows, HEAD_SIZE)
    )
    query_grads_rows, grad_kv_all = attend_back(
        query_rows, kv_all, grad_out, out_full, log_total, query_pos
    )
    key_value_grad = lax.psum_scatter(
        grad_kv_all.astype(jnp.bfloat16), "ctx", scatter_dimension=0, tiled=True
    ).astype(jnp.float32)

    def whole(
        extended_in,
        gate_in,
        steps_in,
        taps_in,
        shift_in,
        offset_in,
        rates_in,
        skip_in,
        gain_in,
        start_in,
    ):
        mixed_in = conv_mix(extended_in, taps_in, shift_in)
        zero_part, own_state, own_decay, out_state, cumul_in = ssm_part(
            mixed_in, steps_in, offset_in, rates_in, skip_in, inner_width
        )
        return (
            finish(zero_part, out_state, cumul_in, start_in, gate_in, gain_in),
            own_state,
            own_decay,
        )

    unused, pull_mix = jax.vjp(
        whole,
        extended,
        gate_z,
        raw_steps,
        taps_f,
        cbias_f,
        step_offset,
        decay_rate,
        skip_gain,
        gmix_f,
        start_state,
    )
    direct = pull_mix((d_mix, jnp.zeros_like(local_state), jnp.zeros_like(decay)))
    decay_later, later_grad = entering_2(
        (decay, direct[9]), "ctx", chain, (jnp.ones_like(decay), jnp.zeros_like(local_state))
    )
    decay_grad = jnp.sum(later_grad * start_state, axis=(1, 2))
    mixer_back = pull_mix((d_mix, later_grad, decay_grad))
    d_extended = mixer_back[0]
    edge_back = from_behind(d_extended[: KC - 1], "ctx", -1)
    d_conv = d_extended[KC - 1 :]
    d_conv = jnp.concatenate(
        [d_conv[: count_rows - (KC - 1)], d_conv[count_rows - (KC - 1) :] + edge_back], axis=0
    )
    d_mixpre = jnp.concatenate([mixer_back[1], d_conv, mixer_back[2]], axis=1).astype(
        brain_float_half
    )
    d_queries = (
        query_grads_rows.reshape(VALUE_HEADS, sequence_group, count_rows, HEAD_SIZE)
        .transpose(2, 0, 1, 3)
        .reshape(count_rows, QUERY_HEADS, HEAD_SIZE)
    )
    unused, pull_query = jax.vjp(lambda heads_in: rotary_apply(heads_in, token_positions), q_pre)
    d_qpre = (
        pull_query(d_queries)[0]
        .reshape(count_rows, QUERY_HEADS * HEAD_SIZE)
        .astype(brain_float_half)
    )
    unused, fetch_key = jax.vjp(
        lambda heads_in: rotary_apply(heads_in, token_positions), key_prerotary
    )
    d_kpre = (
        fetch_key(
            key_value_grad[:, : VALUE_HEADS * HEAD_SIZE].reshape(count_rows, VALUE_HEADS, HEAD_SIZE)
        )[0]
        .reshape(count_rows, VALUE_HEADS * HEAD_SIZE)
        .astype(brain_float_half)
    )
    grad_value_prerotary = key_value_grad[:, VALUE_HEADS * HEAD_SIZE :].astype(brain_float_half)
    grad_query = jnp.dot(normed_batch.T, d_qpre, preferred_element_type=single_float)
    grad_key = jnp.dot(normed_batch.T, d_kpre, preferred_element_type=single_float)
    grad_value = jnp.dot(normed_batch.T, grad_value_prerotary, preferred_element_type=single_float)
    grad_mixin = jnp.dot(normed_batch.T, d_mixpre, preferred_element_type=single_float)
    d_normed = jnp.dot(d_qpre, full_query.T, preferred_element_type=single_float) + jnp.dot(
        d_kpre, key_full_matrix.T, preferred_element_type=single_float
    )
    d_normed = (
        d_normed
        + jnp.dot(grad_value_prerotary, full_value.T, preferred_element_type=single_float)
        + jnp.dot(d_mixpre, full_mixin.T, preferred_element_type=single_float)
    )
    unused, pull_input = jax.vjp(rms_scale, inputs, gin_f)
    d_inputs, d_gin = pull_input(d_normed)
    grad_tokens = grad_res + d_inputs
    head_sums = lax.psum((mixer_back[5], mixer_back[6], mixer_back[7]), ("seq", "ctx"))
    shares = (
        lax.psum_scatter(d_gin, ("seq", "ctx"), scatter_dimension=0, tiled=True),
        lax.psum_scatter(grad_query, ("seq", "ctx"), scatter_dimension=0, tiled=True),
        lax.psum_scatter(grad_key, ("seq", "ctx"), scatter_dimension=0, tiled=True),
        lax.psum_scatter(grad_value, ("seq", "ctx"), scatter_dimension=0, tiled=True),
        lax.psum_scatter(grad_mixin, ("seq", "ctx"), scatter_dimension=0, tiled=True),
        lax.psum_scatter(mixer_back[3], ("seq", "ctx"), scatter_dimension=1, tiled=True),
        lax.psum_scatter(mixer_back[4], ("seq", "ctx"), scatter_dimension=0, tiled=True),
        lax.psum_scatter(mixer_back[8], ("seq", "ctx"), scatter_dimension=0, tiled=True),
        lax.psum_scatter(grad_mixout, ("seq", "ctx"), scatter_dimension=0, tiled=True),
        lax.psum_scatter(grad_attnout, ("seq", "ctx"), scatter_dimension=0, tiled=True),
        lax.psum_scatter(d_gfeed, ("seq", "ctx"), scatter_dimension=0, tiled=True),
        lax.psum_scatter(grad_gate, ("seq", "ctx"), scatter_dimension=0, tiled=True),
        lax.psum_scatter(grad_upw, ("seq", "ctx"), scatter_dimension=0, tiled=True),
        lax.psum_scatter(grad_down, ("seq", "ctx"), scatter_dimension=0, tiled=True),
    )
    owned = (
        lax.all_gather(shares[0].astype(jnp.bfloat16), "ctx", axis=0, tiled=True).astype(
            jnp.float32
        ),
        lax.all_gather(shares[1].astype(jnp.bfloat16), "ctx", axis=0, tiled=True).astype(
            jnp.float32
        ),
        lax.all_gather(shares[2].astype(jnp.bfloat16), "ctx", axis=0, tiled=True).astype(
            jnp.float32
        ),
        lax.all_gather(shares[3].astype(jnp.bfloat16), "ctx", axis=0, tiled=True).astype(
            jnp.float32
        ),
        lax.all_gather(shares[4].astype(jnp.bfloat16), "ctx", axis=0, tiled=True).astype(
            jnp.float32
        ),
        lax.all_gather(shares[5].astype(jnp.bfloat16), "ctx", axis=1, tiled=True).astype(
            jnp.float32
        ),
        lax.all_gather(shares[6].astype(jnp.bfloat16), "ctx", axis=0, tiled=True).astype(
            jnp.float32
        ),
        lax.all_gather(shares[7].astype(jnp.bfloat16), "ctx", axis=0, tiled=True).astype(
            jnp.float32
        ),
        lax.all_gather(shares[8].astype(jnp.bfloat16), "ctx", axis=0, tiled=True).astype(
            jnp.float32
        ),
        lax.all_gather(shares[9].astype(jnp.bfloat16), "ctx", axis=0, tiled=True).astype(
            jnp.float32
        ),
        lax.all_gather(shares[10].astype(jnp.bfloat16), "ctx", axis=0, tiled=True).astype(
            jnp.float32
        ),
        lax.all_gather(shares[11].astype(jnp.bfloat16), "ctx", axis=0, tiled=True).astype(
            jnp.float32
        ),
        lax.all_gather(shares[12].astype(jnp.bfloat16), "ctx", axis=0, tiled=True).astype(
            jnp.float32
        ),
        lax.all_gather(shares[13].astype(jnp.bfloat16), "ctx", axis=0, tiled=True).astype(
            jnp.float32
        ),
    )
    return (
        layer_out,
        grad_tokens,
        owned[0],
        owned[1],
        owned[2],
        owned[3],
        owned[4],
        owned[5],
        owned[6],
        head_sums[0],
        head_sums[1],
        head_sums[2],
        owned[7],
        owned[8],
        owned[9],
        owned[10],
        owned[11],
        owned[12],
        owned[13],
    )


def solution(mesh):
    in_specs = (
        P(("seq", "ctx"), None),
        P(("seq", "ctx"), None),
        P("seq"),
        P("seq", None),
        P("seq", None),
        P("seq", None),
        P("seq", None),
        P(None, "seq"),
        P("seq"),
        P(),
        P(),
        P(),
        P("seq"),
        P("seq", None),
        P("seq", None),
        P("seq"),
        P("seq", None),
        P("seq", None),
        P("seq", None),
    )
    out_specs = (
        P(("seq", "ctx"), None),
        P(("seq", "ctx"), None),
        P("seq"),
        P("seq", None),
        P("seq", None),
        P("seq", None),
        P("seq", None),
        P(None, "seq"),
        P("seq"),
        P(),
        P(),
        P(),
        P("seq"),
        P("seq", None),
        P("seq", None),
        P("seq"),
        P("seq", None),
        P("seq", None),
        P("seq", None),
    )
    return jax.shard_map(body, mesh=mesh, in_specs=in_specs, out_specs=out_specs, check_vma=False)
```

profile of v0, /device:TPU:1, one launch (start us, length us, event | category | flops | bytes accessed | tf_op | source)
XLA Modules:
  0.0 1878.7 jit_solution(13342443123548646205)
XLA Ops:
  10.2 6.9 all-gather.2
  17.1 6.1 all-gather.3
  25.5 7.2 all-reduce.17
  33.3 53.7 %all-gather.26.cloned.1.call-done = bf16[1024,3352]{0,1:T(8,128)(2,1)} async-done(((bf16[256,3352]{0,1:T(8,128)(2,1)}), bf16[1024,3352]{0,1:T(8,128)(2,1)}) %all-gather.26.cloned.1.call-update) | async-done | bytes 6864912 | tf_op jit(solution)/shard_map/all_gather | solution.py:303
  86.9 5.4 fusion.166
  108.8 9.0 all_gather.120
  118.2 6.5 all_gather.121
  125.2 17.8 all_gather.122
  143.0 5.9 all-gather.5
  149.6 5.1 all-gather.6
  157.9 15.8 while.65
  174.4 9.3 while.66
  187.3 14.2 all-gather.4
  215.1 15.2 all-gather.28.cloned.1.call-done
  233.9 50.8 %all-gather.30.cloned.1.call-done = bf16[1024,2048]{1,0:T(8,128)(2,1)} async-done(((bf16[256,2048]{1,0:T(8,128)(2,1)}), bf16[1024,2048]{1,0:T(8,128)(2,1)}) %all-gather.30.cloned.1.call-update) | async-done | bytes 4194320 | tf_op jit(solution)/shard_map/all_gather | solution.py:312
  288.7 50.6 %all-gather.32.cloned.1.call-done = bf16[1024,2048]{1,0:T(8,128)(2,1)} async-done(((bf16[256,2048]{1,0:T(8,128)(2,1)}), bf16[1024,2048]{1,0:T(8,128)(2,1)}) %all-gather.32.cloned.1.call-update) | async-done | bytes 4194320 | tf_op jit(solution)/shard_map/all_gather | solution.py:313
  343.3 50.6 %all-gather.34.cloned.1.call-done = bf16[2048,1024]{1,0:T(8,128)(2,1)} async-done(((bf16[512,1024]{1,0:T(8,128)(2,1)}), bf16[2048,1024]{1,0:T(8,128)(2,1)}) %all-gather.34.cloned.1.call-update) | async-done | bytes 4194320 | tf_op jit(solution)/shard_map/all_gather | solution.py:314
  393.9 5.6 multiply_convert_fusion
  417.7 20.0 %while.67 = (s32[]{:T(128)}, f32[2,512,64]{1,2,0:T(8,128)}, bf16[2,512,256]{2,1,0:T(8,128)(2,1)}, s32[2]{0:T(128)S(1)}, bf16[1024,256]{0,1:T(8,128)(2,1)}, /*ind...) while((s32[]{:T(128)}, f32[2,512,64]{1,2,0:T(8,128)}, ...), condition=%wide.region_15.16_spmd.clone, body=%wide.region_14.15_spmd.clone.sunk | while | flops 340463616 | bytes 15369129 | solution.py:260
  437.8 5.7 fusion.172
  444.6 4.5 fusion.173
  450.3 4.5 fusion.174
  457.2 5.5 fusion.74
  470.1 11.8 while.64
  496.9 4.5 collective-permute-start.1
  509.7 7.2 fusion.108
  529.0 104.7 %reduce-scatter.26.cloned.1.call-done = f32[32,2048]{1,0:T(8,128)} async-done(((f32[1024,2048]{1,0:T(8,128)}), f32[32,2048]{1,0:T(8,128)}) %reduce-scatter.26.cloned.1.call-update) | async-done | bytes 262160 | tf_op jit(solution)/shard_map/reduce_scatter | solution.py:563
  635.4 150.8 %reduce-scatter.28.cloned.1.call-done = f32[32,2048]{1,0:T(8,128)} async-done(((f32[1024,2048]{1,0:T(8,128)}), f32[32,2048]{1,0:T(8,128)}) %reduce-scatter.28.cloned.1.call-update) | async-done | bytes 262160 | tf_op jit(solution)/shard_map/reduce_scatter | solution.py:564
  787.9 150.4 %reduce-scatter.30.cloned.1.call-done = f32[64,1024]{1,0:T(8,128)} async-done(((f32[2048,1024]{1,0:T(8,128)}), f32[64,1024]{1,0:T(8,128)}) %reduce-scatter.30.cloned.1.call-update) | async-done | bytes 262160 | tf_op jit(solution)/shard_map/reduce_scatter | solution.py:565
  947.0 161.2 %reduce-scatter.20.cloned.1.call-done = f32[32,3352]{1,0:T(8,128)} async-done(((f32[1024,3352]{1,0:T(8,128)}), f32[32,3352]{1,0:T(8,128)}) %reduce-scatter.20.cloned.1.call-update) | async-done | bytes 429072 | tf_op jit(solution)/shard_map/reduce_scatter | solution.py:556
  1110.5 129.1 %reduce-scatter.16.cloned.1.call-done = f32[32,128]{1,0:T(8,128)} async-done(((f32[1024,128]{1,0:T(8,128)}), f32[32,128]{1,0:T(8,128)}) %reduce-scatter.16.cloned.1.call-update) | async-done | bytes 16400 | tf_op jit(solution)/shard_map/reduce_scatter | solution.py:554
  1240.3 19.7 %all_gather.141 = bf16[256,128]{1,0:T(8,128)(2,1)S(1)} all-gather(bf16[32,128]{1,0:T(8,128)(2,1)S(1)} %convert_element_type.285), channel_id=1, replica_groups=mesh['seq'=4,'ctx'=8] {'ctx'}, dimensions={0}, use_global_device_ids=true | all-gather | bytes 73728 | tf_op jit(solution)/shard_map/all_gather | solution.py:574
  1260.7 111.6 %reduce-scatter.18.cloned.1.call-done = f32[32,128]{1,0:T(8,128)} async-done(((f32[1024,128]{1,0:T(8,128)}), f32[32,128]{1,0:T(8,128)}) %reduce-scatter.18.cloned.1.call-update) | async-done | bytes 16400 | tf_op jit(solution)/shard_map/reduce_scatter | solution.py:555
  1373.0 19.7 %all_gather.142 = bf16[256,128]{1,0:T(8,128)(2,1)S(1)} all-gather(bf16[32,128]{1,0:T(8,128)(2,1)S(1)} %convert_element_type.287), channel_id=1, replica_groups=mesh['seq'=4,'ctx'=8] {'ctx'}, dimensions={0}, use_global_device_ids=true | all-gather | bytes 73728 | tf_op jit(solution)/shard_map/all_gather | solution.py:577
  1393.3 115.4 %reduce-scatter.14.cloned.1.call-done = f32[32,512]{1,0:T(8,128)} async-done(((f32[1024,512]{1,0:T(8,128)}), f32[32,512]{1,0:T(8,128)}) %reduce-scatter.14.cloned.1.call-update) | async-done | bytes 65552 | tf_op jit(solution)/shard_map/reduce_scatter | solution.py:553
  1509.6 19.7 %all_gather.140 = bf16[256,512]{1,0:T(8,128)(2,1)S(1)} all-gather(bf16[32,512]{1,0:T(8,128)(2,1)S(1)} %convert_element_type.283), channel_id=1, replica_groups=mesh['seq'=4,'ctx'=8] {'ctx'}, dimensions={0}, use_global_device_ids=true | all-gather | bytes 294912 | tf_op jit(solution)/shard_map/all_gather | solution.py:571
  1530.2 115.0 %reduce-scatter.24.cloned.1.call-done = f32[16,1024]{1,0:T(8,128)} async-done(((f32[512,1024]{1,0:T(8,128)}), f32[16,1024]{1,0:T(8,128)}) %reduce-scatter.24.cloned.1.call-update) | async-done | bytes 65552 | tf_op jit(solution)/shard_map/reduce_scatter | solution.py:561
  1646.1 19.7 %all_gather.148 = bf16[128,1024]{1,0:T(8,128)(2,1)S(1)} all-gather(bf16[16,1024]{1,0:T(8,128)(2,1)S(1)} %convert_element_type.299), channel_id=1, replica_groups=mesh['seq'=4,'ctx'=8] {'ctx'}, dimensions={0}, use_global_device_ids=true | all-gather | bytes 294912 | tf_op jit(solution)/shard_map/all_gather | solution.py:595
  1667.4 4.6 fusion.109
  1672.9 38.2 %all-reduce.27 = (bf16[1024]{0:T(1024)(128)(2,1)S(1)}, bf16[4,1792]{1,0:T(4,128)(2,1)S(1)}, bf16[1792]{0:T(1024)(128)(2,1)S(1)}, f32[24]{0:T(128)}, f32[24]{0:T(...) all-reduce(f32[1024]{0:T(1024)S(1)} %get-tuple-element.551, ...), channel_id=5, replica_groups=mesh['seq'=4,'ctx'=8] {'seq','ctx'}, use_global_device_ids=true, to_apply=%region_30.31.clone | all-reduce | flops 12616 | bytes 75840
  1711.1 11.2 all-gather.7
  1724.1 13.2 all-reduce.28
  1740.8 26.1 %reduce-scatter.22.cloned.1.call-done = f32[48,1024]{1,0:T(8,128)} async-done(((f32[1536,1024]{1,0:T(8,128)}), f32[48,1024]{1,0:T(8,128)}) %reduce-scatter.22.cloned.1.call-update) | async-done | bytes 196624 | tf_op jit(solution)/shard_map/reduce_scatter | solution.py:560
  1767.8 19.0 %all_gather.147 = bf16[384,1024]{1,0:T(8,128)(2,1)S(1)} all-gather(bf16[48,1024]{1,0:T(8,128)(2,1)S(1)} %convert_element_type.297), channel_id=1, replica_groups=mesh['seq'=4,'ctx'=8] {'ctx'}, dimensions={0}, use_global_device_ids=true | all-gather | bytes 884736 | tf_op jit(solution)/shard_map/all_gather | solution.py:592
  1788.1 5.3 all-gather.38.cloned.1.call-done
  1796.2 20.4 %all-gather.40.cloned.1.call-done = bf16[256,2048]{1,0:T(8,128)(2,1)} async-done(((bf16[32,2048]{1,0:T(8,128)(2,1)}), bf16[256,2048]{1,0:T(8,128)(2,1)}) %all-gather.40.cloned.1.call-update) | async-done | bytes 1048592 | tf_op jit(solution)/shard_map/all_gather | solution.py:604
  1819.4 20.6 %all-gather.42.cloned.1.call-done = bf16[512,1024]{1,0:T(8,128)(2,1)} async-done(((bf16[64,1024]{1,0:T(8,128)(2,1)}), bf16[512,1024]{1,0:T(8,128)(2,1)}) %all-gather.42.cloned.1.call-update) | async-done | bytes 1048592 | tf_op jit(solution)/shard_map/all_gather | solution.py:607
  1842.8 24.9 %all-gather.36.cloned.1.call-done = bf16[256,3352]{1,0:T(8,128)(2,1)} async-done(((bf16[32,3352]{1,0:T(8,128)(2,1)}), bf16[256,3352]{1,0:T(8,128)(2,1)}) %all-gather.36.cloned.1.call-update) | async-done | bytes 1716240 | tf_op jit(solution)/shard_map/all_gather | solution.py:580
  (592 shorter events, 213.1 us)
Async XLA Ops:
  7.2 79.7 %all-gather.26.cloned.1.call-start = ((), (), s32[]{:S(2)}) async-start(), calls=%async_computation.12 | async-start | bytes 8581120 | tf_op jit(solution)/shard_map/all_gather | solution.py:303
  8.0 147.4 %all-gather.22.cloned.1.call-start = ((), (), s32[]{:S(2)}) async-start(), calls=%async_computation.10 | async-start | bytes 1310720 | tf_op jit(solution)/shard_map/all_gather | solution.py:300
  8.7 176.2 %all-gather.24.cloned.1.call-start = ((), (), s32[]{:S(2)}) async-start(), calls=%async_computation.11 | async-start | bytes 1310720 | tf_op jit(solution)/shard_map/all_gather | solution.py:308
  9.5 193.4 %all-gather.44.cloned.1.call-start = ((), (), s32[]{:S(2)}) async-start(), calls=%async_computation.31 | async-start | bytes 3538944 | tf_op jit(solution)/shard_map/all_gather | solution.py:29
  10.2 145.2 %copy-start.91 = (f32[128]{0:T(128)}, f32[128]{0:T(128)S(1)}, u32[]{:S(2)}) copy-start(f32[128]{0:T(128)S(1)} %fusion.137) | copy-start | bytes 1540
  24.0 75.2 %copy-start.77 = (f32[1792]{0:T(1024)}, f32[1792]{0:T(1024)S(1)}, u32[]{:S(2)}) copy-start(f32[1792]{0:T(1024)S(1)} %get-tuple-element.553) | copy-start | bytes 21508
  24.0 75.2 %copy-start.79 = (f32[1792]{0:T(1024)}, f32[1792]{0:T(1024)S(1)}, u32[]{:S(2)}) copy-start(f32[1792]{0:T(1024)S(1)} %get-tuple-element.554) | copy-start | bytes 21508
  24.0 75.2 %copy-start.81 = (f32[1792]{0:T(1024)}, f32[1792]{0:T(1024)S(1)}, u32[]{:S(2)}) copy-start(f32[1792]{0:T(1024)S(1)} %get-tuple-element.555) | copy-start | bytes 21508
  93.1 5.3 collective-permute-start
  105.4 124.9 %all-gather.28.cloned.1.call-start = ((), (), s32[]{:S(2)}) async-start(), calls=%async_computation.13 | async-start | bytes 3932160 | tf_op jit(solution)/shard_map/all_gather | solution.py:307
  106.0 178.7 %all-gather.30.cloned.1.call-start = ((), (), s32[]{:S(2)}) async-start(), calls=%async_computation.14 | async-start | bytes 5242880 | tf_op jit(solution)/shard_map/all_gather | solution.py:312
  106.6 232.7 %all-gather.32.cloned.1.call-start = ((), (), s32[]{:S(2)}) async-start(), calls=%async_computation.15 | async-start | bytes 5242880 | tf_op jit(solution)/shard_map/all_gather | solution.py:313
  107.4 286.5 %all-gather.34.cloned.1.call-start = ((), (), s32[]{:S(2)}) async-start(), calls=%async_computation.16 | async-start | bytes 5242880 | tf_op jit(solution)/shard_map/all_gather | solution.py:314
  108.1 361.9 %all-gather.46.cloned.1.call-start = ((), (), s32[]{:S(2)}) async-start(), calls=%async_computation.32 | async-start | bytes 3538944 | tf_op jit(solution)/shard_map/all_gather | solution.py:51
  215.1 191.4 %copy-start.3 = (f32[128,1536]{1,0:T(8,128)}, f32[128,1536]{1,0:T(8,128)S(1)}, u32[]{:S(2)}) copy-start(f32[128,1536]{1,0:T(8,128)S(1)} %get-tuple-element.643) | copy-start | bytes 2359300
  215.1 191.4 %copy-start.106 = (f32[128]{0:T(128)}, f32[128]{0:T(128)S(1)}, u32[]{:S(2)}) copy-start(f32[128]{0:T(128)S(1)} %fusion.138) | copy-start | bytes 1540
  233.0 171.2 %copy-start.5 = (f32[128,1024]{1,0:T(8,128)}, f32[128,1024]{1,0:T(8,128)S(1)}, u32[]{:S(2)}) copy-start(f32[128,1024]{1,0:T(8,128)S(1)} %get-tuple-element.681) | copy-start | bytes 1572868
  233.1 171.2 %copy-start.117 = (f32[128]{0:T(128)}, f32[128]{0:T(128)S(1)}, u32[]{:S(2)}) copy-start(f32[128]{0:T(128)S(1)} %fusion.139) | copy-start | bytes 1540
  414.0 102.9 %reduce-scatter.12.cloned.1.call-start = ((), (), s32[]{:S(2)}) async-start(), calls=%async_computation.17 | async-start | bytes 589824 | tf_op jit(solution)/shard_map/reduce_scatter | solution.py:459
  437.7 196.0 %reduce-scatter.26.cloned.1.call-start = ((), (), s32[]{:S(2)}) async-start(), calls=%async_computation.25 | async-start | bytes 8650752 | tf_op jit(solution)/shard_map/reduce_scatter | solution.py:563
  443.5 342.7 %reduce-scatter.28.cloned.1.call-start = ((), (), s32[]{:S(2)}) async-start(), calls=%async_computation.27 | async-start | bytes 8650752 | tf_op jit(solution)/shard_map/reduce_scatter | solution.py:564
  449.2 489.1 %reduce-scatter.30.cloned.1.call-start = ((), (), s32[]{:S(2)}) async-start(), calls=%async_computation.29 | async-start | bytes 8650752 | tf_op jit(solution)/shard_map/reduce_scatter | solution.py:565
  454.8 653.3 %reduce-scatter.20.cloned.1.call-start = ((), (), s32[]{:S(2)}) async-start(), calls=%async_computation.21 | async-start | bytes 14598144 | tf_op jit(solution)/shard_map/reduce_scatter | solution.py:556
  496.9 11.9 collective-permute-start.1
  516.8 722.8 %reduce-scatter.16.cloned.1.call-start = ((), (), s32[]{:S(2)}) async-start(), calls=%async_computation.19 | async-start | bytes 540672 | tf_op jit(solution)/shard_map/reduce_scatter | solution.py:554
  519.0 853.3 %reduce-scatter.18.cloned.1.call-start = ((), (), s32[]{:S(2)}) async-start(), calls=%async_computation.20 | async-start | bytes 540672 | tf_op jit(solution)/shard_map/reduce_scatter | solution.py:555
  520.9 987.8 %reduce-scatter.14.cloned.1.call-start = ((), (), s32[]{:S(2)}) async-start(), calls=%async_computation.18 | async-start | bytes 2162688 | tf_op jit(solution)/shard_map/reduce_scatter | solution.py:553
  523.0 1122.2 %reduce-scatter.24.cloned.1.call-start = ((), (), s32[]{:S(2)}) async-start(), calls=%async_computation.24 | async-start | bytes 2162688 | tf_op jit(solution)/shard_map/reduce_scatter | solution.py:561
  524.9 1242.0 %reduce-scatter.22.cloned.1.call-start = ((), (), s32[]{:S(2)}) async-start(), calls=%async_computation.23 | async-start | bytes 6488064 | tf_op jit(solution)/shard_map/reduce_scatter | solution.py:560
  528.9 411.1 %copy-start.138 = (u32[32]{0:T(128)S(1)}, u32[32]{0:T(128)}, u32[]{:S(2)}) copy-start(u32[32]{0:T(128)} %constant.225) | copy-start | bytes 388
  528.9 413.6 %copy-start.94 = (f32[1536]{0:T(1024)S(1)}, f32[1536]{0:T(1024)}, u32[]{:S(2)}) copy-start(f32[1536]{0:T(1024)} %get-tuple-element.637) | copy-start | bytes 18436
  528.9 414.4 %copy-start.6 = (f32[128,1024]{1,0:T(8,128)S(1)}, f32[128,1024]{1,0:T(8,128)}, u32[]{:S(2)}) copy-start(f32[128,1024]{1,0:T(8,128)} %copy-done.5) | copy-start | bytes 1572868
  528.9 1264.5 %all-gather.38.cloned.1.call-start = ((), (), s32[]{:S(2)}) async-start(), calls=%async_computation.26 | async-start | bytes 1179648 | tf_op jit(solution)/shard_map/all_gather | solution.py:601
  635.3 1181.3 %all-gather.40.cloned.1.call-start = ((), (), s32[]{:S(2)}) async-start(), calls=%async_computation.28 | async-start | bytes 1179648 | tf_op jit(solution)/shard_map/all_gather | solution.py:604
  787.8 1052.2 %all-gather.42.cloned.1.call-start = ((), (), s32[]{:S(2)}) async-start(), calls=%async_computation.30 | async-start | bytes 1179648 | tf_op jit(solution)/shard_map/all_gather | solution.py:607
  940.0 927.7 %all-gather.36.cloned.1.call-start = ((), (), s32[]{:S(2)}) async-start(), calls=%async_computation.22 | async-start | bytes 1990656 | tf_op jit(solution)/shard_map/all_gather | solution.py:580
  943.3 166.7 %copy-start.53 = (bf16[1024,128]{1,0:T(8,128)(2,1)S(1)}, bf16[1024,128]{1,0:T(8,128)(2,1)}, u32[]{:S(2)}) copy-start(bf16[1024,128]{1,0:T(8,128)(2,1)} %copy-done.52) | copy-start | bytes 786436
  943.3 166.9 %copy-start.55 = (bf16[1024,128]{1,0:T(8,128)(2,1)S(1)}, bf16[1024,128]{1,0:T(8,128)(2,1)}, u32[]{:S(2)}) copy-start(bf16[1024,128]{1,0:T(8,128)(2,1)} %copy-done.54) | copy-start | bytes 786436
  943.3 166.9 %copy-start.65 = (bf16[128,256]{1,0:T(8,128)(2,1)S(1)}, bf16[128,256]{1,0:T(8,128)(2,1)}, u32[]{:S(2)}) copy-start(bf16[128,256]{1,0:T(8,128)(2,1)} %reduce-scatter.12.cloned.1.call-done) | copy-start | bytes 196612
  1110.2 557.1 %copy-start.97 = (f32[1792]{0:T(1024)S(1)}, f32[1792]{0:T(1024)}, u32[]{:S(2)}) copy-start(f32[1792]{0:T(1024)} %get-tuple-element.541) | copy-start | bytes 21508
  1110.2 557.1 %copy-start.96 = (f32[1792]{0:T(1024)S(1)}, f32[1792]{0:T(1024)}, u32[]{:S(2)}) copy-start(f32[1792]{0:T(1024)} %get-tuple-element.540) | copy-start | bytes 21508
  1110.2 557.1 %copy-start.95 = (f32[1792]{0:T(1024)S(1)}, f32[1792]{0:T(1024)}, u32[]{:S(2)}) copy-start(f32[1792]{0:T(1024)} %get-tuple-element.539) | copy-start | bytes 21508
  1110.2 557.2 %copy-start.47 = (bf16[125,1792]{1,0:T(8,128)(2,1)S(1)}, bf16[125,1792]{1,0:T(8,128)(2,1)}, u32[]{:S(2)}) copy-start(bf16[125,1792]{1,0:T(8,128)(2,1)} %copy-done.46) | copy-start | bytes 1344004
  1110.2 557.2 %copy-start.49 = (bf16[128,1536]{1,0:T(8,128)(2,1)S(1)}, bf16[128,1536]{1,0:T(8,128)(2,1)}, u32[]{:S(2)}) copy-start(bf16[128,1536]{1,0:T(8,128)(2,1)} %get-tuple-element.654) | copy-start | bytes 1179652
  1110.3 557.2 %copy-start.69 = (bf16[128,24]{1,0:T(8,128)(2,1)S(1)}, bf16[128,24]{1,0:T(8,128)(2,1)}, u32[]{:S(2)}) copy-start(bf16[128,24]{1,0:T(8,128)(2,1)} %copy-done.68) | copy-start | bytes 18436
  1110.3 557.2 %copy-start.90 = (bf16[3,1792]{1,0:T(4,128)(2,1)S(1)}, bf16[3,1792]{1,0:T(4,128)(2,1)}, u32[]{:S(2)}) copy-start(bf16[3,1792]{1,0:T(4,128)(2,1)} %copy-done.89) | copy-start | bytes 32260
  1672.1 67.6 %copy-start.34 = (f32[128,1024]{1,0:T(8,128)S(1)}, f32[128,1024]{1,0:T(8,128)}, u32[]{:S(2)}) copy-start(f32[128,1024]{1,0:T(8,128)} %copy-done.33) | copy-start | bytes 1572868
  1672.1 67.6 %copy-start.42 = (bf16[128,1024]{1,0:T(8,128)(2,1)S(1)}, bf16[128,1024]{1,0:T(8,128)(2,1)}, u32[]{:S(2)}) copy-start(bf16[128,1024]{1,0:T(8,128)(2,1)} %param.30) | copy-start | bytes 786436
  (127 other events, 951.3 us)
Sparse Core Ops, SparseCore 0:
  9.9 76.9 all-gather.25
  88.8 27.3 all-gather.21
  118.0 27.3 all-gather.23
  147.4 38.6 all-gather.43
  187.8 42.4 all-gather.27
  232.0 52.6 all-gather.29
  286.6 52.6 all-gather.31
  341.2 52.6 all-gather.33
  414.1 38.6 all-gather.45
  455.5 26.1 reduce-scatter.11
  484.1 149.5 reduce-scatter.25
  635.9 150.1 reduce-scatter.27
  788.6 149.6 reduce-scatter.29
  945.2 162.9 reduce-scatter.19
  1110.9 128.6 reduce-scatter.15
  1242.3 129.9 reduce-scatter.17
  1375.0 133.6 reduce-scatter.13
  1511.4 133.7 reduce-scatter.23
  1651.8 115.0 reduce-scatter.21
  1768.9 24.5 all-gather.37
  1795.1 21.5 all-gather.39
  1818.2 21.7 all-gather.41
  1841.6 25.9 all-gather.35
where the time goes:
time: 1890 us; the launch traced here: 1880 us
  waiting for transfers between devices  1360 us (72%)
  blocking collectives  239 us (13%)
  matrix products  122 us (6%)
  other arithmetic  74.6 us (4%)
  local copies, waits for them, and re-layouts  48.2 us (3%)
  between operations  19.1 us (1%)
    reduce_scatter x1, waiting for transfers between devices, body(): lax.psum_scatter(grad_mixin, ('seq', 'ctx'), scatter_dimension=0, tiled=T...  161 us
    reduce_scatter x1, waiting for transfers between devices, body(): lax.psum_scatter(grad_upw, ('seq', 'ctx'), scatter_dimension=0, tiled=True)  151 us
    reduce_scatter x1, waiting for transfers between devices, body(): lax.psum_scatter(grad_down, ('seq', 'ctx'), scatter_dimension=0, tiled=True)  150 us
    reduce_scatter x1, waiting for transfers between devices, body(): lax.psum_scatter(grad_key, ('seq', 'ctx'), scatter_dimension=0, tiled=True)  129 us
    reduce_scatter x1, waiting for transfers between devices, body(): lax.psum_scatter(grad_query, ('seq', 'ctx'), scatter_dimension=0, tiled=T...  115 us
    reduce_scatter x1, waiting for transfers between devices, body(): lax.psum_scatter(grad_attnout, ('seq', 'ctx'), scatter_dimension=0, tiled...  115 us
    reduce_scatter x1, waiting for transfers between devices, body(): lax.psum_scatter(grad_value, ('seq', 'ctx'), scatter_dimension=0, tiled=T...  112 us
    reduce_scatter x1, waiting for transfers between devices, body(): lax.psum_scatter(grad_gate, ('seq', 'ctx'), scatter_dimension=0, tiled=True)  105 us
  transfers between devices with their start and end apart: 25, of which 18 were waited for; matrix products, arithmetic and copies ran while one was open for 11% of the time, Pallas kernels for 0%

commit v1 on v0

v1 whole, which is shorter than its diff:
```python
import jax
import jax.numpy as jnp
from jax import lax
from jax.sharding import PartitionSpec as P

QUERY_HEADS = 8
VALUE_HEADS = 2
HEAD_SIZE = 64
MH = 24
MP = 64
NS = 128
KC = 4
GROUP = QUERY_HEADS // VALUE_HEADS
INNER = MH * MP
CONVW = INNER + 2 * NS
QW = QUERY_HEADS * HEAD_SIZE
KW = VALUE_HEADS * HEAD_SIZE

norm_epsilon = 1e-06
rope_base = 100000000000.0
highest = lax.Precision.HIGHEST
f32 = jnp.float32
bf16 = jnp.bfloat16


def dot(a, b):
    return jnp.dot(a, b, preferred_element_type=f32)


def dot_nt(a, b):
    return lax.dot_general(a, b, (((1,), (1,)), ((), ())), preferred_element_type=f32)


def dot_tn(a, b):
    return lax.dot_general(a, b, (((0,), (0,)), ((), ())), preferred_element_type=f32)


def rms_scale(signal, gain_vec):
    return (
        signal
        * lax.rsqrt(jnp.mean(signal * signal, axis=-1, keepdims=True) + norm_epsilon)
        * gain_vec
    )


def rotary_apply(head_rows, cosine, sine):
    half_dim = head_rows.shape[-1] // 2
    lower = head_rows[..., :half_dim]
    upper = head_rows[..., half_dim:]
    return jnp.concatenate(
        [lower * cosine - upper * sine, upper * cosine + lower * sine], axis=-1
    )


def conv_mix(extended, taps, shift):
    rows = extended.shape[0] - KC + 1
    summed = shift[None, :]
    for tap in range(KC):
        summed = summed + taps[tap][None, :] * extended[tap : tap + rows]
    return jax.nn.silu(summed)


def swap_core(value):
    count = lax.axis_size("ctx")
    return lax.ppermute(value, "ctx", [(i, i ^ 1) for i in range(count)])


def chip_shift(value, steps, wrap):
    count = lax.axis_size("ctx")
    pairs = []
    for i in range(count):
        to = i + 2 * steps
        if wrap:
            pairs.append((i, to % count))
        elif 0 <= to < count:
            pairs.append((i, to))
    return lax.ppermute(value, "ctx", pairs)


def seq_swap(value, k):
    count = lax.axis_size("seq")
    return lax.ppermute(value, "seq", [(i, i ^ k) for i in range(count)])


def take_half(value, core):
    rows = value.shape[0] // 2
    return lax.dynamic_slice_in_dim(value, core * rows, rows, 0)


def gather_weight(local, core):
    own = lax.all_gather(take_half(local, core), "seq", axis=0, tiled=True)
    return own, swap_core(own)


def split_cols(x, seqs, core):
    rows, width = x.shape
    part = width // (2 * seqs)
    blocks = x.reshape(rows, seqs, 2, part)
    first, second = blocks[:, :, 0], blocks[:, :, 1]
    own = jnp.where(core == 0, first, second).reshape(rows, width // 2)
    other = jnp.where(core == 0, second, first).reshape(rows, width // 2)
    return own, other


def merge_cols(own, other, seqs, core):
    rows, half = own.shape
    a = own.reshape(rows, seqs, half // seqs)
    b = other.reshape(rows, seqs, half // seqs)
    first = jnp.where(core == 0, a, b)
    second = jnp.where(core == 0, b, a)
    return jnp.stack([first, second], axis=2).reshape(rows, 2 * half)


def times_weight(x, weight, seqs, core):
    own, other = split_cols(x, seqs, core)
    return dot(own, weight[0]) + dot(other, weight[1])


def times_weight_t(y, weight, seqs, core):
    return merge_cols(dot_nt(y, weight[0]), dot_nt(y, weight[1]), seqs, core)


def gather_rows(value, seqs):
    return jnp.concatenate([value] + [seq_swap(value, k) for k in range(1, seqs)], axis=0)


def send_blocks(blocks, place, seqs):
    parts = []
    for k in range(seqs):
        piece = lax.dynamic_index_in_dim(blocks, place ^ k, 1, False)
        parts.append(piece if k == 0 else seq_swap(piece, k))
    return jnp.concatenate(parts, axis=0)


def sum_over_ctx(grad, chips, chip, core):
    rows, cols = grad.shape
    halves = grad.reshape(2, rows // 2, cols)
    mine = lax.dynamic_index_in_dim(halves, core, 0, False)
    others = lax.dynamic_index_in_dim(halves, 1 - core, 0, False).astype(bf16)
    mine = mine + swap_core(others).astype(f32)
    shards = mine.reshape(chips, rows // (2 * chips), cols)
    total = lax.dynamic_index_in_dim(shards, chip, 0, False)
    for k in range(1, chips):
        piece = lax.dynamic_index_in_dim(shards, (chip + k) % chips, 0, False).astype(bf16)
        total = total + chip_shift(piece, k, True).astype(f32)
    total = total.astype(bf16)
    got = [total] + [chip_shift(total, k, True) for k in range(1, chips)]
    got = jnp.stack(got, axis=0)
    both = jnp.stack([got, swap_core(got)], axis=0)
    parts = []
    for half in range(2):
        for q in range(chips):
            parts.append(both[half ^ core, (chip - q) % chips])
    return jnp.concatenate(parts, axis=0)


def ctx_state(value, decays, chips, chip, core, later):
    half = MH // 2
    low = value.astype(bf16)
    mine = lax.dynamic_slice_in_dim(low, core * half, half, 0)
    others = lax.dynamic_slice_in_dim(low, (1 - core) * half, half, 0)
    got = swap_core(others).astype(f32)
    mine = mine.astype(f32)
    even = jnp.where(core == 0, mine, got)
    odd = jnp.where(core == 0, got, mine)
    dec = lax.dynamic_slice_in_dim(decays, core * half, half, 2)[..., None, None]
    if later:
        chip_value = even + dec[0, 0] * odd
    else:
        chip_value = odd + dec[0, 1] * even
    chip_low = chip_value.astype(bf16)
    sign = -1 if later else 1
    total = jnp.zeros_like(chip_value)
    for k in range(chips - 1, 0, -1):
        arrived = chip_shift(chip_low, sign * k, False).astype(f32)
        rel = (sign * k) % chips
        total = arrived + dec[rel, 0] * dec[rel, 1] * total
    if later:
        for_odd = total
        for_even = odd + dec[0, 1] * total
    else:
        for_even = total
        for_odd = even + dec[0, 0] * total
    keep = jnp.where(core == 0, for_even, for_odd).astype(bf16)
    give = jnp.where(core == 0, for_odd, for_even).astype(bf16)
    back = swap_core(give)
    first = jnp.where(core == 0, keep, back)
    second = jnp.where(core == 0, back, keep)
    return jnp.concatenate([first, second], axis=0).astype(f32)


def body(
    tokens,
    cotangent,
    gain_input,
    w_query,
    key_weight,
    value_weight,
    w_mixin,
    conv_taps,
    conv_bias,
    step_offset,
    decay_rate,
    skip_gain,
    gain_mixer,
    w_mixout,
    w_attnout,
    gain_feed,
    w_gate,
    w_up,
    w_down,
):
    rows, width = tokens.shape
    seqs = lax.axis_size("seq")
    ctxs = lax.axis_size("ctx")
    chips = ctxs // 2
    place = lax.axis_index("seq")
    ctx = lax.axis_index("ctx")
    chip, core = ctx // 2, ctx % 2
    ff = w_gate.shape[1]

    sizes = (gain_input.size, gain_feed.size, conv_bias.size, gain_mixer.size, conv_taps.size)
    small = jnp.concatenate(
        [gain_input, gain_feed, conv_bias, gain_mixer, conv_taps.reshape(-1)]
    )
    small = lax.all_gather(small, "seq").astype(f32)
    at = 0
    pieces = []
    for size in sizes:
        pieces.append(small[:, at : at + size])
        at += size
    gin = pieces[0].reshape(-1)
    gfeed = pieces[1].reshape(-1)
    cbias = pieces[2].reshape(-1)
    gmix = pieces[3].reshape(-1)
    taps = pieces[4].reshape(seqs, KC, -1).transpose(1, 0, 2).reshape(KC, -1)

    in_loc = jnp.concatenate([w_query, key_weight, value_weight, w_mixin], axis=1)
    out_loc = jnp.concatenate([w_mixout, w_attnout], axis=0)
    gu_loc = jnp.concatenate([w_gate, w_up], axis=1)
    w_in = gather_weight(in_loc, core)
    w_out = gather_weight(out_loc, core)
    w_gu = gather_weight(gu_loc, core)
    w_dn = gather_weight(w_down, core)

    first_row = ctx * rows
    position = first_row + jnp.arange(rows, dtype=jnp.int32)
    frequency = rope_base ** (
        -(jnp.arange(HEAD_SIZE // 2, dtype=f32) * 2.0 / HEAD_SIZE)
    )
    angles = position.astype(f32)[:, None] * frequency[None, :]
    cosine = jnp.cos(angles)[:, None, :]
    sine = jnp.sin(angles)[:, None, :]

    x = tokens.astype(f32)
    normed = rms_scale(x, gin).astype(bf16)
    pre = times_weight(normed, w_in, seqs, core)
    q_pre = pre[:, :QW].reshape(rows, QUERY_HEADS, HEAD_SIZE)
    k_pre = pre[:, QW : QW + KW].reshape(rows, VALUE_HEADS, HEAD_SIZE)
    v_low = pre[:, QW + KW : QW + 2 * KW].astype(bf16)
    mix0 = QW + 2 * KW
    gate_z = pre[:, mix0 : mix0 + INNER]
    conv_low = pre[:, mix0 + INNER : mix0 + INNER + CONVW].astype(bf16)
    raw_step = pre[:, mix0 + INNER + CONVW :]

    queries = rotary_apply(q_pre, cosine, sine).astype(bf16)
    keys = rotary_apply(k_pre, cosine, sine).astype(bf16).reshape(rows, KW)

    step0 = jax.nn.softplus(raw_step + step_offset[None, :])
    decay = jnp.exp(jnp.sum(-step0 * decay_rate[None, :], axis=0))
    decay_hi = decay.astype(bf16)
    decay_lo = (decay - decay_hi.astype(f32)).astype(bf16)
    extra = jnp.zeros((16, 2 * KW), bf16)
    extra = extra.at[0, :MH].set(decay_hi).at[1, :MH].set(decay_lo)
    message = jnp.concatenate([jnp.concatenate([keys, v_low], axis=1), extra], axis=0)
    got = jnp.stack([message] + [chip_shift(message, k, True) for k in range(1, chips)])
    got_other = swap_core(got)
    kv_all = jnp.stack([got[:, :rows], got_other[:, :rows]])
    dec_own = got[:, rows, :MH].astype(f32) + got[:, rows + 1, :MH].astype(f32)
    dec_oth = got_other[:, rows, :MH].astype(f32) + got_other[:, rows + 1, :MH].astype(f32)
    decays = jnp.stack(
        [jnp.where(core == 0, dec_own, dec_oth), jnp.where(core == 0, dec_oth, dec_own)], axis=1
    )
    count = lax.axis_size("ctx")
    edge = lax.ppermute(
        conv_low[rows - (KC - 1) :], "ctx", [(i, i + 1) for i in range(count - 1)]
    )
    extended = jnp.concatenate([edge, conv_low], axis=0).astype(f32)

    causal = (
        jnp.arange(rows, dtype=jnp.int32)[:, None] >= jnp.arange(rows, dtype=jnp.int32)[None, :]
    )

    def ssm_local(extended_in, steps_in, taps_in, shift_in, offset_in, rates_in, skip_in):
        mixed = conv_mix(extended_in, taps_in, shift_in)
        head_input = mixed[:, :INNER].reshape(rows, MH, MP)
        b_state = mixed[:, INNER : INNER + NS]
        c_state = mixed[:, INNER + NS :]
        step = jax.nn.softplus(steps_in + offset_in[None, :])
        cum = jnp.cumsum(-step * rates_in[None, :], axis=0)
        gaps = cum.T[:, :, None] - cum.T[:, None, :]
        weights = jnp.where(causal[None], jnp.exp(jnp.where(causal[None], gaps, 0.0)), 0.0)
        inter = jnp.dot(c_state, b_state.T, precision=highest)
        mixing = weights * inter[None] * step.T[:, None, :]
        within = jnp.einsum("hts,shp->thp", mixing, head_input, precision=highest)
        out_zero = within + skip_in[None, :, None] * head_input
        tail = jnp.exp(cum[-1][None, :] - cum) * step
        local_state = jnp.einsum(
            "shp,sn->hpn", tail[:, :, None] * head_input, b_state, precision=highest
        )
        return out_zero, local_state, jnp.exp(cum[-1]), c_state, jnp.exp(cum)

    (out_zero, local_state, own_decay, c_state, exp_cum), pull_local = jax.vjp(
        ssm_local, extended, raw_step, taps, cbias, step_offset, decay_rate, skip_gain
    )
    start_state = ctx_state(local_state, decays, chips, chip, core, False)

    qpos = jnp.tile(position, GROUP)
    query_rows = (
        queries.reshape(rows, VALUE_HEADS, GROUP, HEAD_SIZE)
        .transpose(1, 2, 0, 3)
        .reshape(VALUE_HEADS, GROUP * rows, HEAD_SIZE)
    )
    rel = jnp.arange(chips, dtype=jnp.int32)
    key_chip = chip - rel
    side = jnp.stack([core, 1 - core])
    key_pos = (
        (key_chip[None, :, None] * 2 + side[:, None, None]) * rows
        + jnp.arange(rows, dtype=jnp.int32)[None, None, :]
    )
    key_pos = jnp.where(key_chip[None, :, None] >= 0, key_pos, ctxs * rows).reshape(-1)
    total_keys = key_pos.shape[0]
    kv_flat = kv_all.reshape(total_keys, 2, VALUE_HEADS, HEAD_SIZE)
    key_heads = kv_flat[:, 0].transpose(1, 0, 2)
    value_heads = kv_flat[:, 1].transpose(1, 0, 2)
    allowed = key_pos[None, :] <= qpos[:, None]
    scale = HEAD_SIZE ** (-0.5)
    scores = jnp.einsum("hrd,hkd->hrk", query_rows, key_heads, preferred_element_type=f32) * scale
    masked = jnp.where(allowed[None], scores, -1e30)
    top = jnp.max(masked, axis=-1, keepdims=True)
    expanded = jnp.exp(masked - top)
    prob = expanded / jnp.sum(expanded, axis=-1, keepdims=True)
    prob_low = prob.astype(bf16)
    attended = jnp.einsum("hrk,hkd->hrd", prob_low, value_heads, preferred_element_type=f32)
    attn_b = (
        attended.astype(bf16)
        .reshape(VALUE_HEADS, GROUP, rows, HEAD_SIZE)
        .transpose(2, 0, 1, 3)
        .reshape(rows, QW)
    )

    def finish(zero_in, c_in, exp_in, start_in, gate_in, gain_in):
        across = jnp.einsum("tn,hpn->thp", c_in, start_in, precision=highest) * exp_in[:, :, None]
        gated = (zero_in + across).reshape(rows, INNER) * jax.nn.silu(gate_in)
        return rms_scale(gated, gain_in)

    mix_normed, pull_finish = jax.vjp(
        finish, out_zero, c_state, exp_cum, start_state, gate_z, gmix
    )
    mix_b = mix_normed.astype(bf16)

    out_in = jnp.concatenate(
        [
            mix_b.reshape(rows, seqs, INNER // seqs),
            attn_b.reshape(rows, seqs, QW // seqs),
        ],
        axis=2,
    )
    out_flat = out_in.reshape(rows, INNER + QW)
    residual = x + times_weight(out_flat, w_out, seqs, core)
    feed_b, pull_feed = jax.vjp(rms_scale, residual, gfeed)
    feed_b = feed_b.astype(bf16)
    gate_up = times_weight(feed_b, w_gu, seqs, core)
    gate, up = gate_up[:, :ff], gate_up[:, ff:]
    hidden, pull_hidden = jax.vjp(lambda a, b: jax.nn.silu(a) * b, gate, up)
    hidden_b = hidden.astype(bf16)
    layer_out = (residual + times_weight(hidden_b, w_dn, seqs, core)).astype(bf16)

    left = jnp.concatenate(
        [
            normed.reshape(rows, seqs, -1),
            feed_b.reshape(rows, seqs, -1),
            out_in,
            hidden_b.reshape(rows, seqs, -1),
        ],
        axis=2,
    )
    left = send_blocks(left, place, seqs)
    wide = width // seqs
    outw = (INNER + QW) // seqs
    left_normed = left[:, :wide]
    left_feed = left[:, wide : 2 * wide]
    left_out = left[:, 2 * wide : 2 * wide + outw]
    left_hidden = left[:, 2 * wide + outw :]

    d_hidden = times_weight_t(cotangent, w_dn, seqs, core)
    d_gate, d_up = pull_hidden(d_hidden)
    d_gu = jnp.concatenate([d_gate, d_up], axis=1).astype(bf16)
    d_feed = times_weight_t(d_gu, w_gu, seqs, core)
    d_res_norm, d_gfeed = pull_feed(d_feed)
    grad_res = cotangent.astype(f32) + d_res_norm
    res_b = grad_res.astype(bf16)
    d_out = times_weight_t(res_b, w_out, seqs, core).reshape(rows, seqs, outw)
    d_mix = d_out[:, :, : INNER // seqs].reshape(rows, INNER)
    d_att = d_out[:, :, INNER // seqs :].reshape(rows, QW).astype(bf16)

    right = gather_rows(jnp.concatenate([d_gu, cotangent, res_b], axis=1), seqs)
    grad_gu = dot_tn(left_feed, right[:, : 2 * ff])
    grad_dn = dot_tn(left_hidden, right[:, 2 * ff : 2 * ff + width])
    grad_out = dot_tn(left_out, right[:, 2 * ff + width :])
    sum_gu = sum_over_ctx(grad_gu, chips, chip, core)
    sum_do = sum_over_ctx(
        jnp.concatenate([grad_dn, grad_out], axis=1), chips, chip, core
    )

    d_zero, d_c, d_exp, d_start, d_gate_z, d_gmix = pull_finish(d_mix)
    later_grad = ctx_state(d_start, decays, chips, chip, core, True)
    decay_grad = jnp.sum(later_grad * start_state, axis=(1, 2))

    grad_rows = (
        d_att.reshape(rows, VALUE_HEADS, GROUP, HEAD_SIZE)
        .transpose(1, 2, 0, 3)
        .reshape(VALUE_HEADS, GROUP * rows, HEAD_SIZE)
    )
    d_prob = jnp.einsum("hrd,hkd->hrk", grad_rows, value_heads, preferred_element_type=f32)
    delta = jnp.sum(prob * d_prob, axis=-1, keepdims=True)
    d_score = (prob * (d_prob - delta)).astype(bf16)
    d_query_rows = (
        jnp.einsum("hrk,hkd->hrd", d_score, key_heads, preferred_element_type=f32) * scale
    )
    d_keys = jnp.einsum("hrk,hrd->khd", d_score, query_rows, preferred_element_type=f32) * scale
    d_values = jnp.einsum("hrk,hrd->khd", prob_low, grad_rows, preferred_element_type=f32)
    d_kv = jnp.concatenate(
        [d_keys.reshape(total_keys, KW), d_values.reshape(total_keys, KW)], axis=1
    ).reshape(2, chips, rows, 2 * KW)
    d_kv = d_kv[0] + swap_core(d_kv[1].astype(bf16)).astype(f32)
    d_kv_own = d_kv[0]
    for k in range(1, chips):
        d_kv_own = d_kv_own + chip_shift(d_kv[k].astype(bf16), -k, False).astype(f32)
    d_queries = (
        d_query_rows.reshape(VALUE_HEADS, GROUP, rows, HEAD_SIZE)
        .transpose(2, 0, 1, 3)
        .reshape(rows, QUERY_HEADS, HEAD_SIZE)
    )
    d_q = rotary_apply(d_queries, cosine, -sine).reshape(rows, QW).astype(bf16)
    d_k = (
        rotary_apply(d_kv_own[:, :KW].reshape(rows, VALUE_HEADS, HEAD_SIZE), cosine, -sine)
        .reshape(rows, KW)
        .astype(bf16)
    )
    d_v = d_kv_own[:, KW:].astype(bf16)

    d_ext, d_step, d_taps, d_cbias, d_offset, d_rate, d_skip = pull_local(
        (d_zero, later_grad, decay_grad, d_c, d_exp)
    )
    edge_back = lax.ppermute(
        d_ext[: KC - 1], "ctx", [(i + 1, i) for i in range(count - 1)]
    )
    d_conv = d_ext[KC - 1 :]
    d_conv = jnp.concatenate(
        [d_conv[: rows - (KC - 1)], d_conv[rows - (KC - 1) :] + edge_back], axis=0
    )
    d_pre = jnp.concatenate(
        [d_q, d_k, d_v, d_gate_z.astype(bf16), d_conv.astype(bf16), d_step.astype(bf16)], axis=1
    )

    right_in = gather_rows(d_pre, seqs)
    d_normed = times_weight_t(d_pre, w_in, seqs, core)
    unused, pull_input = jax.vjp(rms_scale, x, gin)
    d_x, d_gin = pull_input(d_normed)
    grad_tokens = grad_res + d_x
    parts = (d_gin, d_gfeed, d_cbias, d_gmix, d_taps.reshape(-1), d_offset, d_rate, d_skip)
    sums = lax.psum(jnp.concatenate(parts), ("seq", "ctx"))
    out_small = []
    at = 0
    for part in parts:
        out_small.append(sums[at : at + part.size])
        at += part.size

    def own_share(vec):
        size = vec.shape[-1] // seqs
        return lax.dynamic_slice_in_dim(vec, place * size, size, vec.ndim - 1)

    grad_in = dot_tn(left_normed, right_in)
    sum_in = sum_over_ctx(grad_in, chips, chip, core).astype(f32)
    sum_gu = sum_gu.astype(f32)
    sum_do = sum_do.astype(f32)
    mixo = INNER // seqs
    return (
        layer_out,
        grad_tokens,
        own_share(out_small[0]),
        sum_in[:, :QW],
        sum_in[:, QW : QW + KW],
        sum_in[:, QW + KW : mix0],
        sum_in[:, mix0:],
        own_share(out_small[4].reshape(KC, CONVW)),
        own_share(out_small[2]),
        out_small[5],
        out_small[6],
        out_small[7],
        own_share(out_small[3]),
        sum_do[:mixo, width:],
        sum_do[mixo:, width:],
        own_share(out_small[1]),
        sum_gu[:, :ff],
        sum_gu[:, ff:],
        sum_do[:, :width],
    )


def solution(mesh):
    rows = P(("seq", "ctx"), None)
    vec = P("seq")
    mat = P("seq", None)
    col = P(None, "seq")
    rep = P()
    in_specs = (
        rows, rows, vec, mat, mat, mat, mat, col, vec, rep, rep, rep, vec, mat, mat, vec, mat, mat, mat,
    )
    out_specs = (
        rows, rows, vec, mat, mat, mat, mat, col, vec, rep, rep, rep, vec, mat, mat, vec, mat, mat, mat,
    )
    return jax.shard_map(body, mesh=mesh, in_specs=in_specs, out_specs=out_specs, check_vma=False)
```

time: 1890 us -> 799 us (0.42)
  waiting for transfers between devices: 1360 us -> 238 us
  blocking collectives: 239 us -> 110 us
  local copies, waits for them, and re-layouts: 48.2 us -> 143 us
  starting transfers between devices: 9.55 us -> 88.3 us
  matrix products: 122 us -> 101 us
    reduce_scatter x10 -> x0, waiting for transfers between devices: 1060 us -> none  [the longest x1 161 us: body(): lax.psum_scatter(grad_mixin, ('seq', 'ctx'), scatter_dimension=0, tiled=T...]
    all_gather x14 -> x0, blocking collectives: 180 us -> none  [the longest x1 19.7 us: body(): lax.all_gather(shares[1].astype(jnp.bfloat16), 'ctx', axis=0, tiled=True)]
    all_gather x13 -> x4, waiting for transfers between devices: 292 us -> 142 us  [gather_weight(): own = lax.all_gather(take_half(local, core), 'seq', axis=0, tiled=True)]
    psum x0 -> x1, blocking collectives: none -> 95.9 us  [body(): sums = lax.psum(jnp.concatenate(parts), ('seq', 'ctx'))]
    ppermute x2 -> x57, waiting for transfers between devices: 0.02 us -> 95.2 us  [the longest x30 94 us: chip_shift(): return lax.ppermute(value, 'ctx', pairs)]
    ppermute x2 -> x57, starting transfers between devices: 8.19 us -> 88.1 us  [the longest x30 62.5 us: chip_shift(): return lax.ppermute(value, 'ctx', pairs)]
    unnamed x3 -> x1, blocking collectives: 58.6 us -> 14.1 us
    dot_general x53 -> x37, matrix products: 122 us -> 96.6 us  [the longest x4 21 us: dot_tn(): lax.dot_general(a, b, (((0,), (0,)), ((), ())), preferred_element_type=f32)]
  transfers between devices with their start and end apart: 25 -> 61, of which waited for: 18 -> 17; matrix products, arithmetic and copies ran while one was open for 11% -> 29% of each run, Pallas kernels for 0% -> 0%
where the time goes in v1:
time: 799 us; the launch traced here: 787 us
  waiting for transfers between devices  238 us (30%)
  local copies, waits for them, and re-layouts  143 us (18%)
  blocking collectives  110 us (14%)
  matrix products  101 us (13%)
  other arithmetic  88.4 us (11%)
  starting transfers between devices  88.3 us (11%)
  between operations  17.5 us (2%)
    all_gather x4, waiting for transfers between devices, gather_weight(): own = lax.all_gather(take_half(local, core), 'seq', axis=0, tiled=True)  142 us
    psum x1, blocking collectives, body(): sums = lax.psum(jnp.concatenate(parts), ('seq', 'ctx'))  95.9 us
    ppermute x30, waiting for transfers between devices, chip_shift(): return lax.ppermute(value, 'ctx', pairs)  94 us
    ppermute x30, starting transfers between devices, chip_shift(): return lax.ppermute(value, 'ctx', pairs)  62.5 us
    unnamed x325, local copies, waits for them, and re-layouts  28.5 us
    dot_general x4, matrix products, dot_tn(): lax.dot_general(a, b, (((0,), (0,)), ((), ())), preferred_element_type=f32)  21 us
    dot_general x8, matrix products, dot_nt(): lax.dot_general(a, b, (((1,), (1,)), ((), ())), preferred_element_type=f32)  20.8 us
    dot_general x8, matrix products, dot(): return jnp.dot(a, b, preferred_element_type=f32)  17.7 us
  transfers between devices with their start and end apart: 61, of which 17 were waited for; matrix products, arithmetic and copies ran while one was open for 29% of the time, Pallas kernels for 0%

profile of v1, /device:TPU:1, one launch (start us, length us, event | category | flops | bytes accessed | tf_op | source)
XLA Modules:
  0.0 786.5 jit_solution(13009096915474993626)
XLA Ops:
  18.7 14.1 %all-reduce.14 = bf16[12544]{0:T(1024)(128)(2,1)S(1)} all-reduce(bf16[12544]{0:T(1024)(128)(2,1)S(1)} %dynamic-update-slice.4), channel_id=2, replica_groups=mesh['seq'=4,'ctx'=8] {'seq'}, use_global_device_ids=true, to_apply=%add.14 | all-reduce | flops 12544 | bytes 50176
  33.4 34.5 %all-gather.6.cloned.1.call-done = bf16[512,4120]{0,1:T(8,128)(2,1)} async-done(((bf16[128,4120]{0,1:T(8,128)(2,1)}), bf16[512,4120]{0,1:T(8,128)(2,1)}) %all-gather.6.cloned.1.call-update) | async-done | bytes 4218896 | tf_op jit(solution)/shard_map/all_gather | solution.py:91
  75.0 30.7 %all-gather.12.cloned.1.call-done = bf16[1024,1024]{1,0:T(8,128)(2,1)} async-done(((bf16[256,1024]{1,0:T(8,128)(2,1)}), bf16[1024,1024]{1,0:T(8,128)(2,1)}) %all-gather.12.cloned.1.call-update) | async-done | bytes 2097168 | tf_op jit(solution)/shard_map/all_gather | solution.py:91
  110.5 32.9 %all-gather.8.cloned.1.call-done = bf16[1024,1024]{1,0:T(8,128)(2,1)} async-done(((bf16[256,1024]{1,0:T(8,128)(2,1)}), bf16[1024,1024]{1,0:T(8,128)(2,1)}) %all-gather.8.cloned.1.call-update) | async-done | bytes 2097168 | tf_op jit(solution)/shard_map/all_gather | solution.py:91
  154.2 44.2 %all-gather.10.cloned.1.call-done = bf16[512,4096]{1,0:T(8,128)(2,1)} async-done(((bf16[128,4096]{1,0:T(8,128)(2,1)}), bf16[512,4096]{1,0:T(8,128)(2,1)}) %all-gather.10.cloned.1.call-update) | async-done | bytes 4194320 | tf_op jit(solution)/shard_map/all_gather | solution.py:91
  199.2 3.7 fusion.276
  203.0 3.7 fusion.274
  208.8 3.1 collective-permute-start.5
  212.9 2.9 collective-permute-start.1
  220.2 2.5 collective-permute-start.3
  234.1 3.7 collective-permute-start.9
  247.2 4.8 fusion.275
  255.5 3.0 fusion.37
  263.9 4.2 multiply_add_fusion.1
  277.9 2.9 fusion.278
  280.8 3.1 convolution_add_fusion.1
  288.0 4.5 broadcast_select_fusion.15
  304.6 3.4 broadcast_select_fusion.1
  318.1 3.3 multiply_reduce_fusion
  332.1 3.3 multiply_reduce_fusion.7
  337.7 6.1 fusion.85
  366.3 2.6 dynamic-slice_bitcast_fusion.3
  409.3 2.9 fusion.143
  412.2 3.7 collective-permute-done.20
  417.0 2.9 collective-permute-done.19
  424.0 2.6 pad_maximum_fusion.13
  430.8 2.8 fusion.28
  437.8 2.6 multiply_reduce_fusion.6
  458.8 3.3 fusion.282
  462.1 3.3 broadcast_select_fusion.13
  467.5 95.9 %psum.7 = f32[12616]{0:T(1024)S(1)} all-reduce(f32[12616]{0:T(1024)S(1)} %concatenate.121), channel_id=1, replica_groups=mesh['seq'=4,'ctx'=8] {'seq','ctx'}, use_global_device_ids=true, to_apply=%region_32.33 | all-reduce | flops 12616 | bytes 100928 | tf_op jit(solution)/shard_map/psum | solution.py:473
  578.8 11.5 %fusion.9 = f32[256,4096]{1,0:T(8,128)S(1)} fusion(bf16[128,6144]{1,0:T(8,128)(2,1)} %collective-permute-done.40, bf16[128,6144]{1,0:T(8,128)(2,1)} %collective-permute-done.39, bf16[128,6144]{1,0:T(8,128)(2,1)} %collective-permute-done.38, bf16[128,1024]{1,0:T(8,128)(2,1)S(1)} %copy-done.21, bf16[128,1024]{1,0:T(8,128)(2,1)S(1)} %copy-done.11, ...), kind=kOutput, calls=%fused_computation.12 | convolution fusion | flops 1104150528 | bytes 12058624 | tf_op jit(solution)/shard_map/dot_general | solution.py:35
  599.7 5.8 fusion.1
  605.5 5.9 reshape.866
  611.3 7.7 constant_dynamic-slice_fusion.2
  626.2 3.0 collective-permute-start.52
  634.0 12.3 %collective-permute-done.43 = bf16[64,2048]{1,0:T(8,128)(2,1)} collective-permute-done((bf16[64,2048]{1,0:T(8,128)(2,1)}, bf16[64,2048]{1,0:T(8,128)(2,1)}, u32[]{:S(2)}, u32[]{:S(2)}) %collective-permute-start.43) | collective-permute-done | bytes 262176 | tf_op jit(solution)/shard_map/ppermute | solution.py:77
  646.3 13.0 %collective-permute-start.32 = (bf16[32,4120]{1,0:T(8,128)(2,1)S(1)}, bf16[32,4120]{1,0:T(8,128)(2,1)S(1)}, u32[]{:S(2)}, u32[]{:S(2)}) collective-permute-start(bf16[32,4120]{1,0:T(8,128)(2,1)S(1)} %get-tuple-element.246), channel_id=1, source_target_pairs={{0,4},{1,5},{2,6},{3,7},{4,0},{5,1},{6,2},{7,3},{8,12},{9,13},{10,... | collective-permute-start | bytes 791048 | tf_op jit(solution)/shard_map/ppermute | solution.py:77
  660.7 3.9 collective-permute-start.31
  664.5 15.8 %collective-permute-done.51 = bf16[32,4096]{1,0:T(8,128)(2,1)} collective-permute-done((bf16[32,4096]{1,0:T(8,128)(2,1)}, bf16[32,4096]{1,0:T(8,128)(2,1)}, u32[]{:S(2)}, u32[]{:S(2)}) %collective-permute-start.51) | collective-permute-done | bytes 262176 | tf_op jit(solution)/shard_map/ppermute | solution.py:77
  683.3 3.9 collective-permute-start.45
  687.2 15.9 %collective-permute-done.32 = bf16[32,4120]{1,0:T(8,128)(2,1)S(1)} collective-permute-done((bf16[32,4120]{1,0:T(8,128)(2,1)S(1)}, bf16[32,4120]{1,0:T(8,128)(2,1)S(1)}, u32[]{:S(2)}, u32[]{:S(2)}) %collective-permute-start.32) | collective-permute-done | bytes 263712 | tf_op jit(solution)/shard_map/ppermute | solution.py:77
  704.8 5.0 collective-permute-start.53
  710.9 14.6 %collective-permute-done.46 = bf16[64,2048]{1,0:T(8,128)(2,1)S(1)} collective-permute-done((bf16[64,2048]{1,0:T(8,128)(2,1)S(1)}, bf16[64,2048]{1,0:T(8,128)(2,1)S(1)}, u32[]{:S(2)}, u32[]{:S(2)}) %collective-permute-start.46) | collective-permute-done | bytes 262176 | tf_op jit(solution)/shard_map/ppermute | solution.py:77
  727.4 4.8 collective-permute-start.34
  732.2 16.1 %collective-permute-done.54 = bf16[32,4096]{1,0:T(8,128)(2,1)S(1)} collective-permute-done((bf16[32,4096]{1,0:T(8,128)(2,1)S(1)}, bf16[32,4096]{1,0:T(8,128)(2,1)S(1)}, u32[]{:S(2)}, u32[]{:S(2)}) %collective-permute-start.54) | collective-permute-done | bytes 262176 | tf_op jit(solution)/shard_map/ppermute | solution.py:77
  750.8 9.1 %collective-permute-done.35 = bf16[32,4120]{1,0:T(8,128)(2,1)S(1)} collective-permute-done((bf16[32,4120]{1,0:T(8,128)(2,1)S(1)}, bf16[32,4120]{1,0:T(8,128)(2,1)S(1)}, u32[]{:S(2)}, u32[]{:S(2)}) %collective-permute-start.35) | collective-permute-done | bytes 263712 | tf_op jit(solution)/shard_map/ppermute | solution.py:77
  774.6 5.1 copy.493
  (695 shorter events, 278.6 us)
Async XLA Ops:
  7.2 60.7 %all-gather.6.cloned.1.call-start = ((), (), s32[]{:S(2)}) async-start(), calls=%async_computation | async-start | bytes 5273600 | tf_op jit(solution)/shard_map/all_gather | solution.py:91
  12.6 93.1 %all-gather.12.cloned.1.call-start = ((), (), s32[]{:S(2)}) async-start(), calls=%async_computation.3 | async-start | bytes 2621440 | tf_op jit(solution)/shard_map/all_gather | solution.py:91
  13.5 129.9 %all-gather.8.cloned.1.call-start = ((), (), s32[]{:S(2)}) async-start(), calls=%async_computation.1 | async-start | bytes 2621440 | tf_op jit(solution)/shard_map/all_gather | solution.py:91
  15.7 182.7 %all-gather.10.cloned.1.call-start = ((), (), s32[]{:S(2)}) async-start(), calls=%async_computation.2 | async-start | bytes 5242880 | tf_op jit(solution)/shard_map/all_gather | solution.py:91
  67.9 135.0 %collective-permute-start = (bf16[512,4120]{0,1:T(8,128)(2,1)}, bf16[512,4120]{0,1:T(8,128)(2,1)}, u32[]{:S(2)}, u32[]{:S(2)}) collective-permute-start(bf16[512,4120]{0,1:T(8,128)(2,1)} %all-gather.6.cloned.1.call-done), channel_id=1, source_target_pairs={{0,1},{1,0},{2,3},{3,2},{4,5},{5,4},{6,7},{7,6},{8,9},{9,8},{10,11... | collective-permute-start | bytes 12656648 | tf_op jit(solution)/shard_map/ppermute | solution.py:65
  105.7 40.8 %collective-permute-start.13 = (bf16[1024,1024]{1,0:T(8,128)(2,1)}, bf16[1024,1024]{1,0:T(8,128)(2,1)S(1)}, u32[]{:S(2)}, u32[]{:S(2)}) collective-permute-start(bf16[1024,1024]{1,0:T(8,128)(2,1)} %all-gather.12.cloned.1.call-done), channel_id=1, source_target_pairs={{0,1},{1,0},{2,3},{3,2},{4,5},{5,4},{6,7},{7,6},{8,9},{9,8},{10,11... | collective-permute-start | bytes 6291464 | tf_op jit(solution)/shard_map/ppermute | solution.py:65
  143.5 131.2 %collective-permute-start.11 = (bf16[1024,1024]{1,0:T(8,128)(2,1)}, bf16[1024,1024]{1,0:T(8,128)(2,1)}, u32[]{:S(2)}, u32[]{:S(2)}) collective-permute-start(bf16[1024,1024]{1,0:T(8,128)(2,1)} %all-gather.8.cloned.1.call-done), channel_id=1, source_target_pairs={{0,1},{1,0},{2,3},{3,2},{4,5},{5,4},{6,7},{7,6},{8,9},{9,8},{10,11... | collective-permute-start | bytes 6291464 | tf_op jit(solution)/shard_map/ppermute | solution.py:65
  198.5 82.3 %collective-permute-start.12 = (bf16[512,4096]{1,0:T(8,128)(2,1)}, bf16[512,4096]{1,0:T(8,128)(2,1)}, u32[]{:S(2)}, u32[]{:S(2)}) collective-permute-start(bf16[512,4096]{1,0:T(8,128)(2,1)} %all-gather.10.cloned.1.call-done), channel_id=1, source_target_pairs={{0,1},{1,0},{2,3},{3,2},{4,5},{5,4},{6,7},{7,6},{8,9},{9,8},{10,11... | collective-permute-start | bytes 12582920 | tf_op jit(solution)/shard_map/ppermute | solution.py:65
  208.8 20.8 %collective-permute-start.5 = (bf16[144,256]{1,0:T(8,128)(2,1)}, bf16[144,256]{1,0:T(8,128)(2,1)}, u32[]{:S(2)}, u32[]{:S(2)}) collective-permute-start(bf16[144,256]{1,0:T(8,128)(2,1)} %get-tuple-element.304), channel_id=1, source_target_pairs={{0,6},{1,7},{2,0},{3,1},{4,2},{5,3},{6,4},{7,5},{8,14},{9,15},{10,... | collective-permute-start | bytes 221192 | tf_op jit(solution)/shard_map/ppermute | solution.py:77
  211.9 17.8 %collective-permute-start.4 = (bf16[144,256]{1,0:T(8,128)(2,1)}, bf16[144,256]{1,0:T(8,128)(2,1)}, u32[]{:S(2)}, u32[]{:S(2)}) collective-permute-start(bf16[144,256]{1,0:T(8,128)(2,1)} %get-tuple-element.304), channel_id=1, source_target_pairs={{0,4},{1,5},{2,6},{3,7},{4,0},{5,1},{6,2},{7,3},{8,12},{9,13},{10,... | collective-permute-start | bytes 221192 | tf_op jit(solution)/shard_map/ppermute | solution.py:77
  234.1 18.4 %collective-permute-start.9 = (bf16[12,64,128]{2,1,0:T(8,128)(2,1)}, bf16[12,64,128]{2,1,0:T(8,128)(2,1)}, u32[]{:S(2)}, u32[]{:S(2)}) collective-permute-start(bf16[12,64,128]{2,1,0:T(8,128)(2,1)} %fusion.135), channel_id=1, source_target_pairs={{0,6},{1,7},{8,14},{9,15},{16,22},{17,23},{24,30},{25,31}} | collective-permute-start | bytes 589832 | tf_op jit(solution)/shard_map/ppermute | solution.py:77
  237.8 14.7 %collective-permute-start.8 = (bf16[12,64,128]{2,1,0:T(8,128)(2,1)}, bf16[12,64,128]{2,1,0:T(8,128)(2,1)}, u32[]{:S(2)}, u32[]{:S(2)}) collective-permute-start(bf16[12,64,128]{2,1,0:T(8,128)(2,1)} %fusion.135), channel_id=1, source_target_pairs={{0,4},{1,5},{2,6},{3,7},{8,12},{9,13},{10,14},{11,15},{16,20},{17,... | collective-permute-start | bytes 589832 | tf_op jit(solution)/shard_map/ppermute | solution.py:77
  239.8 12.8 %collective-permute-start.7 = (bf16[12,64,128]{2,1,0:T(8,128)(2,1)}, bf16[12,64,128]{2,1,0:T(8,128)(2,1)}, u32[]{:S(2)}, u32[]{:S(2)}) collective-permute-start(bf16[12,64,128]{2,1,0:T(8,128)(2,1)} %fusion.135), channel_id=1, source_target_pairs={{0,2},{1,3},{2,4},{3,5},{4,6},{5,7},{8,10},{9,11},{10,12},{11,13},... | collective-permute-start | bytes 589832 | tf_op jit(solution)/shard_map/ppermute | solution.py:77
  360.2 25.6 %collective-permute-start.14 = (bf16[4,128,256]{2,1,0:T(8,128)(2,1)}, bf16[4,128,256]{2,1,0:T(8,128)(2,1)}, u32[]{:S(2)}, u32[]{:S(2)}) collective-permute-start(bf16[4,128,256]{2,1,0:T(8,128)(2,1)} %bitcast.69), channel_id=1, source_target_pairs={{0,1},{1,0},{2,3},{3,2},{4,5},{5,4},{6,7},{7,6},{8,9},{9,8},{10,11... | collective-permute-start | bytes 786440 | tf_op jit(solution)/shard_map/ppermute | solution.py:65
  362.1 27.5 %collective-permute-start.18 = (bf16[12,64,128]{2,1,0:T(8,128)(2,1)}, bf16[12,64,128]{2,1,0:T(8,128)(2,1)}, u32[]{:S(2)}, u32[]{:S(2)}) collective-permute-start(bf16[12,64,128]{2,1,0:T(8,128)(2,1)} %constant_dynamic-slice_fusion.4), channel_id=1, source_target_pairs={{0,1},{1,0},{2,3},{3,2},{4,5},{5,4},{6,7},{7,6},{8,9},{9,8},{10,11... | collective-permute-start | bytes 589832 | tf_op jit(solution)/shard_map/ppermute | solution.py:65
  381.0 40.8 %collective-permute-start.26 = (bf16[128,1536]{1,0:T(8,128)(2,1)}, bf16[128,1536]{1,0:T(8,128)(2,1)}, u32[]{:S(2)}, u32[]{:S(2)}) collective-permute-start(bf16[128,1536]{1,0:T(8,128)(2,1)} %get-tuple-element.257), channel_id=1, source_target_pairs={{0,24},{8,16},{16,8},{24,0},{1,25},{9,17},{17,9},{25,1},{2,26},{10... | collective-permute-start | bytes 1179656 | tf_op jit(solution)/shard_map/ppermute | solution.py:82
  382.1 40.8 %collective-permute-start.25 = (bf16[128,1536]{1,0:T(8,128)(2,1)}, bf16[128,1536]{1,0:T(8,128)(2,1)}, u32[]{:S(2)}, u32[]{:S(2)}) collective-permute-start(bf16[128,1536]{1,0:T(8,128)(2,1)} %get-tuple-element.258), channel_id=1, source_target_pairs={{0,16},{8,24},{16,0},{24,8},{1,17},{9,25},{17,1},{25,9},{2,18},{10... | collective-permute-start | bytes 1179656 | tf_op jit(solution)/shard_map/ppermute | solution.py:82
  393.8 30.2 %collective-permute-start.24 = (bf16[128,1536]{1,0:T(8,128)(2,1)}, bf16[128,1536]{1,0:T(8,128)(2,1)}, u32[]{:S(2)}, u32[]{:S(2)}) collective-permute-start(bf16[128,1536]{1,0:T(8,128)(2,1)} %get-tuple-element.259), channel_id=1, source_target_pairs={{0,8},{8,0},{16,24},{24,16},{1,9},{9,1},{17,25},{25,17},{2,10},{10... | collective-permute-start | bytes 1179656 | tf_op jit(solution)/shard_map/ppermute | solution.py:82
  397.9 17.9 %collective-permute-start.20 = (bf16[12,64,128]{2,1,0:T(8,128)(2,1)}, bf16[12,64,128]{2,1,0:T(8,128)(2,1)}, u32[]{:S(2)}, u32[]{:S(2)}) collective-permute-start(bf16[12,64,128]{2,1,0:T(8,128)(2,1)} %fusion.137), channel_id=1, source_target_pairs={{4,0},{5,1},{6,2},{7,3},{12,8},{13,9},{14,10},{15,11},{20,16},{21,... | collective-permute-start | bytes 589832 | tf_op jit(solution)/shard_map/ppermute | solution.py:77
  407.9 12.0 %collective-permute-start.19 = (bf16[12,64,128]{2,1,0:T(8,128)(2,1)}, bf16[12,64,128]{2,1,0:T(8,128)(2,1)S(1)}, u32[]{:S(2)}, u32[]{:S(2)}) collective-permute-start(bf16[12,64,128]{2,1,0:T(8,128)(2,1)} %fusion.137), channel_id=1, source_target_pairs={{2,0},{3,1},{4,2},{5,3},{6,4},{7,5},{10,8},{11,9},{12,10},{13,11},... | collective-permute-start | bytes 589832 | tf_op jit(solution)/shard_map/ppermute | solution.py:77
  415.9 153.9 %collective-permute-start.40 = (bf16[128,6144]{1,0:T(8,128)(2,1)}, bf16[128,6144]{1,0:T(8,128)(2,1)}, u32[]{:S(2)}, u32[]{:S(2)}) collective-permute-start(bf16[128,6144]{1,0:T(8,128)(2,1)} %pad_maximum_fusion.14), channel_id=1, source_target_pairs={{0,24},{8,16},{16,8},{24,0},{1,25},{9,17},{17,9},{25,1},{2,26},{10... | collective-permute-start | bytes 4718600 | tf_op jit(solution)/shard_map/ppermute | solution.py:82
  419.9 151.8 %collective-permute-start.39 = (bf16[128,6144]{1,0:T(8,128)(2,1)}, bf16[128,6144]{1,0:T(8,128)(2,1)}, u32[]{:S(2)}, u32[]{:S(2)}) collective-permute-start(bf16[128,6144]{1,0:T(8,128)(2,1)} %pad_maximum_fusion.14), channel_id=1, source_target_pairs={{0,16},{8,24},{16,0},{24,8},{1,17},{9,25},{17,1},{25,9},{2,18},{10... | collective-permute-start | bytes 4718600 | tf_op jit(solution)/shard_map/ppermute | solution.py:82
  421.7 150.0 %collective-permute-start.38 = (bf16[128,6144]{1,0:T(8,128)(2,1)}, bf16[128,6144]{1,0:T(8,128)(2,1)}, u32[]{:S(2)}, u32[]{:S(2)}) collective-permute-start(bf16[128,6144]{1,0:T(8,128)(2,1)} %pad_maximum_fusion.14), channel_id=1, source_target_pairs={{0,8},{8,0},{16,24},{24,16},{1,9},{9,1},{17,25},{25,17},{2,10},{10... | collective-permute-start | bytes 4718600 | tf_op jit(solution)/shard_map/ppermute | solution.py:82
  457.4 135.9 %collective-permute-start.29 = (bf16[128,4120]{0,1:T(8,128)(2,1)}, bf16[128,4120]{0,1:T(8,128)(2,1)}, u32[]{:S(2)}, u32[]{:S(2)}) collective-permute-start(bf16[128,4120]{0,1:T(8,128)(2,1)} %copy.485), channel_id=1, source_target_pairs={{0,24},{8,16},{16,8},{24,0},{1,25},{9,17},{17,9},{25,1},{2,26},{10... | collective-permute-start | bytes 3164168 | tf_op jit(solution)/shard_map/ppermute | solution.py:82
  458.6 136.4 %collective-permute-start.28 = (bf16[128,4120]{0,1:T(8,128)(2,1)}, bf16[128,4120]{0,1:T(8,128)(2,1)}, u32[]{:S(2)}, u32[]{:S(2)}) collective-permute-start(bf16[128,4120]{0,1:T(8,128)(2,1)} %copy.485), channel_id=1, source_target_pairs={{0,16},{8,24},{16,0},{24,8},{1,17},{9,25},{17,1},{25,9},{2,18},{10... | collective-permute-start | bytes 3164168 | tf_op jit(solution)/shard_map/ppermute | solution.py:82
  569.7 27.6 %collective-permute-start.27 = (bf16[128,4120]{0,1:T(8,128)(2,1)}, bf16[128,4120]{0,1:T(8,128)(2,1)}, u32[]{:S(2)}, u32[]{:S(2)}) collective-permute-start(bf16[128,4120]{0,1:T(8,128)(2,1)} %copy.485), channel_id=1, source_target_pairs={{0,8},{8,0},{16,24},{24,16},{1,9},{9,1},{17,25},{25,17},{2,10},{10... | collective-permute-start | bytes 3164168 | tf_op jit(solution)/shard_map/ppermute | solution.py:82
  577.1 42.2 %collective-permute-start.41 = (bf16[256,2048]{1,0:T(8,128)(2,1)}, bf16[256,2048]{1,0:T(8,128)(2,1)}, u32[]{:S(2)}, u32[]{:S(2)}) collective-permute-start(bf16[256,2048]{1,0:T(8,128)(2,1)} %fusion.46), channel_id=1, source_target_pairs={{0,1},{1,0},{2,3},{3,2},{4,5},{5,4},{6,7},{7,6},{8,9},{9,8},{10,11... | collective-permute-start | bytes 3145736 | tf_op jit(solution)/shard_map/ppermute | solution.py:65
  592.4 31.3 %collective-permute-start.49 = (bf16[128,4096]{1,0:T(8,128)(2,1)S(1)}, bf16[128,4096]{1,0:T(8,128)(2,1)}, u32[]{:S(2)}, u32[]{:S(2)}) collective-permute-start(bf16[128,4096]{1,0:T(8,128)(2,1)S(1)} %fusion.47), channel_id=1, source_target_pairs={{0,1},{1,0},{2,3},{3,2},{4,5},{5,4},{6,7},{7,6},{8,9},{9,8},{10,11... | collective-permute-start | bytes 3145736 | tf_op jit(solution)/shard_map/ppermute | solution.py:65
  621.9 11.8 %collective-permute-start.44 = (bf16[64,2048]{1,0:T(8,128)(2,1)}, bf16[64,2048]{1,0:T(8,128)(2,1)}, u32[]{:S(2)}, u32[]{:S(2)}) collective-permute-start(bf16[64,2048]{1,0:T(8,128)(2,1)} %get-tuple-element.253), channel_id=1, source_target_pairs={{0,6},{1,7},{2,0},{3,1},{4,2},{5,3},{6,4},{7,5},{8,14},{9,15},{10,... | collective-permute-start | bytes 786440 | tf_op jit(solution)/shard_map/ppermute | solution.py:77
  623.4 22.9 %collective-permute-start.43 = (bf16[64,2048]{1,0:T(8,128)(2,1)}, bf16[64,2048]{1,0:T(8,128)(2,1)}, u32[]{:S(2)}, u32[]{:S(2)}) collective-permute-start(bf16[64,2048]{1,0:T(8,128)(2,1)} %get-tuple-element.254), channel_id=1, source_target_pairs={{0,4},{1,5},{2,6},{3,7},{4,0},{5,1},{6,2},{7,3},{8,12},{9,13},{10,... | collective-permute-start | bytes 786440 | tf_op jit(solution)/shard_map/ppermute | solution.py:77
  623.4 22.9 %collective-permute-start.42 = (bf16[64,2048]{1,0:T(8,128)(2,1)}, bf16[64,2048]{1,0:T(8,128)(2,1)}, u32[]{:S(2)}, u32[]{:S(2)}) collective-permute-start(bf16[64,2048]{1,0:T(8,128)(2,1)} %get-tuple-element.252), channel_id=1, source_target_pairs={{0,2},{1,3},{2,4},{3,5},{4,6},{5,7},{6,0},{7,1},{8,10},{9,11},{10,... | collective-permute-start | bytes 786440 | tf_op jit(solution)/shard_map/ppermute | solution.py:77
  626.2 34.5 %collective-permute-start.52 = (bf16[32,4096]{1,0:T(8,128)(2,1)}, bf16[32,4096]{1,0:T(8,128)(2,1)}, u32[]{:S(2)}, u32[]{:S(2)}) collective-permute-start(bf16[32,4096]{1,0:T(8,128)(2,1)} %get-tuple-element.250), channel_id=1, source_target_pairs={{0,6},{1,7},{2,0},{3,1},{4,2},{5,3},{6,4},{7,5},{8,14},{9,15},{10,... | collective-permute-start | bytes 786440 | tf_op jit(solution)/shard_map/ppermute | solution.py:77
  629.2 51.2 %collective-permute-start.51 = (bf16[32,4096]{1,0:T(8,128)(2,1)}, bf16[32,4096]{1,0:T(8,128)(2,1)}, u32[]{:S(2)}, u32[]{:S(2)}) collective-permute-start(bf16[32,4096]{1,0:T(8,128)(2,1)} %get-tuple-element.251), channel_id=1, source_target_pairs={{0,4},{1,5},{2,6},{3,7},{4,0},{5,1},{6,2},{7,3},{8,12},{9,13},{10,... | collective-permute-start | bytes 786440 | tf_op jit(solution)/shard_map/ppermute | solution.py:77
  633.7 46.6 %collective-permute-start.50 = (bf16[32,4096]{1,0:T(8,128)(2,1)S(1)}, bf16[32,4096]{1,0:T(8,128)(2,1)S(1)}, u32[]{:S(2)}, u32[]{:S(2)}) collective-permute-start(bf16[32,4096]{1,0:T(8,128)(2,1)S(1)} %get-tuple-element.249), channel_id=1, source_target_pairs={{0,2},{1,3},{2,4},{3,5},{4,6},{5,7},{6,0},{7,1},{8,10},{9,11},{10,... | collective-permute-start | bytes 786440 | tf_op jit(solution)/shard_map/ppermute | solution.py:77
  646.3 37.0 %collective-permute-start.33 = (bf16[32,4120]{1,0:T(8,128)(2,1)S(1)}, bf16[32,4120]{1,0:T(8,128)(2,1)S(1)}, u32[]{:S(2)}, u32[]{:S(2)}) collective-permute-start(bf16[32,4120]{1,0:T(8,128)(2,1)S(1)} %get-tuple-element.245), channel_id=1, source_target_pairs={{0,6},{1,7},{2,0},{3,1},{4,2},{5,3},{6,4},{7,5},{8,14},{9,15},{10,... | collective-permute-start | bytes 791048 | tf_op jit(solution)/shard_map/ppermute | solution.py:77
  646.3 56.8 %collective-permute-start.32 = (bf16[32,4120]{1,0:T(8,128)(2,1)S(1)}, bf16[32,4120]{1,0:T(8,128)(2,1)S(1)}, u32[]{:S(2)}, u32[]{:S(2)}) collective-permute-start(bf16[32,4120]{1,0:T(8,128)(2,1)S(1)} %get-tuple-element.246), channel_id=1, source_target_pairs={{0,4},{1,5},{2,6},{3,7},{4,0},{5,1},{6,2},{7,3},{8,12},{9,13},{10,... | collective-permute-start | bytes 791048 | tf_op jit(solution)/shard_map/ppermute | solution.py:77
  660.7 42.4 %collective-permute-start.31 = (bf16[32,4120]{1,0:T(8,128)(2,1)S(1)}, bf16[32,4120]{1,0:T(8,128)(2,1)S(1)}, u32[]{:S(2)}, u32[]{:S(2)}) collective-permute-start(bf16[32,4120]{1,0:T(8,128)(2,1)S(1)} %get-tuple-element.244), channel_id=1, source_target_pairs={{0,2},{1,3},{2,4},{3,5},{4,6},{5,7},{6,0},{7,1},{8,10},{9,11},{10,... | collective-permute-start | bytes 791048 | tf_op jit(solution)/shard_map/ppermute | solution.py:77
  680.3 24.5 %collective-permute-start.47 = (bf16[64,2048]{1,0:T(8,128)(2,1)S(1)}, bf16[64,2048]{1,0:T(8,128)(2,1)S(1)}, u32[]{:S(2)}, u32[]{:S(2)}) collective-permute-start(bf16[64,2048]{1,0:T(8,128)(2,1)S(1)} %fusion.131), channel_id=1, source_target_pairs={{0,6},{1,7},{2,0},{3,1},{4,2},{5,3},{6,4},{7,5},{8,14},{9,15},{10,... | collective-permute-start | bytes 786440 | tf_op jit(solution)/shard_map/ppermute | solution.py:77
  680.3 45.2 %collective-permute-start.46 = (bf16[64,2048]{1,0:T(8,128)(2,1)S(1)}, bf16[64,2048]{1,0:T(8,128)(2,1)S(1)}, u32[]{:S(2)}, u32[]{:S(2)}) collective-permute-start(bf16[64,2048]{1,0:T(8,128)(2,1)S(1)} %fusion.131), channel_id=1, source_target_pairs={{0,4},{1,5},{2,6},{3,7},{4,0},{5,1},{6,2},{7,3},{8,12},{9,13},{10,... | collective-permute-start | bytes 786440 | tf_op jit(solution)/shard_map/ppermute | solution.py:77
  683.3 42.2 %collective-permute-start.45 = (bf16[64,2048]{1,0:T(8,128)(2,1)S(1)}, bf16[64,2048]{1,0:T(8,128)(2,1)S(1)}, u32[]{:S(2)}, u32[]{:S(2)}) collective-permute-start(bf16[64,2048]{1,0:T(8,128)(2,1)S(1)} %fusion.131), channel_id=1, source_target_pairs={{0,2},{1,3},{2,4},{3,5},{4,6},{5,7},{6,0},{7,1},{8,10},{9,11},{10,... | collective-permute-start | bytes 786440 | tf_op jit(solution)/shard_map/ppermute | solution.py:77
  703.0 24.4 %collective-permute-start.55 = (bf16[32,4096]{1,0:T(8,128)(2,1)S(1)}, bf16[32,4096]{1,0:T(8,128)(2,1)S(1)}, u32[]{:S(2)}, u32[]{:S(2)}) collective-permute-start(bf16[32,4096]{1,0:T(8,128)(2,1)S(1)} %fusion.128), channel_id=1, source_target_pairs={{0,6},{1,7},{2,0},{3,1},{4,2},{5,3},{6,4},{7,5},{8,14},{9,15},{10,... | collective-permute-start | bytes 786440 | tf_op jit(solution)/shard_map/ppermute | solution.py:77
  703.0 45.3 %collective-permute-start.54 = (bf16[32,4096]{1,0:T(8,128)(2,1)S(1)}, bf16[32,4096]{1,0:T(8,128)(2,1)S(1)}, u32[]{:S(2)}, u32[]{:S(2)}) collective-permute-start(bf16[32,4096]{1,0:T(8,128)(2,1)S(1)} %fusion.128), channel_id=1, source_target_pairs={{0,4},{1,5},{2,6},{3,7},{4,0},{5,1},{6,2},{7,3},{8,12},{9,13},{10,... | collective-permute-start | bytes 786440 | tf_op jit(solution)/shard_map/ppermute | solution.py:77
  704.8 45.8 %collective-permute-start.53 = (bf16[32,4096]{1,0:T(8,128)(2,1)S(1)}, bf16[32,4096]{1,0:T(8,128)(2,1)S(1)}, u32[]{:S(2)}, u32[]{:S(2)}) collective-permute-start(bf16[32,4096]{1,0:T(8,128)(2,1)S(1)} %fusion.128), channel_id=1, source_target_pairs={{0,2},{1,3},{2,4},{3,5},{4,6},{5,7},{6,0},{7,1},{8,10},{9,11},{10,... | collective-permute-start | bytes 786440 | tf_op jit(solution)/shard_map/ppermute | solution.py:77
  725.5 25.3 %collective-permute-start.36 = (bf16[32,4120]{1,0:T(8,128)(2,1)S(1)}, bf16[32,4120]{1,0:T(8,128)(2,1)S(1)}, u32[]{:S(2)}, u32[]{:S(2)}) collective-permute-start(bf16[32,4120]{1,0:T(8,128)(2,1)S(1)} %fusion.114), channel_id=1, source_target_pairs={{0,6},{1,7},{2,0},{3,1},{4,2},{5,3},{6,4},{7,5},{8,14},{9,15},{10,... | collective-permute-start | bytes 791048 | tf_op jit(solution)/shard_map/ppermute | solution.py:77
  725.5 34.4 %collective-permute-start.35 = (bf16[32,4120]{1,0:T(8,128)(2,1)S(1)}, bf16[32,4120]{1,0:T(8,128)(2,1)S(1)}, u32[]{:S(2)}, u32[]{:S(2)}) collective-permute-start(bf16[32,4120]{1,0:T(8,128)(2,1)S(1)} %fusion.114), channel_id=1, source_target_pairs={{0,4},{1,5},{2,6},{3,7},{4,0},{5,1},{6,2},{7,3},{8,12},{9,13},{10,... | collective-permute-start | bytes 791048 | tf_op jit(solution)/shard_map/ppermute | solution.py:77
  727.4 32.5 %collective-permute-start.34 = (bf16[32,4120]{1,0:T(8,128)(2,1)S(1)}, bf16[32,4120]{1,0:T(8,128)(2,1)S(1)}, u32[]{:S(2)}, u32[]{:S(2)}) collective-permute-start(bf16[32,4120]{1,0:T(8,128)(2,1)S(1)} %fusion.114), channel_id=1, source_target_pairs={{0,2},{1,3},{2,4},{3,5},{4,6},{5,7},{6,0},{7,1},{8,10},{9,11},{10,... | collective-permute-start | bytes 791048 | tf_op jit(solution)/shard_map/ppermute | solution.py:77
  748.3 13.2 %collective-permute-start.48 = (bf16[4,64,2048]{2,1,0:T(8,128)(2,1)S(1)}, bf16[4,64,2048]{2,1,0:T(8,128)(2,1)S(1)}, u32[]{:S(2)}, u32[]{:S(2)}) collective-permute-start(bf16[4,64,2048]{2,1,0:T(8,128)(2,1)S(1)} %get-tuple-element.265), channel_id=1, source_target_pairs={{0,1},{1,0},{2,3},{3,2},{4,5},{5,4},{6,7},{7,6},{8,9},{9,8},{10,11... | collective-permute-start | bytes 3145736 | tf_op jit(solution)/shard_map/ppermute | solution.py:65
  750.7 11.8 %collective-permute-start.56 = (bf16[4,32,4096]{2,1,0:T(8,128)(2,1)S(1)}, bf16[4,32,4096]{2,1,0:T(8,128)(2,1)S(1)}, u32[]{:S(2)}, u32[]{:S(2)}) collective-permute-start(bf16[4,32,4096]{2,1,0:T(8,128)(2,1)S(1)} %get-tuple-element.263), channel_id=1, source_target_pairs={{0,1},{1,0},{2,3},{3,2},{4,5},{5,4},{6,7},{7,6},{8,9},{9,8},{10,11... | collective-permute-start | bytes 3145736 | tf_op jit(solution)/shard_map/ppermute | solution.py:65
  (165 other events, 2096.9 us)
Sparse Core Ops, SparseCore 0:
  12.7 55.1 all-gather.5
  70.3 35.3 all-gather.11
  108.1 35.2 all-gather.7
  145.7 52.6 all-gather.9

commit v2 on v1

--- a/solution.py
+++ b/solution.py
@@ -1,6 +1,10 @@
+import functools
+
 import jax
 import jax.numpy as jnp
 from jax import lax
+from jax.experimental import pallas as pl
+from jax.experimental.pallas import tpu as pltpu
 from jax.sharding import PartitionSpec as P
 
 QUERY_HEADS = 8
@@ -92,58 +96,18 @@
     return own, swap_core(own)
 
 
-def split_cols(x, seqs, core):
-    rows, width = x.shape
-    part = width // (2 * seqs)
-    blocks = x.reshape(rows, seqs, 2, part)
-    first, second = blocks[:, :, 0], blocks[:, :, 1]
-    own = jnp.where(core == 0, first, second).reshape(rows, width // 2)
-    other = jnp.where(core == 0, second, first).reshape(rows, width // 2)
-    return own, other
-
-
-def merge_cols(own, other, seqs, core):
-    rows, half = own.shape
-    a = own.reshape(rows, seqs, half // seqs)
-    b = other.reshape(rows, seqs, half // seqs)
-    first = jnp.where(core == 0, a, b)
-    second = jnp.where(core == 0, b, a)
-    return jnp.stack([first, second], axis=2).reshape(rows, 2 * half)
-
-
-def times_weight(x, weight, seqs, core):
-    own, other = split_cols(x, seqs, core)
-    return dot(own, weight[0]) + dot(other, weight[1])
-
-
-def times_weight_t(y, weight, seqs, core):
-    return merge_cols(dot_nt(y, weight[0]), dot_nt(y, weight[1]), seqs, core)
-
-
-def gather_rows(value, seqs):
-    return jnp.concatenate([value] + [seq_swap(value, k) for k in range(1, seqs)], axis=0)
-
-
-def send_blocks(blocks, place, seqs):
-    parts = []
-    for k in range(seqs):
-        piece = lax.dynamic_index_in_dim(blocks, place ^ k, 1, False)
-        parts.append(piece if k == 0 else seq_swap(piece, k))
-    return jnp.concatenate(parts, axis=0)
-
-
-def sum_over_ctx(grad, chips, chip, core):
-    rows, cols = grad.shape
-    halves = grad.reshape(2, rows // 2, cols)
-    mine = lax.dynamic_index_in_dim(halves, core, 0, False)
-    others = lax.dynamic_index_in_dim(halves, 1 - core, 0, False).astype(bf16)
+def scatter_ctx(mine, others, chips, chip):
+    rows, cols = mine.shape
     mine = mine + swap_core(others).astype(f32)
-    shards = mine.reshape(chips, rows // (2 * chips), cols)
+    shards = mine.reshape(chips, rows // chips, cols)
     total = lax.dynamic_index_in_dim(shards, chip, 0, False)
     for k in range(1, chips):
         piece = lax.dynamic_index_in_dim(shards, (chip + k) % chips, 0, False).astype(bf16)
         total = total + chip_shift(piece, k, True).astype(f32)
-    total = total.astype(bf16)
+    return total.astype(bf16)
+
+
+def spread_ctx(total, chips, chip, core):
     got = [total] + [chip_shift(total, k, True) for k in range(1, chips)]
     got = jnp.stack(got, axis=0)
     both = jnp.stack([got, swap_core(got)], axis=0)
@@ -189,6 +153,431 @@
     return jnp.concatenate([first, second], axis=0).astype(f32)
 
 
+def silu_parts(z):
+    sig = 1.0 / (1.0 + jnp.exp(-z))
+    return z * sig, sig * (1.0 + z * (1.0 - sig))
+
+
+def three(a):
+    hi = a.astype(bf16)
+    rest = a - hi.astype(f32)
+    mid = rest.astype(bf16)
+    return hi, mid, (rest - mid.astype(f32)).astype(bf16)
+
+
+def exact_dot(a, b):
+    hi, mid, low = three(a)
+    return dot(hi, b) + dot(mid, b) + dot(low, b)
+
+
+def two(a):
+    hi = a.astype(bf16)
+    return hi, (a - hi.astype(f32)).astype(bf16)
+
+
+def exact_dot_nt(a, b):
+    hi, mid, low = three(a)
+    return dot_nt(hi, b) + dot_nt(mid, b) + dot_nt(low, b)
+
+
+def head_table():
+    head = lax.broadcasted_iota(jnp.int32, (MH, INNER), 0)
+    column = lax.broadcasted_iota(jnp.int32, (MH, INNER), 1)
+    return (column // MP == head).astype(bf16)
+
+
+def column_halves(ref, seqs, hr, is0):
+    first = jnp.concatenate([ref[:, 2 * j * hr : (2 * j + 1) * hr] for j in range(seqs)], axis=1)
+    second = jnp.concatenate(
+        [ref[:, (2 * j + 1) * hr : (2 * j + 2) * hr] for j in range(seqs)], axis=1
+    )
+    return jnp.where(is0, first, second), jnp.where(is0, second, first)
+
+
+def project_kernel(seqs, where_ref, own_ref, sib_ref, tok_ref, gin_ref, nor_ref, pre_ref):
+    x = tok_ref[...].astype(f32)
+    inv = lax.rsqrt(jnp.mean(x * x, axis=1, keepdims=True) + norm_epsilon)
+    nor_ref[...] = (x * inv * gin_ref[...]).astype(bf16)
+    hr = x.shape[1] // (2 * seqs)
+    own, sib = column_halves(nor_ref, seqs, hr, where_ref[1] == 0)
+    wide = own_ref.shape[1]
+    part = 512
+
+    def one(i, carry):
+        a = pl.ds(pl.multiple_of(i * part, part), part)
+        pre_ref[:, a] = dot(own, own_ref[:, a]) + dot(sib, sib_ref[:, a])
+        return carry
+
+    whole = wide // part
+    lax.fori_loop(0, whole, one, 0)
+    if wide % part:
+        at = whole * part
+        pre_ref[:, at:] = dot(own, own_ref[:, at:]) + dot(sib, sib_ref[:, at:])
+
+
+def project(where, own, sib, tokens, gin, seqs):
+    rows, width = tokens.shape
+    wide = own.shape[1]
+    vm = pl.BlockSpec(memory_space=pltpu.VMEM)
+    return pl.pallas_call(
+        functools.partial(project_kernel, seqs),
+        out_shape=(
+            jax.ShapeDtypeStruct((rows, width), bf16),
+            jax.ShapeDtypeStruct((rows, wide), f32),
+        ),
+        in_specs=[pl.BlockSpec(memory_space=pltpu.SMEM)] + [vm] * 4,
+        out_specs=[vm, vm],
+        compiler_params=pltpu.CompilerParams(vmem_limit_bytes=48 * 2**20),
+        cost_estimate=pl.CostEstimate(
+            flops=4 * rows * own.size, bytes_accessed=own.size * 4 + 3 * 2**20, transcendentals=0
+        ),
+        name="project",
+    )(where, own, sib, tokens, gin)
+
+
+def unproject_kernel(
+    seqs, where_ref, own_ref, sib_ref, tok_ref, gin_ref, gres_ref, back_ref, out_ref
+):
+    x = tok_ref[...].astype(f32)
+    rows, width = x.shape
+    hr = width // (2 * seqs)
+    inv = lax.rsqrt(jnp.mean(x * x, axis=1, keepdims=True) + norm_epsilon)
+    unit = x * inv
+    is0 = where_ref[1] == 0
+    wide = own_ref.shape[1]
+    part = 512
+
+    def one(i, carry):
+        a = pl.ds(pl.multiple_of(i * part, part), part)
+        grad = back_ref[:rows, a]
+        return carry[0] + dot_nt(grad, own_ref[:, a]), carry[1] + dot_nt(grad, sib_ref[:, a])
+
+    nothing = jnp.zeros((rows, width // 2), f32)
+    whole = wide // part
+    own, sib = lax.fori_loop(0, whole, one, (nothing, nothing))
+    if wide % part:
+        at = whole * part
+        grad = back_ref[:rows, at:]
+        own = own + dot_nt(grad, own_ref[:, at:])
+        sib = sib + dot_nt(grad, sib_ref[:, at:])
+    first = jnp.where(is0, own, sib)
+    second = jnp.where(is0, sib, own)
+    for j in range(seqs):
+        out_ref[:, 2 * j * hr : (2 * j + 1) * hr] = first[:, j * hr : (j + 1) * hr]
+        out_ref[:, (2 * j + 1) * hr : (2 * j + 2) * hr] = second[:, j * hr : (j + 1) * hr]
+    d_norm = out_ref[...] * gin_ref[...]
+    d_x = inv * (d_norm - unit * jnp.mean(d_norm * unit, axis=1, keepdims=True))
+    out_ref[...] = gres_ref[...] + d_x
+
+
+def unproject(where, own, sib, tokens, gin, grad_res, back, seqs):
+    rows, width = tokens.shape
+    vm = pl.BlockSpec(memory_space=pltpu.VMEM)
+    return pl.pallas_call(
+        functools.partial(unproject_kernel, seqs),
+        out_shape=jax.ShapeDtypeStruct((rows, width), f32),
+        in_specs=[pl.BlockSpec(memory_space=pltpu.SMEM)] + [vm] * 6,
+        out_specs=vm,
+        compiler_params=pltpu.CompilerParams(vmem_limit_bytes=48 * 2**20),
+        cost_estimate=pl.CostEstimate(
+            flops=4 * rows * own.size, bytes_accessed=own.size * 4 + 3 * 2**20, transcendentals=0
+        ),
+        name="unproject",
+    )(where, own, sib, tokens, gin, grad_res, back)
+
+
+def last_grads_kernel(seqs, where_ref, *refs):
+    lefts, rights, keep_ref, give_ref = refs[:seqs], refs[seqs:-2], refs[-2], refs[-1]
+    is0 = where_ref[1] == 0
+    hr, wide = keep_ref.shape
+    rows = lefts[0].shape[0]
+    a = jnp.concatenate([m[:, :hr] for m in lefts], axis=0)
+    b = jnp.concatenate([m[:, hr : 2 * hr] for m in lefts], axis=0)
+    mine, other = jnp.where(is0, a, b), jnp.where(is0, b, a)
+    part = 512
+
+    def piece(src):
+        right = jnp.concatenate([m[:rows, src] for m in rights], axis=0)
+        keep_ref[:, src] = dot_tn(mine, right)
+        give_ref[:, src] = dot_tn(other, right).astype(bf16)
+
+    def one(i, carry):
+        piece(pl.ds(pl.multiple_of(i * part, part), part))
+        return carry
+
+    lax.fori_loop(0, wide // part, one, 0)
+    if wide % part:
+        piece(slice(wide - wide % part, wide))
+
+
+def last_grads(where, lefts, rights, hr, seqs):
+    wide = rights[0].shape[1]
+    vm = pl.BlockSpec(memory_space=pltpu.VMEM)
+    part = pl.BlockSpec((lefts[0].shape[0], 2 * hr), lambda i: (0, 0))
+    whole = pl.BlockSpec(rights[0].shape, lambda i: (0, 0))
+    out = pl.BlockSpec((hr, wide), lambda i: (0, 0))
+    return pl.pallas_call(
+        functools.partial(last_grads_kernel, seqs),
+        grid=(1,),
+        out_shape=(jax.ShapeDtypeStruct((hr, wide), f32), jax.ShapeDtypeStruct((hr, wide), bf16)),
+        in_specs=[pl.BlockSpec(memory_space=pltpu.SMEM)] + [part] * seqs + [whole] * seqs,
+        out_specs=[out, out],
+        compiler_params=pltpu.CompilerParams(vmem_limit_bytes=48 * 2**20),
+        cost_estimate=pl.CostEstimate(
+            flops=4 * seqs * rights[0].size * hr, bytes_accessed=2 * seqs * rights[0].size,
+            transcendentals=0,
+        ),
+        name="last_grads",
+    )(where, *lefts, *rights)
+
+
+def middle_kernel(
+    seqs, where_ref, own_ref, sib_ref, tok_ref, cot_ref, nor_ref, zero_ref, gz_ref, c_ref,
+    ecum_ref, start_ref, att_ref, gmix_ref, gfeed_ref,
+    lay_ref, msg_ref, gres_ref, datt_ref, dssm_ref, dgz_ref, dstart_ref, dc_ref, dcum_ref,
+    ssm, outs, feeds, hids, gates, ups, dhid, dout, dgu,
+):
+    place, core = where_ref[0], where_ref[1]
+    rows, width = tok_ref.shape
+    ff = hids.shape[1]
+    hr = width // (2 * seqs)
+    mixw, attw = INNER // seqs, QW // seqs
+    outw = mixw + attw
+    base_out, base_dn = 2 * ff, 2 * ff + 2 * width
+    is0 = core == 0
+
+    def picked(ref, unit, b):
+        firsts, seconds = [], []
+        for j in range(seqs):
+            at = j * 2 * unit * hr + b * hr
+            firsts.append(ref[:, at : at + hr])
+            seconds.append(ref[:, at + unit * hr : at + unit * hr + hr])
+        first = jnp.concatenate(firsts, axis=1)
+        second = jnp.concatenate(seconds, axis=1)
+        return jnp.where(is0, first, second), jnp.where(is0, second, first)
+
+    def put(ref, unit, b, own, sib):
+        first = jnp.where(is0, own, sib)
+        second = jnp.where(is0, sib, own)
+        for j in range(seqs):
+            at = j * 2 * unit * hr + b * hr
+            ref[:, at : at + hr] = first[:, j * hr : (j + 1) * hr].astype(ref.dtype)
+            at += unit * hr
+            ref[:, at : at + hr] = second[:, j * hr : (j + 1) * hr].astype(ref.dtype)
+
+    table = head_table()
+    c_hi, c_lo = two(c_ref[...])
+    ecum = exact_dot(ecum_ref[...], table)
+    across = (dot_nt(c_hi, start_ref[...]) + dot_nt(c_lo, start_ref[...])) * ecum
+    whole = zero_ref[...] + across
+    silu_z, slope_z = silu_parts(gz_ref[...])
+    gated = whole * silu_z
+    inv_mix = lax.rsqrt(jnp.mean(gated * gated, axis=1, keepdims=True) + norm_epsilon)
+    gmix = gmix_ref[...]
+    ssm[...] = gated * inv_mix
+    mix_b = (ssm[...] * gmix).astype(bf16)
+    for j in range(seqs):
+        outs[:, j * outw : j * outw + mixw] = mix_b[:, j * mixw : (j + 1) * mixw]
+        outs[:, j * outw + mixw : (j + 1) * outw] = att_ref[:, j * attw : (j + 1) * attw]
+    residual = tok_ref[...].astype(f32)
+    for b in range(2):
+        own, sib = picked(outs, 2, b)
+        at = base_out + b * width
+        residual = residual + dot(own, own_ref[:, at : at + width])
+        residual = residual + dot(sib, sib_ref[:, at : at + width])
+    inv_res = lax.rsqrt(jnp.mean(residual * residual, axis=1, keepdims=True) + norm_epsilon)
+    unit_res = residual * inv_res
+    gfeed = gfeed_ref[...]
+    feeds[...] = (unit_res * gfeed).astype(bf16)
+    feed_own, feed_sib = picked(feeds, 1, 0)
+    part = 512
+
+    def forward(i, carry):
+        a = pl.ds(pl.multiple_of(i * part, part), part)
+        u = pl.ds(pl.multiple_of(ff + i * part, part), part)
+        gate = dot(feed_own, own_ref[:, a]) + dot(feed_sib, sib_ref[:, a])
+        up = dot(feed_own, own_ref[:, u]) + dot(feed_sib, sib_ref[:, u])
+        gates[:, a] = gate
+        ups[:, a] = up
+        hids[:, a] = (gate / (1.0 + jnp.exp(-gate)) * up).astype(bf16)
+        return carry
+
+    lax.fori_loop(0, ff // part, forward, 0)
+    layer = residual
+    cot = cot_ref[...]
+    for b in range(2):
+        own, sib = picked(hids, 2, b)
+        at = base_dn + b * width
+        layer = layer + dot(own, own_ref[:, at : at + width])
+        layer = layer + dot(sib, sib_ref[:, at : at + width])
+        put(
+            dhid, 2, b,
+            dot_nt(cot, own_ref[:, at : at + width]),
+            dot_nt(cot, sib_ref[:, at : at + width]),
+        )
+    lay_ref[...] = layer.astype(bf16)
+
+    def backward(i, carry):
+        a = pl.ds(pl.multiple_of(i * part, part), part)
+        u = pl.ds(pl.multiple_of(ff + i * part, part), part)
+        silu_g, slope_g = silu_parts(gates[:, a])
+        grad = dhid[:, a]
+        d_gate = (grad * ups[:, a] * slope_g).astype(bf16)
+        d_up = (grad * silu_g).astype(bf16)
+        dgu[:, a] = d_gate
+        dgu[:, u] = d_up
+        own = dot_nt(d_gate, own_ref[:, a]) + dot_nt(d_up, own_ref[:, u])
+        sib = dot_nt(d_gate, sib_ref[:, a]) + dot_nt(d_up, sib_ref[:, u])
+        return carry[0] + own, carry[1] + sib
+
+    nothing = jnp.zeros((rows, width // 2), f32)
+    own, sib = lax.fori_loop(0, ff // part, backward, (nothing, nothing))
+    put(gres_ref, 1, 0, own, sib)
+    d_feed = gres_ref[...] * gfeed
+    d_res = inv_res * (d_feed - unit_res * jnp.mean(d_feed * unit_res, axis=1, keepdims=True))
+    grad_res = cot.astype(f32) + d_res
+    gres_ref[...] = grad_res
+    res_b = grad_res.astype(bf16)
+    for b in range(2):
+        at = base_out + b * width
+        put(
+            dout, 2, b,
+            dot_nt(res_b, own_ref[:, at : at + width]),
+            dot_nt(res_b, sib_ref[:, at : at + width]),
+        )
+    for j in range(seqs):
+        datt_ref[:, j * attw : (j + 1) * attw] = dout[
+            :, j * outw + mixw : (j + 1) * outw
+        ].astype(bf16)
+        dssm_ref[:, j * mixw : (j + 1) * mixw] = dout[:, j * outw : j * outw + mixw]
+    for k in range(seqs):
+        to = place ^ k
+        at = 0
+        for ref, size in ((nor_ref, 2 * hr), (feeds, 2 * hr), (outs, outw), (hids, ff // seqs)):
+            msg_ref[k, :, at : at + size] = ref[:, pl.ds(pl.multiple_of(to * size, 128), size)]
+            at += size
+        msg_ref[k, :, at : at + 2 * ff] = dgu[...]
+        msg_ref[k, :, at + 2 * ff : at + 2 * ff + width] = cot
+        msg_ref[k, :, at + 2 * ff + width :] = res_b
+    unit_mix = ssm[...]
+    d_norm = dssm_ref[...] * gmix
+    d_gated = inv_mix * (d_norm - unit_mix * jnp.mean(d_norm * unit_mix, axis=1, keepdims=True))
+    dgz_ref[...] = (d_gated * whole * slope_z).astype(bf16)
+    d_ssm = d_gated * silu_z
+    dssm_ref[...] = d_ssm
+    dcum_ref[...] = exact_dot_nt(d_ssm * across, table)
+    da_hi, da_lo = two(d_ssm * ecum)
+    dc_ref[...] = dot(da_hi, start_ref[...]) + dot(da_lo, start_ref[...])
+    dstart_ref[...] = (dot_tn(da_hi, c_hi) + dot_tn(da_hi, c_lo) + dot_tn(da_lo, c_hi)).astype(
+        bf16
+    )
+
+
+def middle(where, own, sib, tokens, cotangent, normed, out_zero, gate_z, c_state, ecum, start,
+           attn_b, gmix, gfeed, seqs):
+    rows, width = tokens.shape
+    ff = own.shape[1] // 2 - 2 * width
+    message = (2 * width + INNER + QW + ff) // seqs + 2 * ff + 2 * width
+    out_shape = (
+        jax.ShapeDtypeStruct((rows, width), bf16),
+        jax.ShapeDtypeStruct((seqs, rows, message), bf16),
+        jax.ShapeDtypeStruct((rows, width), f32),
+        jax.ShapeDtypeStruct((rows, QW), bf16),
+        jax.ShapeDtypeStruct((rows, INNER), f32),
+        jax.ShapeDtypeStruct((rows, INNER), bf16),
+        jax.ShapeDtypeStruct((INNER, NS), bf16),
+        jax.ShapeDtypeStruct((rows, NS), f32),
+        jax.ShapeDtypeStruct((rows, MH), f32),
+    )
+    vm = pl.BlockSpec(memory_space=pltpu.VMEM)
+    scratch = [
+        pltpu.VMEM((rows, INNER), f32),
+        pltpu.VMEM((rows, INNER + QW), bf16),
+        pltpu.VMEM((rows, width), bf16),
+        pltpu.VMEM((rows, ff), bf16),
+        pltpu.VMEM((rows, ff), f32),
+        pltpu.VMEM((rows, ff), f32),
+        pltpu.VMEM((rows, ff), f32),
+        pltpu.VMEM((rows, INNER + QW), f32),
+        pltpu.VMEM((rows, 2 * ff), bf16),
+    ]
+    return pl.pallas_call(
+        functools.partial(middle_kernel, seqs),
+        out_shape=out_shape,
+        in_specs=[pl.BlockSpec(memory_space=pltpu.SMEM)] + [vm] * 13,
+        out_specs=[vm] * len(out_shape),
+        scratch_shapes=scratch,
+        compiler_params=pltpu.CompilerParams(vmem_limit_bytes=56 * 2**20),
+        cost_estimate=pl.CostEstimate(
+            flops=4 * rows * own.size * 2, bytes_accessed=own.size * 4 + 16 * 2**20,
+            transcendentals=rows * 8192,
+        ),
+        name="middle",
+    )(where, own, sib, tokens, cotangent, normed, out_zero, gate_z, c_state, ecum, start,
+      attn_b, gmix, gfeed)
+
+
+def grads_kernel(seqs, ff, where_ref, *refs):
+    msgs, keep_ref, give_ref = refs[:-2], refs[-2], refs[-1]
+    is0 = where_ref[1] == 0
+    hr = keep_ref.shape[0]
+    width = 2 * hr * seqs
+    outw = 4 * hr
+    right = 2 * (2 * hr) + 2 * outw
+    part = 512
+
+    def left(at):
+        return jnp.concatenate([m[:, at : at + hr] for m in msgs], axis=0)
+
+    def segment(first, second, source, target, size):
+        a, b = left(first), left(second)
+        mine, other = jnp.where(is0, a, b), jnp.where(is0, b, a)
+
+        def one(i, carry):
+            src = pl.ds(pl.multiple_of(source + i * part, 128), part)
+            dst = pl.ds(pl.multiple_of(target + i * part, 128), part)
+            rows = jnp.concatenate([m[:, src] for m in msgs], axis=0)
+            keep_ref[:, dst] = dot_tn(mine, rows)
+            give_ref[:, dst] = dot_tn(other, rows).astype(bf16)
+            return carry
+
+        lax.fori_loop(0, size // part, one, 0)
+
+    at_feed, at_out, at_hid = 2 * hr, 4 * hr, 4 * hr + outw
+    segment(at_feed, at_feed + hr, right, 0, 2 * ff)
+    for b in range(2):
+        segment(
+            at_out + b * hr, at_out + (b + 2) * hr, right + 2 * ff + width,
+            2 * ff + b * width, width,
+        )
+        segment(
+            at_hid + b * hr, at_hid + (b + 2) * hr, right + 2 * ff,
+            2 * ff + (2 + b) * width, width,
+        )
+
+
+def grads(where, msgs, ff, seqs):
+    hr = (msgs[0].shape[1] - 2 * ff) // (12 + 4 * seqs)
+    columns = 2 * ff + 8 * hr * seqs
+    vm = pl.BlockSpec(memory_space=pltpu.VMEM)
+    return pl.pallas_call(
+        functools.partial(grads_kernel, seqs, ff),
+        out_shape=(
+            jax.ShapeDtypeStruct((hr, columns), f32),
+            jax.ShapeDtypeStruct((hr, columns), bf16),
+        ),
+        in_specs=[pl.BlockSpec(memory_space=pltpu.SMEM)] + [vm] * len(msgs),
+        out_specs=[vm, vm],
+        compiler_params=pltpu.CompilerParams(vmem_limit_bytes=56 * 2**20),
+        cost_estimate=pl.CostEstimate(
+            flops=4 * msgs[0].shape[0] * seqs * hr * columns,
+            bytes_accessed=2 * seqs * msgs[0].size + 6 * hr * columns,
+            transcendentals=0,
+        ),
+        name="grads",
+    )(where, *msgs)
+
+
 def body(
     tokens,
     cotangent,
@@ -235,13 +624,27 @@
     gmix = pieces[3].reshape(-1)
     taps = pieces[4].reshape(seqs, KC, -1).transpose(1, 0, 2).reshape(KC, -1)
 
-    in_loc = jnp.concatenate([w_query, key_weight, value_weight, w_mixin], axis=1)
+    used = QW + 2 * KW + w_mixin.shape[1]
+    wide = -(-used // 128) * 128
+    blank = jnp.zeros((w_mixin.shape[0], wide - used), bf16)
+    in_loc = jnp.concatenate([w_query, key_weight, value_weight, w_mixin, blank], axis=1)
+    w_in = gather_weight(in_loc, core)
     out_loc = jnp.concatenate([w_mixout, w_attnout], axis=0)
-    gu_loc = jnp.concatenate([w_gate, w_up], axis=1)
-    w_in = gather_weight(in_loc, core)
-    w_out = gather_weight(out_loc, core)
-    w_gu = gather_weight(gu_loc, core)
-    w_dn = gather_weight(w_down, core)
+    half_out = take_half(out_loc, core)
+    half_dn = take_half(w_down, core)
+    hr = half_out.shape[0] // 2
+    rest = jnp.concatenate(
+        [
+            take_half(w_gate, core),
+            take_half(w_up, core),
+            half_out[:hr],
+            half_out[hr:],
+            half_dn[:hr],
+            half_dn[hr:],
+        ],
+        axis=1,
+    )
+    where = jnp.stack([place, core]).astype(jnp.int32)
 
     first_row = ctx * rows
     position = first_row + jnp.arange(rows, dtype=jnp.int32)
@@ -253,15 +656,17 @@
     sine = jnp.sin(angles)[:, None, :]
 
     x = tokens.astype(f32)
-    normed = rms_scale(x, gin).astype(bf16)
-    pre = times_weight(normed, w_in, seqs, core)
+    rest, kept_in = lax.optimization_barrier((rest, w_in[0]))
+    w_in = (kept_in, w_in[1])
+    rest_own = lax.all_gather(rest, "seq", axis=0, tiled=True)
+    normed, pre = project(where, w_in[0], w_in[1], tokens, gin[None, :], seqs)
     q_pre = pre[:, :QW].reshape(rows, QUERY_HEADS, HEAD_SIZE)
     k_pre = pre[:, QW : QW + KW].reshape(rows, VALUE_HEADS, HEAD_SIZE)
     v_low = pre[:, QW + KW : QW + 2 * KW].astype(bf16)
     mix0 = QW + 2 * KW
     gate_z = pre[:, mix0 : mix0 + INNER]
     conv_low = pre[:, mix0 + INNER : mix0 + INNER + CONVW].astype(bf16)
-    raw_step = pre[:, mix0 + INNER + CONVW :]
+    raw_step = pre[:, mix0 + INNER + CONVW : used]
 
     queries = rotary_apply(q_pre, cosine, sine).astype(bf16)
     keys = rotary_apply(k_pre, cosine, sine).astype(bf16).reshape(rows, KW)
@@ -308,11 +713,12 @@
         local_state = jnp.einsum(
             "shp,sn->hpn", tail[:, :, None] * head_input, b_state, precision=highest
         )
-        return out_zero, local_state, jnp.exp(cum[-1]), c_state, jnp.exp(cum)
-
-    (out_zero, local_state, own_decay, c_state, exp_cum), pull_local = jax.vjp(
+        return out_zero, local_state, jnp.exp(cum[-1]), c_state, cum
+
+    (out_zero, local_state, own_decay, c_state, cum), pull_local = jax.vjp(
         ssm_local, extended, raw_step, taps, cbias, step_offset, decay_rate, skip_gain
     )
+    exp_cum = jnp.exp(cum)
     start_state = ctx_state(local_state, decays, chips, chip, core, False)
 
     qpos = jnp.tile(position, GROUP)
@@ -338,6 +744,8 @@
     scores = jnp.einsum("hrd,hkd->hrk", query_rows, key_heads, preferred_element_type=f32) * scale
     masked = jnp.where(allowed[None], scores, -1e30)
     top = jnp.max(masked, axis=-1, keepdims=True)
+    top, rest_own = lax.optimization_barrier((top, rest_own))
+    rest_sib = swap_core(rest_own)
     expanded = jnp.exp(masked - top)
     prob = expanded / jnp.sum(expanded, axis=-1, keepdims=True)
     prob_low = prob.astype(bf16)
@@ -349,72 +757,15 @@
         .reshape(rows, QW)
     )
 
-    def finish(zero_in, c_in, exp_in, start_in, gate_in, gain_in):
-        across = jnp.einsum("tn,hpn->thp", c_in, start_in, precision=highest) * exp_in[:, :, None]
-        gated = (zero_in + across).reshape(rows, INNER) * jax.nn.silu(gate_in)
-        return rms_scale(gated, gain_in)
-
-    mix_normed, pull_finish = jax.vjp(
-        finish, out_zero, c_state, exp_cum, start_state, gate_z, gmix
-    )
-    mix_b = mix_normed.astype(bf16)
-
-    out_in = jnp.concatenate(
-        [
-            mix_b.reshape(rows, seqs, INNER // seqs),
-            attn_b.reshape(rows, seqs, QW // seqs),
-        ],
-        axis=2,
-    )
-    out_flat = out_in.reshape(rows, INNER + QW)
-    residual = x + times_weight(out_flat, w_out, seqs, core)
-    feed_b, pull_feed = jax.vjp(rms_scale, residual, gfeed)
-    feed_b = feed_b.astype(bf16)
-    gate_up = times_weight(feed_b, w_gu, seqs, core)
-    gate, up = gate_up[:, :ff], gate_up[:, ff:]
-    hidden, pull_hidden = jax.vjp(lambda a, b: jax.nn.silu(a) * b, gate, up)
-    hidden_b = hidden.astype(bf16)
-    layer_out = (residual + times_weight(hidden_b, w_dn, seqs, core)).astype(bf16)
-
-    left = jnp.concatenate(
-        [
-            normed.reshape(rows, seqs, -1),
-            feed_b.reshape(rows, seqs, -1),
-            out_in,
-            hidden_b.reshape(rows, seqs, -1),
-        ],
-        axis=2,
-    )
-    left = send_blocks(left, place, seqs)
-    wide = width // seqs
-    outw = (INNER + QW) // seqs
-    left_normed = left[:, :wide]
-    left_feed = left[:, wide : 2 * wide]
-    left_out = left[:, 2 * wide : 2 * wide + outw]
-    left_hidden = left[:, 2 * wide + outw :]
-
-    d_hidden = times_weight_t(cotangent, w_dn, seqs, core)
-    d_gate, d_up = pull_hidden(d_hidden)
-    d_gu = jnp.concatenate([d_gate, d_up], axis=1).astype(bf16)
-    d_feed = times_weight_t(d_gu, w_gu, seqs, core)
-    d_res_norm, d_gfeed = pull_feed(d_feed)
-    grad_res = cotangent.astype(f32) + d_res_norm
-    res_b = grad_res.astype(bf16)
-    d_out = times_weight_t(res_b, w_out, seqs, core).reshape(rows, seqs, outw)
-    d_mix = d_out[:, :, : INNER // seqs].reshape(rows, INNER)
-    d_att = d_out[:, :, INNER // seqs :].reshape(rows, QW).astype(bf16)
-
-    right = gather_rows(jnp.concatenate([d_gu, cotangent, res_b], axis=1), seqs)
-    grad_gu = dot_tn(left_feed, right[:, : 2 * ff])
-    grad_dn = dot_tn(left_hidden, right[:, 2 * ff : 2 * ff + width])
-    grad_out = dot_tn(left_out, right[:, 2 * ff + width :])
-    sum_gu = sum_over_ctx(grad_gu, chips, chip, core)
-    sum_do = sum_over_ctx(
-        jnp.concatenate([grad_dn, grad_out], axis=1), chips, chip, core
-    )
-
-    d_zero, d_c, d_exp, d_start, d_gate_z, d_gmix = pull_finish(d_mix)
-    later_grad = ctx_state(d_start, decays, chips, chip, core, True)
+    layer_out, msg, grad_res, d_att, d_ssm, d_gate_z, d_start, d_c, d_cum = middle(
+        where, rest_own, rest_sib, tokens, cotangent, normed,
+        out_zero.reshape(rows, INNER), gate_z, c_state, exp_cum,
+        start_state.reshape(INNER, NS).astype(bf16), attn_b, gmix[None, :], gfeed[None, :], seqs,
+    )
+    msgs = [msg[0]] + [seq_swap(msg[k], k) for k in range(1, seqs)]
+    keep, give = grads(where, msgs, ff, seqs)
+
+    later_grad = ctx_state(d_start.reshape(MH, MP, NS), decays, chips, chip, core, True)
     decay_grad = jnp.sum(later_grad * start_state, axis=(1, 2))
 
     grad_rows = (
@@ -451,7 +802,7 @@
     d_v = d_kv_own[:, KW:].astype(bf16)
 
     d_ext, d_step, d_taps, d_cbias, d_offset, d_rate, d_skip = pull_local(
-        (d_zero, later_grad, decay_grad, d_c, d_exp)
+        (d_ssm.reshape(rows, MH, MP), later_grad, decay_grad, d_c, d_cum)
     )
     edge_back = lax.ppermute(
         d_ext[: KC - 1], "ctx", [(i + 1, i) for i in range(count - 1)]
@@ -461,51 +812,100 @@
         [d_conv[: rows - (KC - 1)], d_conv[rows - (KC - 1) :] + edge_back], axis=0
     )
     d_pre = jnp.concatenate(
-        [d_q, d_k, d_v, d_gate_z.astype(bf16), d_conv.astype(bf16), d_step.astype(bf16)], axis=1
-    )
-
-    right_in = gather_rows(d_pre, seqs)
-    d_normed = times_weight_t(d_pre, w_in, seqs, core)
-    unused, pull_input = jax.vjp(rms_scale, x, gin)
-    d_x, d_gin = pull_input(d_normed)
-    grad_tokens = grad_res + d_x
-    parts = (d_gin, d_gfeed, d_cbias, d_gmix, d_taps.reshape(-1), d_offset, d_rate, d_skip)
-    sums = lax.psum(jnp.concatenate(parts), ("seq", "ctx"))
-    out_small = []
-    at = 0
-    for part in parts:
-        out_small.append(sums[at : at + part.size])
-        at += part.size
+        [d_q, d_k, d_v, d_gate_z, d_conv.astype(bf16), d_step.astype(bf16), jnp.zeros((rows, wide - used), bf16)], axis=1
+    )
+
+    last = jnp.concatenate([d_cbias, d_offset, d_rate, d_skip])
+    extra = jnp.stack(
+        [
+            jnp.pad(d_taps[:2].reshape(-1), (0, wide - 2 * CONVW)),
+            jnp.pad(d_taps[2:].reshape(-1), (0, wide - 2 * CONVW)),
+            jnp.pad(last, (0, wide - last.size)),
+        ]
+    )
+    extra_hi = extra.astype(bf16)
+    extra_lo = (extra - extra_hi.astype(f32)).astype(bf16)
+    back_msg = jnp.concatenate([d_pre, extra_hi, extra_lo, jnp.zeros((10, wide), bf16)], axis=0)
+    back_msg, keep, give = lax.optimization_barrier((back_msg, keep, give))
+    total_rest = scatter_ctx(keep, give, chips, chip)
+    backs = [back_msg] + [seq_swap(back_msg, k) for k in range(1, seqs)]
+
+    grad_tokens = unproject(
+        where, w_in[0], w_in[1], tokens, gin[None, :], grad_res, back_msg, seqs
+    )
+
+    smalls = [
+        (m[rows : rows + 3].astype(f32) + m[rows + 3 : rows + 6].astype(f32)) for m in backs
+    ]
+    while len(smalls) > 1:
+        smalls = [smalls[i] + smalls[i + 1] for i in range(0, len(smalls), 2)]
+    small_sum = smalls[0]
+    small_taps = small_sum[:2, : 2 * CONVW].reshape(KC, CONVW)
 
     def own_share(vec):
         size = vec.shape[-1] // seqs
         return lax.dynamic_slice_in_dim(vec, place * size, size, vec.ndim - 1)
 
-    grad_in = dot_tn(left_normed, right_in)
-    sum_in = sum_over_ctx(grad_in, chips, chip, core).astype(f32)
-    sum_gu = sum_gu.astype(f32)
-    sum_do = sum_do.astype(f32)
+    flat = jnp.concatenate(
+        [
+            own_share(small_taps).reshape(-1),
+            own_share(small_sum[2, :CONVW]),
+            small_sum[2, CONVW : CONVW + 3 * MH],
+        ]
+    )
+    step = 1
+    while step < ctxs:
+        flat = flat + lax.ppermute(flat, "ctx", [(i, i ^ step) for i in range(ctxs)])
+        step *= 2
+    own_conv = CONVW // seqs
+    out_taps = flat[: KC * own_conv].reshape(KC, own_conv)
+    out_cbias = flat[KC * own_conv : (KC + 1) * own_conv]
+    heads = flat[(KC + 1) * own_conv :]
+
+    backs[0], total_rest = lax.optimization_barrier((backs[0], total_rest))
+    keep_in, give_in = last_grads(where, msgs, backs, hr, seqs)
+    total_in = scatter_ctx(keep_in, give_in, chips, chip)
+    sum_rest = spread_ctx(total_rest, chips, chip, core)
+    sum_in = spread_ctx(total_in, chips, chip, core).astype(f32)
+    sum_rest = sum_rest.astype(f32)
+    sum_gate, sum_up = sum_rest[:, :ff], sum_rest[:, ff : 2 * ff]
+
+    def unfold(first, second):
+        first = first.reshape(2, hr, width)
+        second = second.reshape(2, hr, width)
+        return jnp.stack([first, second], axis=1).reshape(4 * hr, width)
+
+    at = 2 * ff
+    sum_out = unfold(sum_rest[:, at : at + width], sum_rest[:, at + width : at + 2 * width])
+    at += 2 * width
+    sum_dn = unfold(sum_rest[:, at : at + width], sum_rest[:, at + width : at + 2 * width])
     mixo = INNER // seqs
+    grad_gin = jnp.sum(sum_in * in_loc.astype(f32), axis=1) / gain_input.astype(f32)
+    grad_gfeed = (
+        jnp.sum(sum_gate * w_gate.astype(f32), axis=1)
+        + jnp.sum(sum_up * w_up.astype(f32), axis=1)
+    ) / gain_feed.astype(f32)
+    grad_gmix = jnp.sum(sum_out[:mixo] * w_mixout.astype(f32), axis=1) / gain_mixer.astype(f32)
     return (
         layer_out,
         grad_tokens,
-        own_share(out_small[0]),
+        grad_gin,
         sum_in[:, :QW],
         sum_in[:, QW : QW + KW],
         sum_in[:, QW + KW : mix0],
-        sum_in[:, mix0:],
-        own_share(out_small[4].reshape(KC, CONVW)),
-        own_share(out_small[2]),
-        out_small[5],
-        out_small[6],
-        out_small[7],
-        own_share(out_small[3]),
-        sum_do[:mixo, width:],
-        sum_do[mixo:, width:],
-        own_share(out_small[1]),
-        sum_gu[:, :ff],
-        sum_gu[:, ff:],
-        sum_do[:, :width],
+        sum_in[:, mix0:used],
+        out_taps,
+        out_cbias,
+        heads[:MH],
+        heads[MH : 2 * MH],
+        heads[2 * MH :],
+        grad_gmix,
+        sum_out[:mixo],
+        sum_out[mixo:],
+        grad_gfeed,
+        sum_gate,
+        sum_up,
+        sum_dn,
     )
 
 

time: 799 us -> 603 us (0.75)
  the two profiles are of different devices: /device:TPU:1 before, /device:TPU:25 now
where the time goes in v2:
time: 603 us; the launch traced here: 592 us
  waiting for transfers between devices  240 us (40%)
  local copies, waits for them, and re-layouts  92.1 us (15%)
  other arithmetic  78.2 us (13%)
  starting transfers between devices  61.7 us (10%)
  Pallas kernels  55.8 us (9%)
  matrix products  36.1 us (6%)
  between operations  16.8 us (3%)
  blocking collectives  11.7 us (2%)
    ppermute x24, waiting for transfers between devices, chip_shift(): return lax.ppermute(value, 'ctx', pairs)  127 us
    all_gather x1, waiting for transfers between devices, gather_weight(): own = lax.all_gather(take_half(local, core), 'seq', axis=0, tiled=True)  47.8 us
    all_gather x1, waiting for transfers between devices, body(): rest_own = lax.all_gather(rest, 'seq', axis=0, tiled=True)  40.2 us
    ppermute x24, starting transfers between devices, chip_shift(): return lax.ppermute(value, 'ctx', pairs)  34 us
    pallas_call x1, Pallas kernels, middle(): pl.pallas_call(functools.partial(middle_kernel, seqs), out_shape=out_shap...  23.5 us
    unnamed x239, local copies, waits for them, and re-layouts  22.6 us
    ppermute x12, starting transfers between devices, swap_core(): return lax.ppermute(value, 'ctx', [(i, i ^ 1) for i in range(count)])  18.2 us
  transfers between devices with their start and end apart: 49, of which 22 were waited for; matrix products, arithmetic and copies ran while one was open for 25% of the time, Pallas kernels for 3%

profile of v2, /device:TPU:25, one launch (start us, length us, event | category | flops | bytes accessed | tf_op | source)
XLA Modules:
  0.0 592.4 jit_solution(3693464853898355878)
XLA Ops:
  7.3 3.8 copy.190
  11.2 3.7 concatenate.81
  23.1 47.8 %all-gather.4.cloned.1.call-done.own_ref = bf16[512,4224]{1,0:T(8,128)(2,1)} async-done(((bf16[128,4224]{1,0:T(8,128)(2,1)}), bf16[512,4224]{1,0:T(8,128)(2,1)}) %all-gather.4.cloned.1.call-update) | async-done | bytes 4325392 | tf_op jit(solution)/shard_map/all_gather | solution.py:95
  73.5 11.7 %all-reduce.17 = bf16[12544]{0:T(1024)(128)(2,1)S(1)} all-reduce(bf16[12544]{0:T(1024)(128)(2,1)S(1)} %dynamic-update-slice.4), channel_id=2, replica_groups=mesh['seq'=4,'ctx'=8] {'seq'}, use_global_device_ids=true, to_apply=%add.17 | all-reduce | flops 12544 | bytes 50176
  87.4 6.6 %project.1 = (bf16[128,1024]{1,0:T(8,128)(2,1)S(1)}, f32[128,4224]{1,0:T(8,128)S(1)}) custom-call(s32[2]{0:T(128)S(1)} %pad_add_fusion.3.where_ref, bf16[512,4224]{1,0:T(8,128)(2,1)} %all-gather.4.cloned.1.call-done.own_ref, bf16[512,4224]{1,0:T(8,128)(2,1)} %collective-permute-done.sib_ref, bf16[128,1024]{1,0:T(8,128)(2,1)S(1)} %copy-done, ...), custom_call_target="tpu_custom_call" | custom-call | flops 1107296256 | bytes 11796480 | tf_op jit(solution)/shard_map/project/pallas_call | solution.py:222
  106.0 5.6 collective-permute-start.4
  116.7 4.1 fusion
  120.8 40.2 %all-gather.6.cloned.1.call-done.own_ref = bf16[512,8192]{1,0:T(8,128)(2,1)} async-done(((bf16[128,8192]{1,0:T(8,128)(2,1)}), bf16[512,8192]{1,0:T(8,128)(2,1)}) %all-gather.6.cloned.1.call-update) | async-done | bytes 8388624 | tf_op jit(solution)/shard_map/all_gather | solution.py:661
  190.8 5.2 collective-permute-done.10
  196.0 4.6 collective-permute-done.8
  200.5 6.9 %collective-permute-done.9 = bf16[12,64,128]{2,1,0:T(8,128)(2,1)S(1)} collective-permute-done((bf16[12,64,128]{2,1,0:T(8,128)(2,1)S(1)}, bf16[12,64,128]{2,1,0:T(8,128)(2,1)S(1)}, u32[]{:S(2)}, u32[]{:S(2)}) %collective-permute-start.9) | collective-permute-done | bytes 196640 | tf_op jit(solution)/shard_map/ppermute | solution.py:81
  209.8 4.2 fusion.19
  218.9 3.5 fusion.2
  224.8 23.5 %middle.1 = (bf16[128,1024]{1,0:T(8,128)(2,1)}, bf16[4,128,7680]{2,1,0:T(8,128)(2,1)}, f32[128,1024]{1,0:T(8,128)}, bf16[128,512]{1,0:T(8,128)(2,1)}, f32[128,15...) custom-call(s32[2]{0:T(128)} %copy-done.4, ...), custom_call_target="tpu_custom_call" | custom-call | flops 4294967296 | bytes 33554432 | tf_op jit(solution)/shard_map/middle/pallas_call | solution.py:504
  249.4 4.1 fusion.27
  253.5 3.4 multiply_reduce_fusion.1
  258.9 4.3 multiply_convert_fusion
  273.2 2.3 copy.211
  277.5 5.8 slice_bitcast_fusion
  284.9 4.4 fusion.34
  321.8 2.8 collective-permute-start.19
  328.7 3.0 collective-permute-done.19
  344.7 2.8 fusion.16
  347.5 2.3 copy.212
  349.8 2.7 broadcast_multiply_fusion
  352.6 2.4 broadcast_multiply_fusion.1
  363.1 2.8 collective-permute-start.21
  371.6 11.4 %grads.1 = (f32[128,8192]{1,0:T(8,128)}, bf16[128,8192]{1,0:T(8,128)(2,1)}) custom-call(s32[2]{0:T(128)} %copy-done.4, bf16[128,7680]{1,0:T(8,128)(2,1)} %get-tuple-element.247.refs_0_, bf16[128,7680]{1,0:T(8,128)(2,1)} %collective-permute-done.22.refs_1_, bf16[128,7680]{1,0:T(8,128)(2,1)} %collective-permute-done.23.refs_2_, ...), custom_call_target="tpu_custom_call" | custom-call | flops 2147483648 | bytes 14155776 | tf_op jit(solution)/shard_map/grads/pallas_call | solution.py:563
  383.0 2.3 collective-permute-start.25
  385.4 4.0 collective-permute-done.25
  389.4 2.7 convert_add_fusion
  394.3 4.5 collective-permute-start.26
  400.8 9.3 %collective-permute-done.26 = bf16[32,8192]{1,0:T(8,128)(2,1)S(1)} collective-permute-done((bf16[32,8192]{1,0:T(8,128)(2,1)S(1)}, bf16[32,8192]{1,0:T(8,128)(2,1)S(1)}, u32[]{:S(2)}, u32[]{:S(2)}) %collective-permute-start.26) | collective-permute-done | bytes 524320 | tf_op jit(solution)/shard_map/ppermute | solution.py:81
  411.2 31.9 %collective-permute-done.27 = bf16[32,8192]{1,0:T(8,128)(2,1)} collective-permute-done((bf16[32,8192]{1,0:T(8,128)(2,1)S(1)}, bf16[32,8192]{1,0:T(8,128)(2,1)}, u32[]{:S(2)}, u32[]{:S(2)}) %collective-permute-start.27) | collective-permute-done | bytes 524320 | tf_op jit(solution)/shard_map/ppermute | solution.py:81
  444.9 8.8 %collective-permute-done.31.refs_7_ = bf16[144,4224]{1,0:T(8,128)(2,1)S(1)} collective-permute-done((bf16[144,4224]{1,0:T(8,128)(2,1)S(1)}, bf16[144,4224]{1,0:T(8,128)(2,1)S(1)}, u32[]{:S(2)}, u32[]{:S(2)}) %collective-permute-start.31) | collective-permute-done | bytes 1216544 | tf_op jit(solution)/shard_map/ppermute | solution.py:86
  453.7 5.2 last_grads.1
  461.2 2.9 collective-permute-start.43
  467.8 3.2 collective-permute-start.33
  471.0 4.8 collective-permute-done.43
  477.2 44.8 %collective-permute-done.44 = bf16[32,8192]{1,0:T(8,128)(2,1)S(1)} collective-permute-done((bf16[32,8192]{1,0:T(8,128)(2,1)S(1)}, bf16[32,8192]{1,0:T(8,128)(2,1)S(1)}, u32[]{:S(2)}, u32[]{:S(2)}) %collective-permute-start.44) | collective-permute-done | bytes 524320 | tf_op jit(solution)/shard_map/ppermute | solution.py:81
  522.1 2.4 fusion.130
  525.8 3.4 collective-permute-done.40
  529.3 5.0 collective-permute-done.41
  535.7 2.4 collective-permute-start.37
  539.5 9.0 %unproject.1 = f32[128,1024]{1,0:T(8,128)} custom-call(s32[2]{0:T(128)S(1)} %copy-done.5, bf16[512,4224]{1,0:T(8,128)(2,1)} %all-gather.4.cloned.1.call-done.own_ref, bf16[512,4224]{1,0:T(8,128)(2,1)} %collective-permute-done.sib_ref, bf16[128,1024]{1,0:T(8,128)(2,1)S(1)} %copy-done.1, f32[1,1024]{1,0:T(1,128)S(1)} %bitcast.283, f32[128,1024]{1,0:T(8,128)S(1)} %copy-done.2, ...), custom_call_target="tpu_custom_call" | custom-call | flops 1107296256 | bytes 11796480 | tf_op jit(solution)/shard_map/unproject/pallas_call | solution.py:276
  550.4 11.2 %collective-permute-done.37 = bf16[32,4224]{1,0:T(8,128)(2,1)S(1)} collective-permute-done((bf16[32,4224]{1,0:T(8,128)(2,1)S(1)}, bf16[32,4224]{1,0:T(8,128)(2,1)S(1)}, u32[]{:S(2)}, u32[]{:S(2)}) %collective-permute-start.37) | collective-permute-done | bytes 270368 | tf_op jit(solution)/shard_map/ppermute | solution.py:81
  573.1 2.5 multiply_reduce_fusion.2
  581.7 2.9 copy.223
  (522 shorter events, 186.4 us)
Async XLA Ops:
  7.2 63.7 %all-gather.4.cloned.1.call-start = ((), (), s32[]{:S(2)}) async-start(), calls=%async_computation | async-start | bytes 5406720 | tf_op jit(solution)/shard_map/all_gather | solution.py:95
  16.0 145.0 %all-gather.6.cloned.1.call-start = ((), (), s32[]{:S(2)}) async-start(), calls=%async_computation.1 | async-start | bytes 10485760 | tf_op jit(solution)/shard_map/all_gather | solution.py:661
  70.9 16.4 %collective-permute-start = (bf16[512,4224]{1,0:T(8,128)(2,1)}, bf16[512,4224]{1,0:T(8,128)(2,1)}, u32[]{:S(2)}, u32[]{:S(2)}) collective-permute-start(bf16[512,4224]{1,0:T(8,128)(2,1)} %all-gather.4.cloned.1.call-done.own_ref), channel_id=1, source_target_pairs={{0,1},{1,0},{2,3},{3,2},{4,5},{5,4},{6,7},{7,6},{8,9},{9,8},{10,11... | collective-permute-start | bytes 12976136 | tf_op jit(solution)/shard_map/ppermute | solution.py:69
  98.3 3.8 collective-permute-start.1
  98.6 4.4 collective-permute-start.2
  99.8 5.3 collective-permute-start.3
  106.0 6.9 %collective-permute-start.4 = (bf16[4,144,256]{2,1,0:T(8,128)(2,1)S(1)}, bf16[4,144,256]{2,1,0:T(8,128)(2,1)}, u32[]{:S(2)}, u32[]{:S(2)}) collective-permute-start(bf16[4,144,256]{2,1,0:T(8,128)(2,1)S(1)} %pad_maximum_fusion.9), channel_id=1, source_target_pairs={{0,1},{1,0},{2,3},{3,2},{4,5},{5,4},{6,7},{7,6},{8,9},{9,8},{10,11... | collective-permute-start | bytes 884744 | tf_op jit(solution)/shard_map/ppermute | solution.py:69
  161.0 63.7 %collective-permute-start.5 = (bf16[512,8192]{1,0:T(8,128)(2,1)}, bf16[512,8192]{1,0:T(8,128)(2,1)}, u32[]{:S(2)}, u32[]{:S(2)}) collective-permute-start(bf16[512,8192]{1,0:T(8,128)(2,1)} %all-gather.6.cloned.1.call-done.own_ref), channel_id=1, source_target_pairs={{0,1},{1,0},{2,3},{3,2},{4,5},{5,4},{6,7},{7,6},{8,9},{9,8},{10,11... | collective-permute-start | bytes 25165832 | tf_op jit(solution)/shard_map/ppermute | solution.py:69
  165.6 8.8 %collective-permute-start.6 = (bf16[3,1792]{1,0:T(4,128)(2,1)S(1)}, bf16[3,1792]{1,0:T(4,128)(2,1)S(1)}, u32[]{:S(2)}, u32[]{:S(2)}) collective-permute-start(bf16[3,1792]{1,0:T(4,128)(2,1)S(1)} %slice.469), channel_id=1, source_target_pairs={{0,1},{1,2},{2,3},{3,4},{4,5},{5,6},{6,7},{8,9},{9,10},{10,11},{11... | collective-permute-start | bytes 32264 | tf_op jit(solution)/shard_map/ppermute | solution.py:690
  186.1 9.8 %collective-permute-start.10 = (bf16[12,64,128]{2,1,0:T(8,128)(2,1)S(1)}, bf16[12,64,128]{2,1,0:T(8,128)(2,1)S(1)}, u32[]{:S(2)}, u32[]{:S(2)}) collective-permute-start(bf16[12,64,128]{2,1,0:T(8,128)(2,1)S(1)} %fusion.67), channel_id=1, source_target_pairs={{0,6},{1,7},{8,14},{9,15},{16,22},{17,23},{24,30},{25,31}} | collective-permute-start | bytes 589832 | tf_op jit(solution)/shard_map/ppermute | solution.py:81
  187.4 13.1 %collective-permute-start.8 = (bf16[12,64,128]{2,1,0:T(8,128)(2,1)S(1)}, bf16[12,64,128]{2,1,0:T(8,128)(2,1)S(1)}, u32[]{:S(2)}, u32[]{:S(2)}) collective-permute-start(bf16[12,64,128]{2,1,0:T(8,128)(2,1)S(1)} %fusion.67), channel_id=1, source_target_pairs={{0,2},{1,3},{2,4},{3,5},{4,6},{5,7},{8,10},{9,11},{10,12},{11,13},... | collective-permute-start | bytes 589832 | tf_op jit(solution)/shard_map/ppermute | solution.py:81
  188.7 18.7 %collective-permute-start.9 = (bf16[12,64,128]{2,1,0:T(8,128)(2,1)S(1)}, bf16[12,64,128]{2,1,0:T(8,128)(2,1)S(1)}, u32[]{:S(2)}, u32[]{:S(2)}) collective-permute-start(bf16[12,64,128]{2,1,0:T(8,128)(2,1)S(1)} %fusion.67), channel_id=1, source_target_pairs={{0,4},{1,5},{2,6},{3,7},{8,12},{9,13},{10,14},{11,15},{16,20},{17,... | collective-permute-start | bytes 589832 | tf_op jit(solution)/shard_map/ppermute | solution.py:81
  208.5 7.8 %collective-permute-start.11 = (bf16[12,64,128]{2,1,0:T(8,128)(2,1)}, bf16[12,64,128]{2,1,0:T(8,128)(2,1)}, u32[]{:S(2)}, u32[]{:S(2)}) collective-permute-start(bf16[12,64,128]{2,1,0:T(8,128)(2,1)} %select_convert_fusion.2), channel_id=1, source_target_pairs={{0,1},{1,0},{2,3},{3,2},{4,5},{5,4},{6,7},{7,6},{8,9},{9,8},{10,11... | collective-permute-start | bytes 589832 | tf_op jit(solution)/shard_map/ppermute | solution.py:69
  283.4 86.5 %collective-permute-start.22 = (bf16[128,7680]{1,0:T(8,128)(2,1)}, bf16[128,7680]{1,0:T(8,128)(2,1)}, u32[]{:S(2)}, u32[]{:S(2)}) collective-permute-start(bf16[128,7680]{1,0:T(8,128)(2,1)} %get-tuple-element.246), channel_id=1, source_target_pairs={{0,8},{8,0},{16,24},{24,16},{1,9},{9,1},{17,25},{25,17},{2,10},{10... | collective-permute-start | bytes 5898248 | tf_op jit(solution)/shard_map/ppermute | solution.py:86
  284.6 85.3 %collective-permute-start.23 = (bf16[128,7680]{1,0:T(8,128)(2,1)}, bf16[128,7680]{1,0:T(8,128)(2,1)}, u32[]{:S(2)}, u32[]{:S(2)}) collective-permute-start(bf16[128,7680]{1,0:T(8,128)(2,1)} %get-tuple-element.245), channel_id=1, source_target_pairs={{0,16},{8,24},{16,0},{24,8},{1,17},{9,25},{17,1},{25,9},{2,18},{10... | collective-permute-start | bytes 5898248 | tf_op jit(solution)/shard_map/ppermute | solution.py:86
  291.8 23.3 %collective-permute-start.16 = (bf16[12,64,128]{2,1,0:T(8,128)(2,1)}, bf16[12,64,128]{2,1,0:T(8,128)(2,1)S(1)}, u32[]{:S(2)}, u32[]{:S(2)}) collective-permute-start(bf16[12,64,128]{2,1,0:T(8,128)(2,1)} %constant_dynamic-slice_fusion.3), channel_id=1, source_target_pairs={{0,1},{1,0},{2,3},{3,2},{4,5},{5,4},{6,7},{7,6},{8,9},{9,8},{10,11... | collective-permute-start | bytes 589832 | tf_op jit(solution)/shard_map/ppermute | solution.py:69
  293.3 17.5 %collective-permute-start.12 = (bf16[4,128,256]{2,1,0:T(8,128)(2,1)}, bf16[4,128,256]{2,1,0:T(8,128)(2,1)}, u32[]{:S(2)}, u32[]{:S(2)}) collective-permute-start(bf16[4,128,256]{2,1,0:T(8,128)(2,1)} %bitcast.54), channel_id=1, source_target_pairs={{0,1},{1,0},{2,3},{3,2},{4,5},{5,4},{6,7},{7,6},{8,9},{9,8},{10,11... | collective-permute-start | bytes 786440 | tf_op jit(solution)/shard_map/ppermute | solution.py:69
  312.0 5.9 collective-permute-start.13
  313.3 6.6 %collective-permute-start.14 = (bf16[128,256]{1,0:T(8,128)(2,1)S(1)}, bf16[128,256]{1,0:T(8,128)(2,1)S(1)}, u32[]{:S(2)}, u32[]{:S(2)}) collective-permute-start(bf16[128,256]{1,0:T(8,128)(2,1)S(1)} %get-tuple-element.285), channel_id=1, source_target_pairs={{4,0},{5,1},{6,2},{7,3},{12,8},{13,9},{14,10},{15,11},{20,16},{21,... | collective-permute-start | bytes 196616 | tf_op jit(solution)/shard_map/ppermute | solution.py:81
  315.1 6.7 %collective-permute-start.15 = (bf16[128,256]{1,0:T(8,128)(2,1)S(1)}, bf16[128,256]{1,0:T(8,128)(2,1)S(1)}, u32[]{:S(2)}, u32[]{:S(2)}) collective-permute-start(bf16[128,256]{1,0:T(8,128)(2,1)S(1)} %get-tuple-element.284), channel_id=1, source_target_pairs={{6,0},{7,1},{14,8},{15,9},{22,16},{23,17},{30,24},{31,25}} | collective-permute-start | bytes 196616 | tf_op jit(solution)/shard_map/ppermute | solution.py:81
  317.9 9.6 %collective-permute-start.17 = (bf16[12,64,128]{2,1,0:T(8,128)(2,1)}, bf16[12,64,128]{2,1,0:T(8,128)(2,1)}, u32[]{:S(2)}, u32[]{:S(2)}) collective-permute-start(bf16[12,64,128]{2,1,0:T(8,128)(2,1)} %fusion.69), channel_id=1, source_target_pairs={{2,0},{3,1},{4,2},{5,3},{6,4},{7,5},{10,8},{11,9},{12,10},{13,11},... | collective-permute-start | bytes 589832 | tf_op jit(solution)/shard_map/ppermute | solution.py:81
  319.9 8.8 %collective-permute-start.18 = (bf16[12,64,128]{2,1,0:T(8,128)(2,1)}, bf16[12,64,128]{2,1,0:T(8,128)(2,1)}, u32[]{:S(2)}, u32[]{:S(2)}) collective-permute-start(bf16[12,64,128]{2,1,0:T(8,128)(2,1)} %fusion.69), channel_id=1, source_target_pairs={{4,0},{5,1},{6,2},{7,3},{12,8},{13,9},{14,10},{15,11},{20,16},{21,... | collective-permute-start | bytes 589832 | tf_op jit(solution)/shard_map/ppermute | solution.py:81
  321.8 9.9 %collective-permute-start.19 = (bf16[12,64,128]{2,1,0:T(8,128)(2,1)}, bf16[12,64,128]{2,1,0:T(8,128)(2,1)}, u32[]{:S(2)}, u32[]{:S(2)}) collective-permute-start(bf16[12,64,128]{2,1,0:T(8,128)(2,1)} %fusion.69), channel_id=1, source_target_pairs={{6,0},{7,1},{14,8},{15,9},{22,16},{23,17},{30,24},{31,25}} | collective-permute-start | bytes 589832 | tf_op jit(solution)/shard_map/ppermute | solution.py:81
  327.5 44.1 %collective-permute-start.24 = (bf16[128,7680]{1,0:T(8,128)(2,1)}, bf16[128,7680]{1,0:T(8,128)(2,1)}, u32[]{:S(2)}, u32[]{:S(2)}) collective-permute-start(bf16[128,7680]{1,0:T(8,128)(2,1)} %get-tuple-element.244), channel_id=1, source_target_pairs={{0,24},{8,16},{16,8},{24,0},{1,25},{9,17},{17,9},{25,1},{2,26},{10... | collective-permute-start | bytes 5898248 | tf_op jit(solution)/shard_map/ppermute | solution.py:86
  334.0 5.7 collective-permute-start.20
  363.1 3.6 collective-permute-start.21
  383.0 6.3 %collective-permute-start.25 = (bf16[128,8192]{1,0:T(8,128)(2,1)}, bf16[128,8192]{1,0:T(8,128)(2,1)S(1)}, u32[]{:S(2)}, u32[]{:S(2)}) collective-permute-start(bf16[128,8192]{1,0:T(8,128)(2,1)} %get-tuple-element.86), channel_id=1, source_target_pairs={{0,1},{1,0},{2,3},{3,2},{4,5},{5,4},{6,7},{7,6},{8,9},{9,8},{10,11... | collective-permute-start | bytes 6291464 | tf_op jit(solution)/shard_map/ppermute | solution.py:69
  394.3 15.7 %collective-permute-start.26 = (bf16[32,8192]{1,0:T(8,128)(2,1)S(1)}, bf16[32,8192]{1,0:T(8,128)(2,1)S(1)}, u32[]{:S(2)}, u32[]{:S(2)}) collective-permute-start(bf16[32,8192]{1,0:T(8,128)(2,1)S(1)} %get-tuple-element.254), channel_id=1, source_target_pairs={{0,2},{1,3},{2,4},{3,5},{4,6},{5,7},{6,0},{7,1},{8,10},{9,11},{10,... | collective-permute-start | bytes 1572872 | tf_op jit(solution)/shard_map/ppermute | solution.py:81
  398.8 44.4 %collective-permute-start.27 = (bf16[32,8192]{1,0:T(8,128)(2,1)S(1)}, bf16[32,8192]{1,0:T(8,128)(2,1)}, u32[]{:S(2)}, u32[]{:S(2)}) collective-permute-start(bf16[32,8192]{1,0:T(8,128)(2,1)S(1)} %get-tuple-element.256), channel_id=1, source_target_pairs={{0,4},{1,5},{2,6},{3,7},{4,0},{5,1},{6,2},{7,3},{8,12},{9,13},{10,... | collective-permute-start | bytes 1572872 | tf_op jit(solution)/shard_map/ppermute | solution.py:81
  398.8 44.4 %collective-permute-start.28 = (bf16[32,8192]{1,0:T(8,128)(2,1)S(1)}, bf16[32,8192]{1,0:T(8,128)(2,1)}, u32[]{:S(2)}, u32[]{:S(2)}) collective-permute-start(bf16[32,8192]{1,0:T(8,128)(2,1)S(1)} %get-tuple-element.255), channel_id=1, source_target_pairs={{0,6},{1,7},{2,0},{3,1},{4,2},{5,3},{6,4},{7,5},{8,14},{9,15},{10,... | collective-permute-start | bytes 1572872 | tf_op jit(solution)/shard_map/ppermute | solution.py:81
  399.3 45.6 %collective-permute-start.29 = (bf16[144,4224]{1,0:T(8,128)(2,1)S(1)}, bf16[144,4224]{1,0:T(8,128)(2,1)S(1)}, u32[]{:S(2)}, u32[]{:S(2)}) collective-permute-start(bf16[144,4224]{1,0:T(8,128)(2,1)S(1)} %maximum_maximum_fusion.back_ref.refs_4_), channel_id=1, source_target_pairs={{0,8},{8,0},{16,24},{24,16},{1,9},{9,1},{17,25},{25,17},{2,10},{10... | collective-permute-start | bytes 3649544 | tf_op jit(solution)/shard_map/ppermute | solution.py:86
  400.5 44.4 %collective-permute-start.30 = (bf16[144,4224]{1,0:T(8,128)(2,1)S(1)}, bf16[144,4224]{1,0:T(8,128)(2,1)S(1)}, u32[]{:S(2)}, u32[]{:S(2)}) collective-permute-start(bf16[144,4224]{1,0:T(8,128)(2,1)S(1)} %maximum_maximum_fusion.back_ref.refs_4_), channel_id=1, source_target_pairs={{0,16},{8,24},{16,0},{24,8},{1,17},{9,25},{17,1},{25,9},{2,18},{10... | collective-permute-start | bytes 3649544 | tf_op jit(solution)/shard_map/ppermute | solution.py:86
  410.0 43.7 %collective-permute-start.31 = (bf16[144,4224]{1,0:T(8,128)(2,1)S(1)}, bf16[144,4224]{1,0:T(8,128)(2,1)S(1)}, u32[]{:S(2)}, u32[]{:S(2)}) collective-permute-start(bf16[144,4224]{1,0:T(8,128)(2,1)S(1)} %maximum_maximum_fusion.back_ref.refs_4_), channel_id=1, source_target_pairs={{0,24},{8,16},{16,8},{24,0},{1,25},{9,17},{17,9},{25,1},{2,26},{10... | collective-permute-start | bytes 3649544 | tf_op jit(solution)/shard_map/ppermute | solution.py:86
  458.9 5.9 collective-permute-start.32
  461.2 14.6 %collective-permute-start.43 = (bf16[32,8192]{1,0:T(8,128)(2,1)S(1)}, bf16[32,8192]{1,0:T(8,128)(2,1)S(1)}, u32[]{:S(2)}, u32[]{:S(2)}) collective-permute-start(bf16[32,8192]{1,0:T(8,128)(2,1)S(1)} %fusion.26), channel_id=1, source_target_pairs={{0,2},{1,3},{2,4},{3,5},{4,6},{5,7},{6,0},{7,1},{8,10},{9,11},{10,... | collective-permute-start | bytes 1572872 | tf_op jit(solution)/shard_map/ppermute | solution.py:81
  464.1 57.9 %collective-permute-start.44 = (bf16[32,8192]{1,0:T(8,128)(2,1)S(1)}, bf16[32,8192]{1,0:T(8,128)(2,1)S(1)}, u32[]{:S(2)}, u32[]{:S(2)}) collective-permute-start(bf16[32,8192]{1,0:T(8,128)(2,1)S(1)} %fusion.26), channel_id=1, source_target_pairs={{0,4},{1,5},{2,6},{3,7},{4,0},{5,1},{6,2},{7,3},{8,12},{9,13},{10,... | collective-permute-start | bytes 1572872 | tf_op jit(solution)/shard_map/ppermute | solution.py:81
  464.7 57.4 %collective-permute-start.45 = (bf16[32,8192]{1,0:T(8,128)(2,1)S(1)}, bf16[32,8192]{1,0:T(8,128)(2,1)S(1)}, u32[]{:S(2)}, u32[]{:S(2)}) collective-permute-start(bf16[32,8192]{1,0:T(8,128)(2,1)S(1)} %fusion.26), channel_id=1, source_target_pairs={{0,6},{1,7},{2,0},{3,1},{4,2},{5,3},{6,4},{7,5},{8,14},{9,15},{10,... | collective-permute-start | bytes 1572872 | tf_op jit(solution)/shard_map/ppermute | solution.py:81
  467.8 66.5 %collective-permute-start.33 = (bf16[32,4224]{1,0:T(8,128)(2,1)}, bf16[32,4224]{1,0:T(8,128)(2,1)S(1)}, u32[]{:S(2)}, u32[]{:S(2)}) collective-permute-start(bf16[32,4224]{1,0:T(8,128)(2,1)} %get-tuple-element.262), channel_id=1, source_target_pairs={{0,2},{1,3},{2,4},{3,5},{4,6},{5,7},{6,0},{7,1},{8,10},{9,11},{10,... | collective-permute-start | bytes 811016 | tf_op jit(solution)/shard_map/ppermute | solution.py:81
  471.0 63.3 %collective-permute-start.34 = (bf16[32,4224]{1,0:T(8,128)(2,1)S(1)}, bf16[32,4224]{1,0:T(8,128)(2,1)}, u32[]{:S(2)}, u32[]{:S(2)}) collective-permute-start(bf16[32,4224]{1,0:T(8,128)(2,1)S(1)} %get-tuple-element.264), channel_id=1, source_target_pairs={{0,4},{1,5},{2,6},{3,7},{4,0},{5,1},{6,2},{7,3},{8,12},{9,13},{10,... | collective-permute-start | bytes 811016 | tf_op jit(solution)/shard_map/ppermute | solution.py:81
  475.8 58.5 %collective-permute-start.35 = (bf16[32,4224]{1,0:T(8,128)(2,1)S(1)}, bf16[32,4224]{1,0:T(8,128)(2,1)}, u32[]{:S(2)}, u32[]{:S(2)}) collective-permute-start(bf16[32,4224]{1,0:T(8,128)(2,1)S(1)} %get-tuple-element.263), channel_id=1, source_target_pairs={{0,6},{1,7},{2,0},{3,1},{4,2},{5,3},{6,4},{7,5},{8,14},{9,15},{10,... | collective-permute-start | bytes 811016 | tf_op jit(solution)/shard_map/ppermute | solution.py:81
  524.4 38.7 %collective-permute-start.46 = (bf16[4,32,8192]{2,1,0:T(8,128)(2,1)}, bf16[4,32,8192]{2,1,0:T(8,128)(2,1)}, u32[]{:S(2)}, u32[]{:S(2)}) collective-permute-start(bf16[4,32,8192]{2,1,0:T(8,128)(2,1)} %get-tuple-element.266), channel_id=1, source_target_pairs={{0,1},{1,0},{2,3},{3,2},{4,5},{5,4},{6,7},{7,6},{8,9},{9,8},{10,11... | collective-permute-start | bytes 6291464 | tf_op jit(solution)/shard_map/ppermute | solution.py:69
  525.8 3.4 collective-permute-start.40
  529.3 5.0 collective-permute-start.41
  534.2 14.3 %collective-permute-start.42 = (f32[2312]{0:T(1024)S(1)}, f32[2312]{0:T(1024)S(1)}, u32[]{:S(2)}, u32[]{:S(2)}) collective-permute-start(f32[2312]{0:T(1024)S(1)} %add.479), channel_id=1, source_target_pairs={{0,4},{1,5},{2,6},{3,7},{4,0},{5,1},{6,2},{7,3},{8,12},{9,13},{10,... | collective-permute-start | bytes 27752 | tf_op jit(solution)/shard_map/ppermute | solution.py:858
  535.6 14.8 %collective-permute-start.36 = (bf16[32,4224]{1,0:T(8,128)(2,1)S(1)}, bf16[32,4224]{1,0:T(8,128)(2,1)S(1)}, u32[]{:S(2)}, u32[]{:S(2)}) collective-permute-start(bf16[32,4224]{1,0:T(8,128)(2,1)S(1)} %fusion.51), channel_id=1, source_target_pairs={{0,2},{1,3},{2,4},{3,5},{4,6},{5,7},{6,0},{7,1},{8,10},{9,11},{10,... | collective-permute-start | bytes 811016 | tf_op jit(solution)/shard_map/ppermute | solution.py:81
  535.7 25.9 %collective-permute-start.37 = (bf16[32,4224]{1,0:T(8,128)(2,1)S(1)}, bf16[32,4224]{1,0:T(8,128)(2,1)S(1)}, u32[]{:S(2)}, u32[]{:S(2)}) collective-permute-start(bf16[32,4224]{1,0:T(8,128)(2,1)S(1)} %fusion.51), channel_id=1, source_target_pairs={{0,4},{1,5},{2,6},{3,7},{4,0},{5,1},{6,2},{7,3},{8,12},{9,13},{10,... | collective-permute-start | bytes 811016 | tf_op jit(solution)/shard_map/ppermute | solution.py:81
  538.1 23.4 %collective-permute-start.38 = (bf16[32,4224]{1,0:T(8,128)(2,1)S(1)}, bf16[32,4224]{1,0:T(8,128)(2,1)S(1)}, u32[]{:S(2)}, u32[]{:S(2)}) collective-permute-start(bf16[32,4224]{1,0:T(8,128)(2,1)S(1)} %fusion.51), channel_id=1, source_target_pairs={{0,6},{1,7},{2,0},{3,1},{4,2},{5,3},{6,4},{7,5},{8,14},{9,15},{10,... | collective-permute-start | bytes 811016 | tf_op jit(solution)/shard_map/ppermute | solution.py:81
  561.8 16.4 %collective-permute-start.39 = (bf16[4,32,4224]{2,1,0:T(8,128)(2,1)S(1)}, bf16[4,32,4224]{2,1,0:T(8,128)(2,1)S(1)}, u32[]{:S(2)}, u32[]{:S(2)}) collective-permute-start(bf16[4,32,4224]{2,1,0:T(8,128)(2,1)S(1)} %get-tuple-element.268), channel_id=1, source_target_pairs={{0,1},{1,0},{2,3},{3,2},{4,5},{5,4},{6,7},{7,6},{8,9},{9,8},{10,11... | collective-permute-start | bytes 3244040 | tf_op jit(solution)/shard_map/ppermute | solution.py:69
  (113 other events, 1360.4 us)
Sparse Core Ops, SparseCore 0:
  16.1 54.7 all-gather.3
  73.3 87.6 all-gather.5

commit v3 on v2

v3 whole, which is shorter than its diff:
```python
import functools

import jax
import jax.numpy as jnp
from jax import lax
from jax.experimental import pallas as pl
from jax.experimental.pallas import tpu as pltpu
from jax.sharding import PartitionSpec as P

QUERY_HEADS = 8
VALUE_HEADS = 2
HEAD_SIZE = 64
MH = 24
MP = 64
NS = 128
KC = 4
GROUP = QUERY_HEADS // VALUE_HEADS
INNER = MH * MP
CONVW = INNER + 2 * NS
QW = QUERY_HEADS * HEAD_SIZE
KW = VALUE_HEADS * HEAD_SIZE

norm_epsilon = 1e-06
rope_base = 100000000000.0
f32 = jnp.float32
bf16 = jnp.bfloat16


def dot(a, b):
    return jnp.dot(a, b, preferred_element_type=f32)


def dot_nt(a, b):
    return lax.dot_general(a, b, (((1,), (1,)), ((), ())), preferred_element_type=f32)


def dot_tn(a, b):
    return lax.dot_general(a, b, (((0,), (0,)), ((), ())), preferred_element_type=f32)


def swap_core(value):
    count = lax.axis_size("ctx")
    return lax.ppermute(value, "ctx", [(i, i ^ 1) for i in range(count)])


def chip_shift(value, steps, wrap):
    count = lax.axis_size("ctx")
    pairs = []
    for i in range(count):
        to = i + 2 * steps
        if wrap:
            pairs.append((i, to % count))
        elif 0 <= to < count:
            pairs.append((i, to))
    return lax.ppermute(value, "ctx", pairs)


def seq_swap(value, k):
    count = lax.axis_size("seq")
    return lax.ppermute(value, "seq", [(i, i ^ k) for i in range(count)])


def take_half(value, core):
    rows = value.shape[0] // 2
    return lax.dynamic_slice_in_dim(value, core * rows, rows, 0)


def first_phase(value):
    seqs = lax.axis_size("seq")
    return [seq_swap(value, k) for k in (range(1, seqs) if seqs != 4 else (1, 2))]


def second_phase(near, cut):
    if len(near) != 2:
        return [(k + 1, 0, piece) for k, piece in enumerate(near)]
    far_a = seq_swap(near[0][:cut], 2)
    far_b = seq_swap(near[1][cut:], 1)
    return [(1, 0, near[0]), (2, 0, near[1]), (3, 0, far_a), (3, cut, far_b)]


def gather_pieces(value, cut):
    return second_phase(first_phase(value), cut)


def both_cores(pieces):
    out = []
    for k, row, array in pieces:
        out.append((k, 0, row, array))
        out.append((k, 1, row, swap_core(array)))
    return out


def chip_swap(value, bit):
    count = lax.axis_size("ctx")
    return lax.ppermute(value, "ctx", [(i, i ^ (2 * bit)) for i in range(count)])


def sum_halves(mine, arrived, chips, chip, small):
    rows = mine.shape[0]

    def widened(message, rows):
        return message[rows : rows + 8].astype(f32) + message[rows + 8 : rows + 16].astype(f32)

    def narrowed(values):
        hi, low = two(values)
        return jnp.concatenate([hi, low], axis=0)

    if small is not None:
        tail = narrowed(small)
        small = widened(tail, 0) + widened(arrived, rows)
        arrived = arrived[:rows]
    total = mine + arrived.astype(f32)
    bit = 1
    while bit < chips:
        rows //= 2
        side = jnp.where((chip & bit) != 0, 1, 0)
        give = lax.dynamic_slice_in_dim(total, (1 - side) * rows, rows, 0).astype(bf16)
        if small is not None:
            tail = narrowed(small)
            give = jnp.concatenate([give, tail], axis=0)
        arrived = chip_swap(give, bit)
        if small is not None:
            small = widened(tail, 0) + widened(arrived, rows)
            arrived = arrived[:rows]
        total = lax.dynamic_slice_in_dim(total, side * rows, rows, 0) + arrived.astype(f32)
        bit *= 2
    return total.astype(bf16), small


def spread_halves(total, chips, chip):
    bit = chips // 2
    while bit >= 1:
        other = chip_swap(total, bit)
        upper = (chip & bit) != 0
        total = jnp.concatenate(
            [jnp.where(upper, other, total), jnp.where(upper, total, other)], axis=0
        )
        bit //= 2
    return total


def ctx_state(low, decays, chips, core, later):
    half = INNER // 2
    mine = lax.dynamic_slice_in_dim(low, core * half, half, 0).astype(f32)
    others = lax.dynamic_slice_in_dim(low, (1 - core) * half, half, 0)
    got = swap_core(others).astype(f32)
    even = jnp.where(core == 0, mine, got)
    odd = jnp.where(core == 0, got, mine)
    dec = lax.dynamic_slice_in_dim(decays, core * (MH // 2), MH // 2, 2)
    dec = jnp.repeat(dec, MP, axis=2)[..., None]
    if later:
        chip_value = even + dec[0, 0] * odd
    else:
        chip_value = odd + dec[0, 1] * even
    chip_low = chip_value.astype(bf16)
    sign = -1 if later else 1
    total = jnp.zeros_like(chip_value)
    for k in range(chips - 1, 0, -1):
        arrived = chip_shift(chip_low, sign * k, False).astype(f32)
        rel = (sign * k) % chips
        total = arrived + dec[rel, 0] * dec[rel, 1] * total
    if later:
        for_odd = total
        for_even = odd + dec[0, 1] * total
    else:
        for_even = total
        for_odd = even + dec[0, 0] * total
    keep = jnp.where(core == 0, for_even, for_odd).astype(bf16)
    give = jnp.where(core == 0, for_odd, for_even).astype(bf16)
    back = swap_core(give)
    first = jnp.where(core == 0, keep, back)
    second = jnp.where(core == 0, back, keep)
    return jnp.concatenate([first, second], axis=0)


def silu_parts(z):
    sig = 1.0 / (1.0 + jnp.exp(-z))
    return z * sig, sig * (1.0 + z * (1.0 - sig))


def three(a):
    hi = a.astype(bf16)
    rest = a - hi.astype(f32)
    mid = rest.astype(bf16)
    return hi, mid, (rest - mid.astype(f32)).astype(bf16)


def exact_dot(a, b):
    hi, mid, low = three(a)
    return dot(hi, b) + dot(mid, b) + dot(low, b)


def two(a):
    hi = a.astype(bf16)
    return hi, (a - hi.astype(f32)).astype(bf16)


def exact_dot_nt(a, b):
    hi, mid, low = three(a)
    return dot_nt(hi, b) + dot_nt(mid, b) + dot_nt(low, b)


def head_table():
    head = lax.broadcasted_iota(jnp.int32, (128, INNER), 0)
    column = lax.broadcasted_iota(jnp.int32, (128, INNER), 1)
    return (column // MP == head).astype(bf16)


def placed(place, core, pieces, hr):
    return [
        ((place ^ k) * 2 * hr + jnp.where(core == side, 0, hr) + row) for k, side, row in pieces
    ]


def run_copies(copies):
    for copy in copies:
        copy.start()


def wait_copies(copies):
    for copy in copies:
        copy.wait()


def in_copies(pieces, where_ref, local_ref, refs, weight, sems):
    place, core = where_ref[0], where_ref[1]
    hr = local_ref.shape[0] // 2
    copies = [
        pltpu.make_async_copy(
            local_ref,
            weight.at[pl.ds(pl.multiple_of(place * 2 * hr, 16), 2 * hr), :],
            sems.at[0],
        )
    ]
    for i, (at, ref) in enumerate(zip(placed(place, core, pieces, hr), refs)):
        copies.append(
            pltpu.make_async_copy(
                ref,
                weight.at[pl.ds(pl.multiple_of(at, 16), ref.shape[0]), :],
                sems.at[i + 1],
            )
        )
    return copies


def project_kernel(pieces, where_ref, tok_ref, gin_ref, cos_ref, sin_ref, off_ref, rate_ref,
                   local_ref, *refs):
    count = len(pieces)
    parts, outs = refs[:count], refs[count:]
    nor_ref, q_ref, kv_ref, gz_ref, conv_ref, raw_ref, pre, weight, sems = outs
    copies = in_copies(pieces, where_ref, local_ref, parts, weight, sems)
    run_copies(copies)
    x = tok_ref[...].astype(f32)
    rows = x.shape[0]
    inv = lax.rsqrt(jnp.mean(x * x, axis=1, keepdims=True) + norm_epsilon)
    nor_ref[...] = (x * inv * gin_ref[...]).astype(bf16)
    wide = weight.shape[1]
    part = 384
    wait_copies(copies)

    def one(i, carry):
        a = pl.ds(pl.multiple_of(i * part, 128), part)
        pre[:, a] = dot(nor_ref[...], weight[:, a])
        return carry

    lax.fori_loop(0, wide // part, one, 0)
    for at in range(0, QW, 128):
        u = pre[:, at : at + 128]
        q_ref[:, at : at + 128] = (u * cos_ref[...] + half_turned(u) * sin_ref[...]).astype(bf16)
    u = pre[:, QW : QW + KW]
    kv_ref[:rows, :KW] = (u * cos_ref[...] + half_turned(u) * sin_ref[...]).astype(bf16)
    kv_ref[:rows, KW:] = pre[:, QW + KW : QW + 2 * KW].astype(bf16)
    at = QW + 2 * KW
    gz_ref[...] = pre[:, at : at + INNER]
    at += INNER
    conv_ref[...] = pre[:, at : at + CONVW].astype(bf16)
    at += CONVW
    raw = pre[:, at:]
    raw_ref[...] = raw
    unused, unused, cum, unused = heads_of(raw, off_ref[...], rate_ref[...])
    decay = jnp.exp(cum[rows - 1 : rows, :])
    hi, low = two(decay)
    row = lax.broadcasted_iota(jnp.int32, (16, 128), 0)
    both = jnp.where(row == 0, hi.astype(f32), jnp.where(row == 1, low.astype(f32), 0.0))
    kv_ref[rows:, :KW] = both.astype(bf16)
    kv_ref[rows:, KW:] = jnp.zeros((16, KW), bf16)


def project(where, tokens, gin, cosine, sine, offset, rates, local, pieces):
    rows, width = tokens.shape
    wide = local.shape[1]
    vm = pl.BlockSpec(memory_space=pltpu.VMEM)
    hbm = pl.BlockSpec(memory_space=pl.ANY)
    return pl.pallas_call(
        functools.partial(project_kernel, [p[:3] for p in pieces]),
        out_shape=(
            jax.ShapeDtypeStruct((rows, width), bf16),
            jax.ShapeDtypeStruct((rows, QW), bf16),
            jax.ShapeDtypeStruct((rows + 16, 2 * KW), bf16),
            jax.ShapeDtypeStruct((rows, INNER), f32),
            jax.ShapeDtypeStruct((rows, CONVW), bf16),
            jax.ShapeDtypeStruct((rows, 128), f32),
        ),
        in_specs=[pl.BlockSpec(memory_space=pltpu.SMEM)] + [vm] * 6 + [hbm] * (1 + len(pieces)),
        out_specs=[vm] * 6,
        scratch_shapes=[
            pltpu.VMEM((rows, wide), f32),
            pltpu.VMEM((width, wide), bf16),
            pltpu.SemaphoreType.DMA((1 + len(pieces),)),
        ],
        compiler_params=pltpu.CompilerParams(vmem_limit_bytes=40 * 2**20),
        cost_estimate=pl.CostEstimate(
            flops=2 * rows * width * wide, bytes_accessed=2 * width * wide + 3 * 2**20,
            transcendentals=0,
        ),
        name="project",
    )(where, tokens, gin, cosine, sine, offset, rates, local, *[p[3] for p in pieces])


def unproject_kernel(pieces, where_ref, tok_ref, gin_ref, gres_ref, back_ref, local_ref, *refs):
    parts, (out_ref, weight, sems) = refs[:-3], refs[-3:]
    copies = in_copies(pieces, where_ref, local_ref, parts, weight, sems)
    run_copies(copies)
    x = tok_ref[...].astype(f32)
    rows, width = x.shape
    inv = lax.rsqrt(jnp.mean(x * x, axis=1, keepdims=True) + norm_epsilon)
    unit = x * inv
    wide = weight.shape[1]
    part = 384
    out_ref[...] = jnp.zeros_like(out_ref)
    wait_copies(copies)

    def one(i, carry):
        a = pl.ds(pl.multiple_of(i * part, 128), part)
        out_ref[...] += dot_nt(back_ref[:rows, a], weight[:, a])
        return carry

    lax.fori_loop(0, wide // part, one, 0)
    d_norm = out_ref[...] * gin_ref[...]
    d_x = inv * (d_norm - unit * jnp.mean(d_norm * unit, axis=1, keepdims=True))
    out_ref[...] = gres_ref[...] + d_x


def unproject(where, tokens, gin, grad_res, back, local, pieces):
    rows, width = tokens.shape
    wide = local.shape[1]
    vm = pl.BlockSpec(memory_space=pltpu.VMEM)
    hbm = pl.BlockSpec(memory_space=pl.ANY)
    return pl.pallas_call(
        functools.partial(unproject_kernel, [p[:3] for p in pieces]),
        out_shape=jax.ShapeDtypeStruct((rows, width), f32),
        in_specs=[pl.BlockSpec(memory_space=pltpu.SMEM)] + [vm] * 4 + [hbm] * (1 + len(pieces)),
        out_specs=vm,
        scratch_shapes=[
            pltpu.VMEM((width, wide), bf16),
            pltpu.SemaphoreType.DMA((1 + len(pieces),)),
        ],
        compiler_params=pltpu.CompilerParams(vmem_limit_bytes=40 * 2**20),
        cost_estimate=pl.CostEstimate(
            flops=2 * rows * width * wide, bytes_accessed=2 * width * wide + 3 * 2**20,
            transcendentals=0,
        ),
        name="unproject",
    )(where, tokens, gin, grad_res, back, local, *[p[3] for p in pieces])


def last_grads_kernel(seqs, cut, where_ref, *refs):
    lefts, rights = refs[:seqs], refs[seqs:-3]
    keep_ref, give_ref, small_ref = refs[-3:]
    is0 = where_ref[1] == 0
    hr, wide = keep_ref.shape
    rows = lefts[0].shape[0]
    a = jnp.concatenate([m[:, :hr] for m in lefts], axis=0)
    b = jnp.concatenate([m[:, hr : 2 * hr] for m in lefts], axis=0)
    mine, other = jnp.where(is0, a, b), jnp.where(is0, b, a)
    part = 384
    if cut:
        spans = [rows] * (seqs - 1) + [cut, rows - cut]
        ends = list(range(seqs - 1)) + [seqs]
        starts = [rows] * (seqs - 1) + [rows - cut]
    else:
        spans, ends, starts = [rows] * seqs, list(range(seqs)), [rows] * seqs
    extras = [
        rights[i][at : at + 8, :].astype(f32) + rights[i][at + 8 : at + 16, :].astype(f32)
        for i, at in zip(ends, starts)
    ]
    while len(extras) > 1:
        extras = [extras[i] + extras[i + 1] for i in range(0, len(extras), 2)]
    small_ref[...] = extras[0]
    hi, low = two(extras[0])
    give_ref[hr:, :] = jnp.concatenate([hi.astype(f32), low.astype(f32)], axis=0).astype(bf16)

    def one(i, carry):
        src = pl.ds(pl.multiple_of(i * part, 128), part)
        right = jnp.concatenate([m[:n, src] for m, n in zip(rights, spans)], axis=0)
        keep_ref[:, src] = dot_tn(mine, right)
        give_ref[:hr, src] = dot_tn(other, right).astype(bf16)
        return carry

    lax.fori_loop(0, wide // part, one, 0)


def last_grads(where, lefts, rights, hr, cut):
    wide = rights[0].shape[1]
    seqs = len(lefts)
    vm = pl.BlockSpec(memory_space=pltpu.VMEM)
    return pl.pallas_call(
        functools.partial(last_grads_kernel, seqs, cut if len(rights) > seqs else 0),
        out_shape=(
            jax.ShapeDtypeStruct((hr, wide), f32),
            jax.ShapeDtypeStruct((hr + 16, wide), bf16),
            jax.ShapeDtypeStruct((8, wide), f32),
        ),
        in_specs=[pl.BlockSpec(memory_space=pltpu.SMEM)] + [vm] * (len(lefts) + len(rights)),
        out_specs=[vm, vm, vm],
        compiler_params=pltpu.CompilerParams(vmem_limit_bytes=40 * 2**20),
        cost_estimate=pl.CostEstimate(
            flops=4 * seqs * rights[0].size * hr, bytes_accessed=2 * seqs * rights[0].size,
            transcendentals=0,
        ),
        name="last_grads",
    )(where, *lefts, *rights)


def middle_kernel(
    seqs, pieces, where_ref, tok_ref, cot_ref, nor_ref, zero_ref, gz_ref, c_ref,
    ecum_ref, start_ref, att_ref, gmix_ref, gfeed_ref,
    gate_ref, up_ref, mix_ref, attw_ref, down_ref, *refs,
):
    count = len(pieces)
    parts = refs[:count]
    (
        lay_ref, msg1_ref, msg2_ref, dgu_ref, gres_ref, datt_ref, dssm_ref, dgz_ref, dstart_ref,
        dc_ref, dcum_ref,
        ssm, outs, feeds, hids, gates, ups, dhid, dout, w_gu, w_out, w_dn, sems,
    ) = refs[count:]
    place, core = where_ref[0], where_ref[1]
    rows, width = tok_ref.shape
    ff = hids.shape[1]
    hr = width // (2 * seqs)
    mixw, attw = INNER // seqs, QW // seqs
    outw = mixw + attw
    base_out, base_dn = 2 * ff, 2 * ff + 2 * width

    def at_rows(ref, row, size):
        return ref.at[pl.ds(pl.multiple_of(row, 16), size), :]

    starts = placed(place, core, pieces, hr)
    copies = {"out": [], "gu": [], "dn": []}

    def add(group, source, target):
        number = sum(len(c) for c in copies.values())
        copies[group].append(pltpu.make_async_copy(source, target, sems.at[number]))

    add("out", mix_ref, at_rows(w_out, place * 4 * hr, mixw))
    add("out", attw_ref, at_rows(w_out, place * 4 * hr + mixw, attw))

    def blocks(group, base, target):
        for (k, side, row), ref in zip(pieces, parts):
            for b in range(2):
                at = (place ^ k) * 4 * hr + jnp.where(core == side, 0, 2 * hr) + b * hr + row
                add(
                    group, ref.at[:, base + b * width : base + (b + 1) * width],
                    at_rows(target, at, ref.shape[0]),
                )

    blocks("out", base_out, w_out)
    own_rows = pl.ds(pl.multiple_of(place * 2 * hr, 16), 2 * hr)
    add("gu", gate_ref, w_gu.at[own_rows, :ff])
    add("gu", up_ref, w_gu.at[own_rows, ff:])
    for at, ref in zip(starts, parts):
        add("gu", ref.at[:, : 2 * ff], at_rows(w_gu, at, ref.shape[0]))
    add("dn", down_ref, at_rows(w_dn, place * 4 * hr, 4 * hr))
    blocks("dn", base_dn, w_dn)
    for group in ("out", "gu", "dn"):
        run_copies(copies[group])

    table = head_table()
    c_hi, c_lo = two(c_ref[...])
    ecum = exact_dot(ecum_ref[...], table)
    across = (dot_nt(c_hi, start_ref[...]) + dot_nt(c_lo, start_ref[...])) * ecum
    whole = zero_ref[...] + across
    silu_z, slope_z = silu_parts(gz_ref[...])
    gated = whole * silu_z
    inv_mix = lax.rsqrt(jnp.mean(gated * gated, axis=1, keepdims=True) + norm_epsilon)
    gmix = gmix_ref[...]
    ssm[...] = gated * inv_mix
    mix_b = (ssm[...] * gmix).astype(bf16)
    for j in range(seqs):
        outs[:, j * outw : j * outw + mixw] = mix_b[:, j * mixw : (j + 1) * mixw]
        outs[:, j * outw + mixw : (j + 1) * outw] = att_ref[:, j * attw : (j + 1) * attw]
    part = 512
    wait_copies(copies["out"])

    def attach(i, carry):
        a = pl.ds(pl.multiple_of(i * part, part), part)
        gres_ref[:, a] = tok_ref[:, a].astype(f32) + dot(outs[...], w_out[:, a])
        return carry

    lax.fori_loop(0, width // part, attach, 0)
    residual = gres_ref[...]
    inv_res = lax.rsqrt(jnp.mean(residual * residual, axis=1, keepdims=True) + norm_epsilon)
    gfeed = gfeed_ref[...]
    feeds[...] = (residual * inv_res * gfeed).astype(bf16)
    wait_copies(copies["gu"])

    def forward(i, carry):
        a = pl.ds(pl.multiple_of(i * part, part), part)
        u = pl.ds(pl.multiple_of(ff + i * part, part), part)
        gate = dot(feeds[...], w_gu[:, a])
        up = dot(feeds[...], w_gu[:, u])
        gates[:, a] = gate
        ups[:, a] = up
        hids[:, a] = (gate / (1.0 + jnp.exp(-gate)) * up).astype(bf16)
        return carry

    lax.fori_loop(0, ff // part, forward, 0)
    cot = cot_ref[...]
    wait_copies(copies["dn"])

    def finish(i, carry):
        a = pl.ds(pl.multiple_of(i * part, part), part)
        lay_ref[:, a] = (gres_ref[:, a] + dot(hids[...], w_dn[:, a])).astype(bf16)
        return carry

    lax.fori_loop(0, width // part, finish, 0)

    def through(i, carry):
        a = pl.ds(pl.multiple_of(i * part, part), part)
        dhid[:, a] = dot_nt(cot, w_dn[a, :])
        return carry

    lax.fori_loop(0, ff // part, through, 0)
    dout[:, :width] = jnp.zeros((rows, width), f32)

    def backward(i, carry):
        a = pl.ds(pl.multiple_of(i * part, part), part)
        u = pl.ds(pl.multiple_of(ff + i * part, part), part)
        silu_g, slope_g = silu_parts(gates[:, a])
        grad = dhid[:, a]
        d_gate = (grad * ups[:, a] * slope_g).astype(bf16)
        d_up = (grad * silu_g).astype(bf16)
        dgu_ref[:, a] = d_gate
        dgu_ref[:, u] = d_up
        dout[:, :width] += dot_nt(d_gate, w_gu[:, a]) + dot_nt(d_up, w_gu[:, u])
        return carry

    lax.fori_loop(0, ff // part, backward, 0)
    unit_res = gres_ref[...] * inv_res
    d_feed = dout[:, :width] * gfeed
    d_res = inv_res * (d_feed - unit_res * jnp.mean(d_feed * unit_res, axis=1, keepdims=True))
    grad_res = cot.astype(f32) + d_res
    gres_ref[...] = grad_res
    res_b = grad_res.astype(bf16)

    def leave(i, carry):
        a = pl.ds(pl.multiple_of(i * part, part), part)
        dout[:, a] = dot_nt(res_b, w_out[a, :])
        return carry

    lax.fori_loop(0, (INNER + QW) // part, leave, 0)
    for j in range(seqs):
        datt_ref[:, j * attw : (j + 1) * attw] = dout[
            :, j * outw + mixw : (j + 1) * outw
        ].astype(bf16)
        dssm_ref[:, j * mixw : (j + 1) * mixw] = dout[:, j * outw : j * outw + mixw]
    for k in range(seqs):
        to = place ^ k
        for ref, sources in (
            (msg1_ref, ((outs, outw), (hids, ff // seqs))),
            (msg2_ref, ((nor_ref, 2 * hr), (feeds, 2 * hr))),
        ):
            at = 0
            for source, size in sources:
                ref[k, :, at : at + size] = source[:, pl.ds(pl.multiple_of(to * size, 128), size)]
                at += size
        msg1_ref[k, :, outw + ff // seqs :] = res_b
    unit_mix = ssm[...]
    d_norm = dssm_ref[...] * gmix
    d_gated = inv_mix * (d_norm - unit_mix * jnp.mean(d_norm * unit_mix, axis=1, keepdims=True))
    dgz_ref[...] = (d_gated * whole * slope_z).astype(bf16)
    d_ssm = d_gated * silu_z
    dssm_ref[...] = d_ssm
    dcum_ref[...] = exact_dot_nt(d_ssm * across, table)
    da_hi, da_lo = two(d_ssm * ecum)
    dc_ref[...] = dot(da_hi, start_ref[...]) + dot(da_lo, start_ref[...])
    dstart_ref[...] = (dot_tn(da_hi, c_hi) + dot_tn(da_hi, c_lo) + dot_tn(da_lo, c_hi)).astype(
        bf16
    )


def middle(where, tokens, cotangent, normed, out_zero, gate_z, c_state, ecum, start,
           attn_b, gmix, gfeed, locals_, pieces, seqs):
    rows, width = tokens.shape
    ff = locals_[0].shape[1]
    outw = INNER + QW
    out_shape = (
        jax.ShapeDtypeStruct((rows, width), bf16),
        jax.ShapeDtypeStruct((seqs, rows, (outw + ff) // seqs + width), bf16),
        jax.ShapeDtypeStruct((seqs, rows, 2 * width // seqs), bf16),
        jax.ShapeDtypeStruct((rows, 2 * ff), bf16),
        jax.ShapeDtypeStruct((rows, width), f32),
        jax.ShapeDtypeStruct((rows, QW), bf16),
        jax.ShapeDtypeStruct((rows, INNER), f32),
        jax.ShapeDtypeStruct((rows, INNER), bf16),
        jax.ShapeDtypeStruct((INNER, NS), bf16),
        jax.ShapeDtypeStruct((rows, NS), f32),
        jax.ShapeDtypeStruct((rows, 128), f32),
    )
    vm = pl.BlockSpec(memory_space=pltpu.VMEM)
    hbm = pl.BlockSpec(memory_space=pl.ANY)
    scratch = [
        pltpu.VMEM((rows, INNER), f32),
        pltpu.VMEM((rows, outw), bf16),
        pltpu.VMEM((rows, width), bf16),
        pltpu.VMEM((rows, ff), bf16),
        pltpu.VMEM((rows, ff), f32),
        pltpu.VMEM((rows, ff), f32),
        pltpu.VMEM((rows, ff), f32),
        pltpu.VMEM((rows, outw), f32),
        pltpu.VMEM((width, 2 * ff), bf16),
        pltpu.VMEM((outw, width), bf16),
        pltpu.VMEM((ff, width), bf16),
        pltpu.SemaphoreType.DMA((5 + 5 * len(pieces),)),
    ]
    weights = width * 2 * ff + (outw + ff) * width
    return pl.pallas_call(
        functools.partial(middle_kernel, seqs, [p[:3] for p in pieces]),
        out_shape=out_shape,
        in_specs=[pl.BlockSpec(memory_space=pltpu.SMEM)] + [vm] * 11
        + [hbm] * (5 + len(pieces)),
        out_specs=[vm] * len(out_shape),
        scratch_shapes=scratch,
        compiler_params=pltpu.CompilerParams(vmem_limit_bytes=52 * 2**20),
        cost_estimate=pl.CostEstimate(
            flops=4 * rows * weights, bytes_accessed=2 * weights + 8 * 2**20,
            transcendentals=rows * 8192,
        ),
        name="middle",
    )(where, tokens, cotangent, normed, out_zero, gate_z, c_state, ecum, start,
      attn_b, gmix, gfeed, *locals_, *[p[3] for p in pieces])


def segment(is0, a, b, rights, span, target, keep_ref, give_ref):
    mine, other = jnp.where(is0, a, b), jnp.where(is0, b, a)
    part = 512

    def one(i, carry):
        src = pl.ds(pl.multiple_of(span[0] + i * part, 128), part)
        dst = pl.ds(pl.multiple_of(target + i * part, 128), part)
        rows = jnp.concatenate([m[:, src] for m in rights], axis=0)
        keep_ref[:, dst] = dot_tn(mine, rows)
        give_ref[:, dst] = dot_tn(other, rows).astype(bf16)
        return carry

    lax.fori_loop(0, span[1] // part, one, 0)


def grads_kernel(seqs, where_ref, *refs):
    msgs, cots, keep_ref, give_ref = refs[:seqs], refs[seqs:-2], refs[-2], refs[-1]
    is0 = where_ref[1] == 0
    hr = keep_ref.shape[0]
    width = 2 * hr * seqs
    at_res = msgs[0].shape[1] - width

    def left(at):
        return jnp.concatenate([m[:, at : at + hr] for m in msgs], axis=0)

    for b in range(2):
        segment(
            is0, left(b * hr), left((b + 2) * hr), msgs, (at_res, width), b * width,
            keep_ref, give_ref,
        )
        at = 4 * hr + b * hr
        segment(
            is0, left(at), left(at + 2 * hr), cots, (0, width), (2 + b) * width,
            keep_ref, give_ref,
        )


def feed_grads_kernel(seqs, where_ref, *refs):
    msgs, rights, keep_ref, give_ref = refs[:seqs], refs[seqs:-2], refs[-2], refs[-1]
    is0 = where_ref[1] == 0
    hr, columns = keep_ref.shape

    def left(at):
        return jnp.concatenate([m[:, at : at + hr] for m in msgs], axis=0)

    segment(is0, left(2 * hr), left(3 * hr), rights, (0, columns), 0, keep_ref, give_ref)


def grads(kernel, name, where, lefts, rights, hr, columns):
    vm = pl.BlockSpec(memory_space=pltpu.VMEM)
    seqs = len(lefts)
    return pl.pallas_call(
        functools.partial(kernel, seqs),
        out_shape=(
            jax.ShapeDtypeStruct((hr, columns), f32),
            jax.ShapeDtypeStruct((hr, columns), bf16),
        ),
        in_specs=[pl.BlockSpec(memory_space=pltpu.SMEM)] + [vm] * (len(lefts) + len(rights)),
        out_specs=[vm, vm],
        compiler_params=pltpu.CompilerParams(vmem_limit_bytes=40 * 2**20),
        cost_estimate=pl.CostEstimate(
            flops=4 * lefts[0].shape[0] * seqs * hr * columns,
            bytes_accessed=2 * seqs * (lefts[0].size + rights[0].size) + 6 * hr * columns,
            transcendentals=0,
        ),
        name=name,
    )(where, *lefts, *rights)


def halves_in_order(is0, mine_ref, other_ref, cols):
    mine, other = mine_ref[:, cols].astype(f32), other_ref[:, cols].astype(f32)
    return jnp.where(is0, mine, other), jnp.where(is0, other, mine)


def last_in_kernel(where_ref, mine_ref, other_ref, weight_ref, gain_ref,
                   q_ref, k_ref, v_ref, mix_ref, gin_ref):
    is0 = where_ref[1] == 0
    hr = mine_ref.shape[0]
    total = [jnp.zeros((hr, 1), f32), jnp.zeros((hr, 1), f32)]
    at = 0
    for ref in (q_ref, k_ref, v_ref, mix_ref):
        size = ref.shape[1]
        for start in range(0, size, 512):
            step = min(512, size - start)
            cols = slice(at + start, at + start + step)
            for i, grad in enumerate(halves_in_order(is0, mine_ref, other_ref, cols)):
                here = slice(i * hr, (i + 1) * hr)
                ref[here, start : start + step] = grad
                total[i] = total[i] + jnp.sum(
                    grad * weight_ref[here, cols].astype(f32), axis=1, keepdims=True
                )
        at += size
    for i in range(2):
        here = slice(i * hr, (i + 1) * hr)
        gin_ref[here, :] = total[i] / gain_ref[here, :].astype(f32)


def last_in(where, mine, other, weight, gain, mixed):
    vm = pl.BlockSpec(memory_space=pltpu.VMEM)
    rows = 2 * mine.shape[0]
    sizes = (QW, KW, KW, mixed, 1)
    return pl.pallas_call(
        last_in_kernel,
        out_shape=tuple(jax.ShapeDtypeStruct((rows, size), f32) for size in sizes),
        in_specs=[pl.BlockSpec(memory_space=pltpu.SMEM)] + [vm] * 4,
        out_specs=[vm] * 5,
        compiler_params=pltpu.CompilerParams(vmem_limit_bytes=40 * 2**20),
        name="last_in",
    )(where, mine, other, weight, gain)


def last_feed_kernel(where_ref, mine_ref, other_ref, gate_ref, up_ref, gain_ref,
                     out_gate_ref, out_up_ref, gfeed_ref):
    is0 = where_ref[1] == 0
    hr = mine_ref.shape[0]
    ff = gate_ref.shape[1]
    total = [jnp.zeros((hr, 1), f32), jnp.zeros((hr, 1), f32)]
    for base, weight_ref, out_ref in ((0, gate_ref, out_gate_ref), (ff, up_ref, out_up_ref)):
        for start in range(0, ff, 512):
            cols = slice(base + start, base + start + 512)
            to = slice(start, start + 512)
            for i, grad in enumerate(halves_in_order(is0, mine_ref, other_ref, cols)):
                here = slice(i * hr, (i + 1) * hr)
                out_ref[here, to] = grad
                total[i] = total[i] + jnp.sum(
                    grad * weight_ref[here, to].astype(f32), axis=1, keepdims=True
                )
    for i in range(2):
        here = slice(i * hr, (i + 1) * hr)
        gfeed_ref[here, :] = total[i] / gain_ref[here, :].astype(f32)


def last_feed(where, mine, other, gate, up, gain):
    vm = pl.BlockSpec(memory_space=pltpu.VMEM)
    rows, ff = gate.shape
    return pl.pallas_call(
        last_feed_kernel,
        out_shape=tuple(jax.ShapeDtypeStruct((rows, size), f32) for size in (ff, ff, 1)),
        in_specs=[pl.BlockSpec(memory_space=pltpu.SMEM)] + [vm] * 5,
        out_specs=[vm] * 3,
        compiler_params=pltpu.CompilerParams(vmem_limit_bytes=40 * 2**20),
        name="last_feed",
    )(where, mine, other, gate, up, gain)


def last_out_kernel(where_ref, mine_ref, other_ref, weight_ref, gain_ref,
                    mix_ref, att_ref, down_ref, gmix_ref):
    is0 = where_ref[1] == 0
    hr = mine_ref.shape[0]
    width = mix_ref.shape[1]
    mixw = mix_ref.shape[0]
    for b in range(2):
        cols = slice(b * width, (b + 1) * width)
        for i, grad in enumerate(halves_in_order(is0, mine_ref, other_ref, cols)):
            at = i * 2 * hr + b * hr
            end = at + hr
            inside = min(end, mixw) - at
            if inside > 0:
                here = slice(at, at + inside)
                own = grad[:inside]
                mix_ref[here, :] = own
                total = jnp.sum(own * weight_ref[here, :].astype(f32), axis=1, keepdims=True)
                gmix_ref[here, :] = total / gain_ref[here, :].astype(f32)
            if inside < hr:
                begin = max(inside, 0)
                att_ref[at + begin - mixw : end - mixw, :] = grad[begin:]
        cols = slice((2 + b) * width, (3 + b) * width)
        for i, grad in enumerate(halves_in_order(is0, mine_ref, other_ref, cols)):
            at = i * 2 * hr + b * hr
            down_ref[at : at + hr, :] = grad


def last_out(where, mine, other, weight, gain, attw):
    vm = pl.BlockSpec(memory_space=pltpu.VMEM)
    mixw, width = weight.shape
    shapes = ((mixw, width), (attw, width), (mixw + attw, width), (mixw, 1))
    return pl.pallas_call(
        last_out_kernel,
        out_shape=tuple(jax.ShapeDtypeStruct(shape, f32) for shape in shapes),
        in_specs=[pl.BlockSpec(memory_space=pltpu.SMEM)] + [vm] * 4,
        out_specs=[vm] * 4,
        compiler_params=pltpu.CompilerParams(vmem_limit_bytes=40 * 2**20),
        name="last_out",
    )(where, mine, other, weight, gain)


def heads_of(raw, offset, rates):
    z = raw + offset
    step = jnp.maximum(z, 0.0) + jnp.log(1.0 + jnp.exp(-jnp.abs(z)))
    hi, mid, low = three(-step * rates)
    shape = (raw.shape[0], raw.shape[0])
    causal = lax.broadcasted_iota(jnp.int32, shape, 0) >= lax.broadcasted_iota(
        jnp.int32, shape, 1
    )
    tril = causal.astype(bf16)
    cum = dot(tril, hi) + dot(tril, mid) + dot(tril, low)
    return z, step, cum, causal


def dot3(kind, a, b):
    a_hi, a_lo = two(a)
    b_hi, b_lo = two(b)
    return kind(a_hi, b_hi) + kind(a_hi, b_lo) + kind(a_lo, b_hi)


def lane_halves(shape):
    return lax.broadcasted_iota(jnp.int32, shape, 1) < MP


def conv_sums(ext, taps_ref, bias_ref, act_ref, rows):
    part = 256
    for at in range(0, CONVW, part):
        cols = slice(at, at + part)
        total = bias_ref[:, cols]
        for tap in range(KC):
            start = 16 - (KC - 1) + tap
            total = total + taps_ref[tap : tap + 1, cols] * ext[start : start + rows, cols]
        act_ref[:, cols] = total


def ssm_kernel(
    conv_ref, edge_ref, raw_ref, taps_ref, bias_ref, off_ref, rate_ref, skip_ref,
    act_ref, zero_ref, state_ref, c_ref, ecum_ref, ext,
):
    rows = conv_ref.shape[0]
    ext[0:16, :] = edge_ref[...].astype(f32)
    ext[16:, :] = conv_ref[...].astype(f32)
    conv_sums(ext, taps_ref, bias_ref, act_ref, rows)
    unused, step, cum, causal = heads_of(raw_ref[...], off_ref[...], rate_ref[...])
    cum_t, step_t = jnp.transpose(cum), jnp.transpose(step)
    table = head_table()
    b_state = silu_parts(act_ref[:, INNER : INNER + NS])[0]
    c_state = silu_parts(act_ref[:, INNER + NS :])[0]
    c_ref[...] = c_state
    ecum_ref[...] = jnp.exp(cum)
    inter = dot3(dot_nt, c_state, b_state)
    last = cum[rows - 1 : rows, :]
    tail = exact_dot(jnp.exp(last - cum) * step, table)
    low_lane = lane_halves((rows, 2 * MP))
    b_hi, b_lo = two(b_state)
    for pair in range(MH // 2):
        cols = slice(pair * 2 * MP, (pair + 1) * 2 * MP)
        x = silu_parts(act_ref[:, cols])[0]
        mixes = []
        for h in (2 * pair, 2 * pair + 1):
            gaps = jnp.where(causal, cum[:, h : h + 1] - cum_t[h : h + 1, :], -1e30)
            mixes.append((jnp.exp(gaps) * inter * step_t[h : h + 1, :]).astype(bf16))
        low = x.astype(bf16)
        none = jnp.zeros_like(low)
        stacked = jnp.concatenate(
            [jnp.where(low_lane, low, none), jnp.where(low_lane, none, low)], axis=0
        )
        within = dot(jnp.concatenate(mixes, axis=1), stacked)
        zero_ref[:, cols] = within + skip_ref[:, cols] * x
        t_hi, t_lo = two(tail[:, cols] * x)
        state = dot_tn(t_hi, b_hi) + dot_tn(t_hi, b_lo) + dot_tn(t_lo, b_hi)
        state_ref[cols, :] = state.astype(bf16)


def ssm_forward(conv_low, edge, raw, taps, bias, offset, rates, skip_wide):
    rows = conv_low.shape[0]
    vm = pl.BlockSpec(memory_space=pltpu.VMEM)
    return pl.pallas_call(
        ssm_kernel,
        out_shape=(
            jax.ShapeDtypeStruct((rows, CONVW), f32),
            jax.ShapeDtypeStruct((rows, INNER), f32),
            jax.ShapeDtypeStruct((INNER, NS), bf16),
            jax.ShapeDtypeStruct((rows, NS), f32),
            jax.ShapeDtypeStruct((rows, 128), f32),
        ),
        in_specs=[vm] * 8,
        out_specs=[vm] * 5,
        scratch_shapes=[pltpu.VMEM((rows + 16, CONVW), f32)],
        compiler_params=pltpu.CompilerParams(vmem_limit_bytes=32 * 2**20),
        cost_estimate=pl.CostEstimate(
            flops=2 * MH * rows * rows * 512, bytes_accessed=6 * 2**20, transcendentals=10**6
        ),
        name="ssm_forward",
    )(conv_low, edge, raw, taps, bias, offset, rates, skip_wide)


def ssm_back_kernel(
    conv_ref, edge_ref, raw_ref, taps_ref, off_ref, rate_ref, skip_ref, act_ref,
    dssm_ref, dc_in_ref, dcum_ref, later_ref, start_ref,
    dconv_ref, dedge_ref, draw_ref, extra_ref, ext, dact, rowg, colq, rows_out,
):
    rows = conv_ref.shape[0]
    ext[0:16, :] = edge_ref[...].astype(f32)
    ext[16:, :] = conv_ref[...].astype(f32)
    z, step, cum, causal = heads_of(raw_ref[...], off_ref[...], rate_ref[...])
    cum_t, step_t = jnp.transpose(cum), jnp.transpose(step)
    table = head_table()
    b_state, b_slope = silu_parts(act_ref[:, INNER : INNER + NS])
    c_state, c_slope = silu_parts(act_ref[:, INNER + NS :])
    inter = dot3(dot_nt, c_state, b_state)
    last = cum[rows - 1 : rows, :]
    reach = jnp.exp(last - cum)
    tail = exact_dot(reach * step, table)
    low_lane = lane_halves((rows, 2 * MP))
    b_hi, b_lo = two(b_state)
    dact[0:8, :] = jnp.zeros((8, CONVW), f32)
    dact[rows + 8 :, :] = jnp.zeros((8, CONVW), f32)
    rowg[...] = jnp.zeros_like(rowg)
    colq[...] = jnp.zeros_like(colq)
    d_inter = jnp.zeros((rows, rows), f32)
    d_b = jnp.zeros((rows, NS), f32)
    d_tail = jnp.zeros((rows, 128), f32)
    d_decay = jnp.zeros((8, 128), f32)
    d_skip = jnp.zeros((8, 128), f32)
    ones = jnp.ones((8, NS), bf16)
    for pair in range(MH // 2):
        cols = slice(pair * 2 * MP, (pair + 1) * 2 * MP)
        x, slope = silu_parts(act_ref[:, cols])
        dy = dssm_ref[:, cols]
        x_low, dy_low = x.astype(bf16), dy.astype(bf16)
        none = jnp.zeros_like(dy_low)
        stacked = jnp.concatenate(
            [jnp.where(low_lane, dy_low, none), jnp.where(low_lane, none, dy_low)], axis=0
        )
        d_mix = dot_nt(stacked, x_low)
        mixes = []
        for i, h in enumerate((2 * pair, 2 * pair + 1)):
            gaps = jnp.where(causal, cum[:, h : h + 1] - cum_t[h : h + 1, :], -1e30)
            weight = jnp.exp(gaps)
            step_row = step_t[h : h + 1, :]
            dm_w = d_mix[i * rows : (i + 1) * rows, :] * weight
            q = dm_w * inter
            d_inter = d_inter + dm_w * step_row
            colq[h : h + 1, :] = jnp.sum(q, axis=0, keepdims=True)
            rowg[:, h : h + 1] = jnp.sum(q * step_row, axis=1, keepdims=True)
            mixes.append((weight * inter * step_row).astype(bf16))
        dx = dot_tn(jnp.concatenate(mixes, axis=0), stacked)
        later = later_ref[cols, :]
        from_state = dot_nt(b_hi, later) + dot_nt(b_lo, later)
        tail_part = tail[:, cols]
        dx = dx + skip_ref[:, cols] * dy + tail_part * from_state
        dact[8 : rows + 8, cols] = dx * slope
        part_table = table[:, cols]
        d_tail = d_tail + exact_dot_nt(x * from_state, part_table)
        t_hi, t_lo = two(tail_part * x)
        d_b = d_b + dot(t_hi, later) + dot(t_lo, later)
        held = later.astype(f32) * start_ref[cols, :].astype(f32)
        hi, mid, low = three(held)
        sums = dot_nt(ones, hi) + dot_nt(ones, mid) + dot_nt(ones, low)
        d_decay = d_decay + exact_dot_nt(sums, part_table)
        skips = jnp.broadcast_to(jnp.sum(dy * x, axis=0, keepdims=True), (8, 2 * MP))
        d_skip = d_skip + exact_dot_nt(skips, part_table)
    d_b = d_b + dot3(dot_tn, d_inter, c_state)
    d_c = dc_in_ref[...] + dot3(dot, d_inter, b_state)
    dact[8 : rows + 8, INNER : INNER + NS] = d_b * b_slope
    dact[8 : rows + 8, INNER + NS :] = d_c * c_slope
    col = jnp.transpose(colq[...])
    moved = d_tail * reach
    fade = moved * step
    d_cum = dcum_ref[...] + rowg[...] - col * step - fade
    at_last = jnp.sum(fade, axis=0, keepdims=True) + d_decay[0:1, :] * jnp.exp(last)
    is_last = lax.broadcasted_iota(jnp.int32, (rows, 128), 0) == rows - 1
    d_cum = d_cum + jnp.where(is_last, at_last, 0.0)
    shape = (rows, rows)
    triu = (
        lax.broadcasted_iota(jnp.int32, shape, 0) <= lax.broadcasted_iota(jnp.int32, shape, 1)
    ).astype(bf16)
    hi, mid, low = three(d_cum)
    d_log = dot(triu, hi) + dot(triu, mid) + dot(triu, low)
    d_step = col + moved - rate_ref[...] * d_log
    d_raw = d_step / (1.0 + jnp.exp(-z))
    draw_ref[...] = d_raw
    rows_out[...] = jnp.zeros_like(rows_out)
    rows_out[2:3, CONVW : CONVW + 128] = jnp.sum(d_raw, axis=0, keepdims=True)
    rows_out[2:3, CONVW + 128 : CONVW + 256] = jnp.sum(-step * d_log, axis=0, keepdims=True)
    rows_out[2:3, CONVW + 256 : CONVW + 384] = d_skip[0:1, :]
    part = 256
    for at in range(0, CONVW, part):
        cols = slice(at, at + part)
        own = dact[8 : rows + 8, cols]
        total = jnp.zeros((rows, part), f32)
        edge = jnp.zeros((8, part), f32)
        for tap in range(KC):
            weight = taps_ref[tap : tap + 1, cols]
            start = 8 + KC - 1 - tap
            total = total + weight * dact[start : start + rows, cols]
            edge = edge + weight * dact[8 - tap : 16 - tap, cols]
            seen = ext[16 - (KC - 1) + tap : 16 - (KC - 1) + tap + rows, cols]
            to = (tap % 2) * CONVW + at
            rows_out[tap // 2 : tap // 2 + 1, to : to + part] = jnp.sum(
                own * seen, axis=0, keepdims=True
            )
        rows_out[2:3, cols] = jnp.sum(own, axis=0, keepdims=True)
        dconv_ref[:, cols] = total
        dedge_ref[:, cols] = edge
    hi, low = two(rows_out[...])
    extra_ref[...] = jnp.concatenate([hi.astype(f32), low.astype(f32)], axis=0).astype(bf16)


def ssm_backward(conv_low, edge, raw, taps, offset, rates, skip_wide, act,
                 d_ssm, d_c, d_cum, later, start, wide):
    rows = conv_low.shape[0]
    vm = pl.BlockSpec(memory_space=pltpu.VMEM)
    return pl.pallas_call(
        ssm_back_kernel,
        out_shape=(
            jax.ShapeDtypeStruct((rows, CONVW), f32),
            jax.ShapeDtypeStruct((8, CONVW), f32),
            jax.ShapeDtypeStruct((rows, 128), f32),
            jax.ShapeDtypeStruct((16, wide), bf16),
        ),
        in_specs=[vm] * 13,
        out_specs=[vm] * 4,
        scratch_shapes=[
            pltpu.VMEM((rows + 16, CONVW), f32),
            pltpu.VMEM((rows + 16, CONVW), f32),
            pltpu.VMEM((rows, 128), f32),
            pltpu.VMEM((128, rows), f32),
            pltpu.VMEM((8, wide), f32),
        ],
        compiler_params=pltpu.CompilerParams(vmem_limit_bytes=32 * 2**20),
        cost_estimate=pl.CostEstimate(
            flops=2 * MH * rows * rows * 1024, bytes_accessed=8 * 2**20, transcendentals=10**6
        ),
        name="ssm_backward",
    )(conv_low, edge, raw, taps, offset, rates, skip_wide, act,
      d_ssm, d_c, d_cum, later, start)


def allowed_keys(place_ref, rows, chips):
    core, chip = place_ref[1], place_ref[2]
    total = 2 * chips * rows
    key = lax.broadcasted_iota(jnp.int32, (rows, total), 1)
    query = (chip * 2 + core) * rows + lax.broadcasted_iota(jnp.int32, (rows, total), 0)
    block = key // rows
    side = block // chips
    key_chip = chip - block % chips
    parity = jnp.where(side == 0, core, 1 - core)
    position = (key_chip * 2 + parity) * rows + key % rows
    return (key_chip >= 0) & (position <= query)


def key_block(own_ref, sib_ref, rows, at):
    chips = own_ref.shape[0]
    parts = [own_ref[k, :rows, at : at + HEAD_SIZE] for k in range(chips)]
    parts += [sib_ref[k, :rows, at : at + HEAD_SIZE] for k in range(chips)]
    return jnp.concatenate(parts, axis=0)


def attend_kernel(place_ref, q_ref, own_ref, sib_ref, out_ref, top_ref, sum_ref):
    rows = q_ref.shape[0]
    allowed = allowed_keys(place_ref, rows, own_ref.shape[0])
    scale = HEAD_SIZE ** (-0.5)
    top_ref[...] = jnp.zeros_like(top_ref)
    sum_ref[...] = jnp.zeros_like(sum_ref)
    for g in range(VALUE_HEADS):
        keys = key_block(own_ref, sib_ref, rows, g * HEAD_SIZE)
        values = key_block(own_ref, sib_ref, rows, KW + g * HEAD_SIZE)
        for i in range(GROUP):
            h = g * GROUP + i
            cols = slice(h * HEAD_SIZE, (h + 1) * HEAD_SIZE)
            scores = dot_nt(q_ref[:, cols], keys) * scale
            scores = jnp.where(allowed, scores, -1e30)
            top = jnp.max(scores, axis=1, keepdims=True)
            raised = jnp.exp(scores - top)
            total = jnp.sum(raised, axis=1, keepdims=True)
            prob = (raised * (1.0 / total)).astype(bf16)
            out_ref[:, cols] = dot(prob, values).astype(bf16)
            top_ref[:, h : h + 1] = top
            sum_ref[:, h : h + 1] = 1.0 / total


def attend(where, queries, kv_own, kv_sib):
    rows = queries.shape[0]
    vm = pl.BlockSpec(memory_space=pltpu.VMEM)
    keys = 2 * kv_own.shape[0] * rows
    return pl.pallas_call(
        attend_kernel,
        out_shape=(
            jax.ShapeDtypeStruct((rows, QW), bf16),
            jax.ShapeDtypeStruct((rows, 128), f32),
            jax.ShapeDtypeStruct((rows, 128), f32),
        ),
        in_specs=[pl.BlockSpec(memory_space=pltpu.SMEM)] + [vm] * 3,
        out_specs=[vm] * 3,
        compiler_params=pltpu.CompilerParams(vmem_limit_bytes=48 * 2**20),
        cost_estimate=pl.CostEstimate(
            flops=4 * rows * keys * QW, bytes_accessed=4 * kv_own.size,
            transcendentals=rows * keys * QUERY_HEADS,
        ),
        name="attend",
    )(where, queries, kv_own, kv_sib)


def half_turned(x):
    lane = lax.broadcasted_iota(jnp.int32, x.shape, 1)
    first = lane % HEAD_SIZE < HEAD_SIZE // 2
    return jnp.where(
        first, pltpu.roll(x, 128 - HEAD_SIZE // 2, 1), pltpu.roll(x, HEAD_SIZE // 2, 1)
    )


def attend_back_kernel(
    place_ref, q_ref, own_ref, sib_ref, top_ref, sum_ref, dout_ref, cos_ref, sin_ref,
    dq_ref, down_ref, dsib_ref, dq_s,
):
    rows = q_ref.shape[0]
    chips = own_ref.shape[0]
    allowed = allowed_keys(place_ref, rows, chips)
    scale = HEAD_SIZE ** (-0.5)
    for g in range(VALUE_HEADS):
        keys = key_block(own_ref, sib_ref, rows, g * HEAD_SIZE)
        values = key_block(own_ref, sib_ref, rows, KW + g * HEAD_SIZE)
        d_keys = jnp.zeros(keys.shape, f32)
        d_values = jnp.zeros(keys.shape, f32)
        for i in range(GROUP):
            h = g * GROUP + i
            cols = slice(h * HEAD_SIZE, (h + 1) * HEAD_SIZE)
            q = q_ref[:, cols]
            d_out = dout_ref[:, cols]
            scores = dot_nt(q, keys) * scale
            scores = jnp.where(allowed, scores, -1e30)
            prob = jnp.exp(scores - top_ref[:, h : h + 1]) * sum_ref[:, h : h + 1]
            d_prob = dot_nt(d_out, values)
            delta = jnp.sum(prob * d_prob, axis=1, keepdims=True)
            d_score = (prob * (d_prob - delta)).astype(bf16)
            dq_s[:, cols] = dot(d_score, keys) * scale
            d_keys = d_keys + dot_tn(d_score, q)
            d_values = d_values + dot_tn(prob.astype(bf16), d_out)
        d_keys = d_keys * scale
        for k in range(chips):
            at = k * rows
            cols = slice(g * HEAD_SIZE, (g + 1) * HEAD_SIZE)
            more = slice(KW + g * HEAD_SIZE, KW + (g + 1) * HEAD_SIZE)
            down_ref[k, :, cols] = d_keys[at : at + rows]
            down_ref[k, :, more] = d_values[at : at + rows]
            at += chips * rows
            dsib_ref[k, :, cols] = d_keys[at : at + rows].astype(bf16)
            dsib_ref[k, :, more] = d_values[at : at + rows].astype(bf16)
    for at in range(0, QW, 128):
        x = dq_s[:, at : at + 128]
        turned = x * cos_ref[...] - half_turned(x) * sin_ref[...]
        dq_ref[:, at : at + 128] = turned.astype(bf16)


def attend_back(where, queries, kv_own, kv_sib, top, total, d_att, cosine, sine):
    rows = queries.shape[0]
    chips = kv_own.shape[0]
    vm = pl.BlockSpec(memory_space=pltpu.VMEM)
    keys = 2 * chips * rows
    return pl.pallas_call(
        attend_back_kernel,
        out_shape=(
            jax.ShapeDtypeStruct((rows, QW), bf16),
            jax.ShapeDtypeStruct((chips, rows, 2 * KW), f32),
            jax.ShapeDtypeStruct((chips, rows, 2 * KW), bf16),
        ),
        in_specs=[pl.BlockSpec(memory_space=pltpu.SMEM)] + [vm] * 8,
        out_specs=[vm] * 3,
        scratch_shapes=[pltpu.VMEM((rows, QW), f32)],
        compiler_params=pltpu.CompilerParams(vmem_limit_bytes=48 * 2**20),
        cost_estimate=pl.CostEstimate(
            flops=10 * rows * keys * QW, bytes_accessed=8 * kv_own.size,
            transcendentals=rows * keys * QUERY_HEADS,
        ),
        name="attend_back",
    )(where, queries, kv_own, kv_sib, top, total, d_att, cosine, sine)


def pack_kernel(
    dq_ref, dkv_ref, cos_ref, sin_ref, dgz_ref, dconv_ref, edge_ref, draw_ref, extra_ref, *refs
):
    arrived, out_ref, conv = refs[:-2], refs[-2], refs[-1]
    rows = dq_ref.shape[0]
    d_kv = dkv_ref[...]
    for ref in arrived:
        d_kv = d_kv + ref[...].astype(f32)
    d_k = d_kv[:, :KW]
    d_k = d_k * cos_ref[...] - half_turned(d_k) * sin_ref[...]
    out_ref[:rows, :QW] = dq_ref[...]
    out_ref[:rows, QW : QW + KW] = d_k.astype(bf16)
    out_ref[:rows, QW + KW : QW + 2 * KW] = d_kv[:, KW:].astype(bf16)
    at = QW + 2 * KW
    out_ref[:rows, at : at + INNER] = dgz_ref[...]
    at += INNER
    conv[...] = dconv_ref[...]
    more = edge_ref[0 : KC - 1, :]
    conv[rows - (KC - 1) :, :] = conv[rows - (KC - 1) :, :] + more
    out_ref[:rows, at : at + CONVW] = conv[...].astype(bf16)
    at += CONVW
    out_ref[:rows, at:] = draw_ref[...].astype(bf16)
    out_ref[rows:, :] = extra_ref[...]


def pack(d_q, d_kv, cosine, sine, d_gate_z, d_conv, edge, d_raw, extra, arrived):
    rows = d_q.shape[0]
    vm = pl.BlockSpec(memory_space=pltpu.VMEM)
    return pl.pallas_call(
        pack_kernel,
        out_shape=jax.ShapeDtypeStruct((rows + 16, extra.shape[1]), bf16),
        in_specs=[vm] * (9 + len(arrived)),
        out_specs=vm,
        scratch_shapes=[pltpu.VMEM((rows, CONVW), f32)],
        compiler_params=pltpu.CompilerParams(vmem_limit_bytes=32 * 2**20),
        cost_estimate=pl.CostEstimate(flops=10**6, bytes_accessed=4 * 2**20, transcendentals=0),
        name="pack",
    )(d_q, d_kv, cosine, sine, d_gate_z, d_conv, edge, d_raw, extra, *arrived)


def body(
    tokens,
    cotangent,
    gain_input,
    w_query,
    key_weight,
    value_weight,
    w_mixin,
    conv_taps,
    conv_bias,
    step_offset,
    decay_rate,
    skip_gain,
    gain_mixer,
    w_mixout,
    w_attnout,
    gain_feed,
    w_gate,
    w_up,
    w_down,
):
    rows, width = tokens.shape
    seqs = lax.axis_size("seq")
    ctxs = lax.axis_size("ctx")
    chips = ctxs // 2
    place = lax.axis_index("seq")
    ctx = lax.axis_index("ctx")
    chip, core = ctx // 2, ctx % 2
    ff = w_gate.shape[1]

    sizes = (gain_input.size, gain_feed.size, conv_bias.size, gain_mixer.size, conv_taps.size)
    small = jnp.concatenate(
        [gain_input, gain_feed, conv_bias, gain_mixer, conv_taps.reshape(-1)]
    )
    small = [small] + [seq_swap(small, k) for k in range(1, seqs)]
    bit = 1
    while bit < seqs:
        flip = (place & bit) != 0
        small = [jnp.where(flip, small[j ^ bit], small[j]) for j in range(seqs)]
        bit *= 2
    small = jnp.stack(small).astype(f32)
    at = 0
    pieces = []
    for size in sizes:
        pieces.append(small[:, at : at + size])
        at += size
    gin = pieces[0].reshape(-1)
    gfeed = pieces[1].reshape(-1)
    cbias = pieces[2].reshape(-1)
    gmix = pieces[3].reshape(-1)
    taps = pieces[4].reshape(seqs, KC, -1).transpose(1, 0, 2).reshape(KC, -1)

    used = QW + 2 * KW + w_mixin.shape[1]
    wide = -(-used // 128) * 128
    blank = jnp.zeros((w_mixin.shape[0], wide - used), bf16)
    in_loc = jnp.concatenate([w_query, key_weight, value_weight, w_mixin, blank], axis=1)
    cut = width // (4 * seqs)
    cut = cut if cut % 16 == 0 else 0
    w_in = gather_pieces(take_half(in_loc, core), cut)
    out_loc = jnp.concatenate([w_mixout, w_attnout], axis=0)
    half_out = take_half(out_loc, core)
    half_dn = take_half(w_down, core)
    hr = half_out.shape[0] // 2
    rest = jnp.concatenate(
        [
            take_half(w_gate, core),
            take_half(w_up, core),
            half_out[:hr],
            half_out[hr:],
            half_dn[:hr],
            half_dn[hr:],
        ],
        axis=1,
    )
    where = jnp.stack([place, core, chip]).astype(jnp.int32)

    position = ctx * rows + jnp.arange(rows, dtype=jnp.int32)
    frequency = rope_base ** (
        -(jnp.arange(HEAD_SIZE // 2, dtype=f32) * 2.0 / HEAD_SIZE)
    )
    angles = position.astype(f32)[:, None] * jnp.tile(frequency, 4)[None, :]
    sign = jnp.tile(jnp.repeat(jnp.array([-1.0, 1.0], f32), HEAD_SIZE // 2), 2)
    cosine = jnp.cos(angles)
    sine = jnp.sin(angles) * sign[None, :]
    offset = jnp.pad(step_offset, (0, 128 - MH))[None, :]
    rates = jnp.pad(decay_rate, (0, 128 - MH))[None, :]
    skip_wide = jnp.repeat(skip_gain, MP)[None, :]

    rest, far_in = lax.optimization_barrier((rest, w_in[-1][2]))
    w_in[-1] = (*w_in[-1][:2], far_in)
    w_in = both_cores(w_in)
    near = first_phase(rest)
    normed, queries, message, gate_z, conv_low, raw_step = project(
        where, tokens, gin[None, :], cosine, sine, offset, rates, in_loc, w_in
    )
    mix0 = QW + 2 * KW

    edge = lax.ppermute(
        conv_low[rows - 16 :], "ctx", [(i, i + 1) for i in range(ctxs - 1)]
    )
    kv_own = jnp.stack([message] + [chip_shift(message, k, True) for k in range(1, chips)])
    kv_sib = swap_core(kv_own)
    dec_own = kv_own[:, rows, :MH].astype(f32) + kv_own[:, rows + 1, :MH].astype(f32)
    dec_sib = kv_sib[:, rows, :MH].astype(f32) + kv_sib[:, rows + 1, :MH].astype(f32)
    decays = jnp.stack(
        [jnp.where(core == 0, dec_own, dec_sib), jnp.where(core == 0, dec_sib, dec_own)], axis=1
    )

    act, out_zero, local_state, c_state, exp_cum = ssm_forward(
        conv_low, edge, raw_step, taps, cbias[None, :], offset, rates, skip_wide
    )
    start_state = ctx_state(local_state, decays, chips, core, False)
    cots = [cotangent] + [p[2] for p in gather_pieces(cotangent, rows // 2)]
    queries, near = lax.optimization_barrier((queries, near))
    rest_far = second_phase(near, cut)
    w_rest = both_cores(rest_far)
    attn_b, top, total = attend(where, queries, kv_own, kv_sib)

    layer_out, msg1, msg2, d_gu, grad_res, d_att, d_ssm, d_gate_z, d_start, d_c, d_cum = middle(
        where, tokens, cotangent, normed, out_zero, gate_z, c_state, exp_cum, start_state, attn_b,
        gmix[None, :], gfeed[None, :], (w_gate, w_up, w_mixout, w_attnout, w_down), w_rest, seqs,
    )
    msgs1 = [msg1[0]] + [seq_swap(msg1[k], k) for k in range(1, seqs)]
    msgs2 = [msg2[0]] + [seq_swap(msg2[k], k) for k in range(1, seqs)]

    later_grad = ctx_state(d_start, decays, chips, core, True)
    d_q, d_kv, d_kv_sib = attend_back(
        where, queries, kv_own, kv_sib, top, total, d_att, cosine, sine
    )
    d_kv = d_kv + swap_core(d_kv_sib).astype(f32)
    arrived = [chip_shift(d_kv[k].astype(bf16), -k, False) for k in range(1, chips)]
    d_conv, d_edge, d_raw, extra = ssm_backward(
        conv_low, edge, raw_step, taps, offset, rates, skip_wide, act,
        d_ssm, d_c, d_cum, later_grad, start_state, wide,
    )
    edge_back = lax.ppermute(d_edge, "ctx", [(i + 1, i) for i in range(ctxs - 1)])
    back_msg = pack(
        d_q, d_kv[0], cosine, sine, d_gate_z, d_conv, edge_back, d_raw, extra, arrived
    )
    keep1, give1 = grads(grads_kernel, "out_grads", where, msgs1, cots, hr, 4 * width)
    back_msg, keep1, give1 = lax.optimization_barrier((back_msg, keep1, give1))
    total1, unused = sum_halves(keep1, swap_core(give1), chips, chip, None)
    rights2 = [d_gu] + [p[2] for p in gather_pieces(d_gu, rows // 2)]
    keep2, give2 = grads(feed_grads_kernel, "feed_grads", where, msgs2, rights2, hr, 2 * ff)
    total2, unused = sum_halves(keep2, swap_core(give2), chips, chip, None)
    backs = [back_msg] + [p[2] for p in gather_pieces(back_msg, rows // 2)]
    backs[0], total2 = lax.optimization_barrier((backs[0], total2))
    keep3, give3, small = last_grads(where, msgs2, backs, hr, rows // 2)
    mine1 = spread_halves(total1, chips, chip)
    mine2 = spread_halves(total2, chips, chip)
    total3, small_sum = sum_halves(keep3, swap_core(give3), chips, chip, small)
    grad_tokens = unproject(where, tokens, gin[None, :], grad_res, back_msg, in_loc, w_in)
    mine3 = spread_halves(total3, chips, chip)

    sum_mix, sum_att, sum_dn, grad_gmix = last_out(
        where, mine1, swap_core(mine1), w_mixout, gain_mixer[:, None], QW // seqs
    )
    sum_gate, sum_up, grad_gfeed = last_feed(
        where, mine2, swap_core(mine2), w_gate, w_up, gain_feed[:, None]
    )
    sum_q, sum_k, sum_v, sum_mixin, grad_gin = last_in(
        where, mine3, swap_core(mine3), in_loc, gain_input[:, None], used - mix0
    )
    small_taps = small_sum[:2, : 2 * CONVW].reshape(KC, CONVW)

    def own_share(vec):
        size = vec.shape[-1] // seqs
        return lax.dynamic_slice_in_dim(vec, place * size, size, vec.ndim - 1)

    heads = small_sum[2, CONVW:]
    return (
        layer_out,
        grad_tokens,
        grad_gin[:, 0],
        sum_q,
        sum_k,
        sum_v,
        sum_mixin,
        own_share(small_taps),
        own_share(small_sum[2, :CONVW]),
        heads[:MH],
        heads[128 : 128 + MH],
        heads[256 : 256 + MH],
        grad_gmix[:, 0],
        sum_mix,
        sum_att,
        grad_gfeed[:, 0],
        sum_gate,
        sum_up,
        sum_dn,
    )


def solution(mesh):
    rows = P(("seq", "ctx"), None)
    vec = P("seq")
    mat = P("seq", None)
    col = P(None, "seq")
    rep = P()
    in_specs = (
        rows, rows, vec, mat, mat, mat, mat, col, vec, rep, rep, rep, vec, mat, mat, vec, mat, mat, mat,
    )
    out_specs = (
        rows, rows, vec, mat, mat, mat, mat, col, vec, rep, rep, rep, vec, mat, mat, vec, mat, mat, mat,
    )
    return jax.shard_map(body, mesh=mesh, in_specs=in_specs, out_specs=out_specs, check_vma=False)
```

time: 603 us -> 485 us (0.80)
  the two profiles are of different devices: /device:TPU:25 before, /device:TPU:1 now
where the time goes in v3:
time: 485 us; the launch traced here: 476 us
  waiting for transfers between devices  187 us (39%)
  starting transfers between devices  105 us (22%)
  Pallas kernels  81.5 us (17%)
  local copies, waits for them, and re-layouts  71.7 us (15%)
  other arithmetic  28.7 us (6%)
    ppermute x12, waiting for transfers between devices, chip_swap(): return lax.ppermute(value, 'ctx', [(i, i ^ 2 * bit) for i in range(count)])  81.1 us
    ppermute x29, waiting for transfers between devices, seq_swap(): return lax.ppermute(value, 'seq', [(i, i ^ k) for i in range(count)])  77.9 us
    unnamed x192, local copies, waits for them, and re-layouts  37.6 us
    ppermute x12, starting transfers between devices, chip_shift(): return lax.ppermute(value, 'ctx', pairs)  32.9 us
    ppermute x20, starting transfers between devices, swap_core(): return lax.ppermute(value, 'ctx', [(i, i ^ 1) for i in range(count)])  28.2 us
    ppermute x29, starting transfers between devices, seq_swap(): return lax.ppermute(value, 'seq', [(i, i ^ k) for i in range(count)])  26.9 us
    ppermute x12, waiting for transfers between devices, chip_shift(): return lax.ppermute(value, 'ctx', pairs)  23.4 us
    pallas_call x1, Pallas kernels, middle(): pl.pallas_call(functools.partial(middle_kernel, seqs, [p[:3] for p in pie...  20.3 us
  transfers between devices with their start and end apart: 75, of which 25 were waited for; matrix products, arithmetic and copies ran while one was open for 13% of the time, Pallas kernels for 16%

profile of v3, /device:TPU:1, one launch (start us, length us, event | category | flops | bytes accessed | tf_op | source)
XLA Modules:
  0.0 476.4 jit_solution(1474867222846622713)
XLA Ops:
  0.7 3.8 copy.42
  4.6 3.7 concatenate.43.local_ref.weight_ref
  9.4 2.1 collective-permute-start.5
  15.8 19.5 %collective-permute-done.5.refs_2_ = bf16[128,4224]{1,0:T(8,128)(2,1)} collective-permute-done((bf16[128,4224]{1,0:T(8,128)(2,1)}, bf16[128,4224]{1,0:T(8,128)(2,1)}, u32[]{:S(2)}, u32[]{:S(2)}) %collective-permute-start.5) | collective-permute-done | bytes 1081376 | tf_op jit(solution)/shard_map/ppermute | solution.py:60
  44.3 5.7 %collective-permute-done.9.refs_6_ = bf16[64,4224]{1,0:T(8,128)(2,1)} collective-permute-done((bf16[64,4224]{1,0:T(8,128)(2,1)}, bf16[64,4224]{1,0:T(8,128)(2,1)}, u32[]{:S(2)}, u32[]{:S(2)}) %collective-permute-start.9) | collective-permute-done | bytes 540704 | tf_op jit(solution)/shard_map/ppermute | solution.py:60
  50.1 2.2 collective-permute-start.10
  52.9 2.1 collective-permute-start
  64.5 4.2 collective-permute-start.8
  70.4 7.6 %project.1 = (bf16[128,1024]{1,0:T(8,128)(2,1)S(1)}, bf16[128,512]{1,0:T(8,128)(2,1)S(1)}, bf16[144,256]{1,0:T(8,128)(2,1)}, f32[128,1536]{1,0:T(8,128)S(1)}, bf...) custom-call(s32[3]{0:T(128)S(1)} %pad_add_fusion.where_ref.place_ref, bf16[128,1024]{1,0:T(8,128)(2,1)S(1)} %copy-done.9, ...), custom_call_target="tpu_custom_call" | custom-call | flops 1107296256 | bytes 11796480 | tf_op jit(solution)/shard_map/project/pallas_call | solution.py:294
  83.0 2.3 collective-permute-start.14
  87.6 3.5 collective-permute-done.14
  94.9 3.4 collective-permute-start.11
  108.3 2.3 slice.222
  111.8 2.3 slice.223
  116.7 5.9 %collective-permute-start.23 = (bf16[128,8192]{1,0:T(8,128)(2,1)}, bf16[128,8192]{1,0:T(8,128)(2,1)S(1)}, u32[]{:S(2)}, u32[]{:S(2)}) collective-permute-start(bf16[128,8192]{1,0:T(8,128)(2,1)} %collective-permute-done.21.refs_0_), channel_id=1, source_target_pairs={{0,1},{1,0},{2,3},{3,2},{4,5},{5,4},{6,7},{7,6},{8,9},{9,8},{10,11... | collective-permute-start | bytes 6291464 | tf_op jit(solution)/shard_map/ppermute | solution.py:43
  124.6 3.2 collective-permute-start.17
  127.8 3.8 collective-permute-done.17
  131.6 5.2 %collective-permute-start.18 = (bf16[768,128]{1,0:T(8,128)(2,1)S(1)}, bf16[768,128]{1,0:T(8,128)(2,1)S(1)}, u32[]{:S(2)}, u32[]{:S(2)}) collective-permute-start(bf16[768,128]{1,0:T(8,128)(2,1)S(1)} %fusion.2), channel_id=1, source_target_pairs={{0,4},{1,5},{2,6},{3,7},{8,12},{9,13},{10,14},{11,15},{16,20},{17,... | collective-permute-start | bytes 589832 | tf_op jit(solution)/shard_map/ppermute | solution.py:55
  139.9 11.8 %collective-permute-start.19 = (bf16[768,128]{1,0:T(8,128)(2,1)S(1)}, bf16[768,128]{1,0:T(8,128)(2,1)S(1)}, u32[]{:S(2)}, u32[]{:S(2)}) collective-permute-start(bf16[768,128]{1,0:T(8,128)(2,1)S(1)} %fusion.2), channel_id=1, source_target_pairs={{0,6},{1,7},{8,14},{9,15},{16,22},{17,23},{24,30},{25,31}} | collective-permute-start | bytes 589832 | tf_op jit(solution)/shard_map/ppermute | solution.py:55
  152.7 2.6 collective-permute-done.19
  161.6 4.8 %attend.1 = (bf16[128,512]{1,0:T(8,128)(2,1)S(1)}, f32[128,128]{1,0:T(8,128)S(1)}, f32[128,128]{1,0:T(8,128)S(1)}) custom-call(s32[3]{0:T(128)S(1)} %pad_add_fusion.where_ref.place_ref, bf16[128,512]{1,0:T(8,128)(2,1)S(1)} %copy-done.54, bf16[4,144,256]{2,1,0:T(8,128)(2,1)S(1)} %pad_maximum_fusion.10.own_ref, ...), custom_call_target="tpu_custom_call" | custom-call | flops 268435456 | bytes 589824 | tf_op jit(solution)/shard_map/attend/pallas_call | solution.py:1116
  169.8 20.3 %middle.1 = (bf16[128,1024]{1,0:T(8,128)(2,1)}, bf16[4,128,2048]{2,1,0:T(8,128)(2,1)}, bf16[4,128,512]{2,1,0:T(8,128)(2,1)}, bf16[128,4096]{1,0:T(8,128)(2,1)}, ...) custom-call(s32[3]{0:T(128)S(1)} %pad_add_fusion.where_ref.place_ref, ...), custom_call_target="tpu_custom_call" | custom-call | flops 4294967296 | bytes 25165824 | tf_op jit(solution)/shard_map/middle/pallas_call | solution.py:627
  192.3 6.2 %attend_back.1 = (bf16[128,512]{1,0:T(8,128)(2,1)S(1)}, f32[4,128,256]{2,1,0:T(8,128)S(1)}, bf16[4,128,256]{2,1,0:T(8,128)(2,1)S(1)}) custom-call(s32[3]{0:T(128)S(1)} %pad_add_fusion.where_ref.place_ref, bf16[128,512]{1,0:T(8,128)(2,1)S(1)} %copy-done.54, bf16[4,144,256]{2,1,0:T(8,128)(2,1)S(1)} %pad_maximum_fusion.10.own_ref, ...), custom_call_target="tpu_custom_call" | custom-call | flops 671088640 | bytes 1179648 | tf_op jit(solution)/shard_map/attend_back/pallas_call | solution.py:1190
  204.0 7.6 %collective-permute-done.31 = bf16[768,128]{1,0:T(8,128)(2,1)S(1)} collective-permute-done((bf16[768,128]{1,0:T(8,128)(2,1)S(1)}, bf16[768,128]{1,0:T(8,128)(2,1)S(1)}, u32[]{:S(2)}, u32[]{:S(2)}) %collective-permute-start.31) | collective-permute-done | bytes 196640 | tf_op jit(solution)/shard_map/ppermute | solution.py:55
  213.3 5.0 %collective-permute-done.33 = bf16[768,128]{1,0:T(8,128)(2,1)S(1)} collective-permute-done((bf16[768,128]{1,0:T(8,128)(2,1)S(1)}, bf16[768,128]{1,0:T(8,128)(2,1)S(1)}, u32[]{:S(2)}, u32[]{:S(2)}) %collective-permute-start.33) | collective-permute-done | bytes 196640 | tf_op jit(solution)/shard_map/ppermute | solution.py:55
  218.8 3.0 collective-permute-start.34
  223.8 5.5 %ssm_backward.1 = (f32[128,1792]{1,0:T(8,128)S(1)}, f32[8,1792]{1,0:T(8,128)S(1)}, f32[128,128]{1,0:T(8,128)S(1)}, bf16[16,4224]{1,0:T(8,128)(2,1)S(1)}) custom-call(bf16[128,1792]{1,0:T(8,128)(2,1)S(1)} %copy-done.30, bf16[16,1792]{1,0:T(8,128)(2,1)S(1)} %copy-done.46, f32[128,128]{1,0:T(8,128)S(1)} %copy-done.43, f32[4,1792]{1,0:T(4,128)S(1)} %reshape.114.taps_ref, ...), custom_call_target="tpu_custom_call" | custom-call | flops 805306368 | bytes 8388608 | tf_op jit(solution)/shard_map/ssm_backward/pallas_call | solution.py:1043
  233.2 9.2 %collective-permute-start.35 = (f32[8,1792]{1,0:T(8,128)S(1)}, f32[8,1792]{1,0:T(8,128)S(1)}, u32[]{:S(2)}, u32[]{:S(2)}) collective-permute-start(f32[8,1792]{1,0:T(8,128)S(1)} %get-tuple-element.111), channel_id=1, source_target_pairs={{1,0},{2,1},{3,2},{4,3},{5,4},{6,5},{7,6},{9,8},{10,9},{11,10},{12... | collective-permute-start | bytes 172040 | tf_op jit(solution)/shard_map/ppermute | solution.py:1384
  242.4 4.8 %out_grads.1 = (f32[128,4096]{1,0:T(8,128)S(1)}, bf16[128,4096]{1,0:T(8,128)(2,1)}) custom-call(s32[3]{0:T(128)S(1)} %pad_add_fusion.where_ref.place_ref, bf16[128,2048]{1,0:T(8,128)(2,1)S(1)} %get-tuple-element.197.refs_0_, bf16[128,2048]{1,0:T(8,128)(2,1)S(1)} %collective-permute-done.39.refs_1_, bf16[128,2048]{1,0:T(8,128)(2,1)S(1)} %collective-permute-done.40.refs_2_, ...), custom_call_target="tpu_custom_call" | custom-call | flops 1073741824 | bytes 6291456 | tf_op jit(solution)/shard_map/out_grads/pallas_call | solution.py:695
  257.6 15.9 %collective-permute-done.49.refs_5_ = bf16[128,4096]{1,0:T(8,128)(2,1)} collective-permute-done((bf16[128,4096]{1,0:T(8,128)(2,1)}, bf16[128,4096]{1,0:T(8,128)(2,1)}, u32[]{:S(2)}, u32[]{:S(2)}) %collective-permute-start.49) | collective-permute-done | bytes 1048608 | tf_op jit(solution)/shard_map/ppermute | solution.py:60
  282.0 33.5 %collective-permute-done.48.refs_3_ = bf16[128,512]{1,0:T(8,128)(2,1)S(1)} collective-permute-done((bf16[128,512]{1,0:T(8,128)(2,1)S(1)}, bf16[128,512]{1,0:T(8,128)(2,1)S(1)}, u32[]{:S(2)}, u32[]{:S(2)}) %collective-permute-start.48) | collective-permute-done | bytes 131104 | tf_op jit(solution)/shard_map/ppermute | solution.py:60
  315.5 5.3 %feed_grads.1 = (f32[128,4096]{1,0:T(8,128)S(1)}, bf16[128,4096]{1,0:T(8,128)(2,1)}) custom-call(s32[3]{0:T(128)S(1)} %pad_add_fusion.where_ref.place_ref, bf16[128,512]{1,0:T(8,128)(2,1)S(1)} %get-tuple-element.215.refs_0_, bf16[128,512]{1,0:T(8,128)(2,1)} %collective-permute-done.46.refs_1_, bf16[128,512]{1,0:T(8,128)(2,1)S(1)} %collective-permute-done.47.refs_2_, ...), custom_call_target="tpu_custom_call" | custom-call | flops 1073741824 | bytes 7864320 | tf_op jit(solution)/shard_map/feed_grads/pallas_call | solution.py:695
  322.2 3.6 collective-permute-start.53
  331.0 2.7 collective-permute-start.69
  335.3 10.6 %collective-permute-done.69 = bf16[32,4096]{1,0:T(8,128)(2,1)S(1)} collective-permute-done((bf16[32,4096]{1,0:T(8,128)(2,1)S(1)}, bf16[32,4096]{1,0:T(8,128)(2,1)S(1)}, u32[]{:S(2)}, u32[]{:S(2)}) %collective-permute-start.69) | collective-permute-done | bytes 262176 | tf_op jit(solution)/shard_map/ppermute | solution.py:95
  346.0 7.4 %collective-permute-done.54 = bf16[64,4096]{1,0:T(8,128)(2,1)S(1)} collective-permute-done((bf16[64,4096]{1,0:T(8,128)(2,1)S(1)}, bf16[64,4096]{1,0:T(8,128)(2,1)S(1)}, u32[]{:S(2)}, u32[]{:S(2)}) %collective-permute-start.54) | collective-permute-done | bytes 524320 | tf_op jit(solution)/shard_map/ppermute | solution.py:95
  353.8 13.6 %collective-permute-done.55 = bf16[32,4096]{1,0:T(8,128)(2,1)S(1)} collective-permute-done((bf16[32,4096]{1,0:T(8,128)(2,1)S(1)}, bf16[32,4096]{1,0:T(8,128)(2,1)S(1)}, u32[]{:S(2)}, u32[]{:S(2)}) %collective-permute-start.55) | collective-permute-done | bytes 262176 | tf_op jit(solution)/shard_map/ppermute | solution.py:95
  367.5 5.6 %last_grads.1 = (f32[128,4224]{1,0:T(8,128)S(1)}, bf16[144,4224]{1,0:T(8,128)(2,1)S(1)}, f32[8,4224]{1,0:T(8,128)S(1)}) custom-call(s32[3]{0:T(128)S(1)} %pad_add_fusion.where_ref.place_ref, bf16[128,512]{1,0:T(8,128)(2,1)S(1)} %get-tuple-element.215.refs_0_, bf16[128,512]{1,0:T(8,128)(2,1)} %collective-permute-done.46.refs_1_, ...), custom_call_target="tpu_custom_call" | custom-call | flops 1245708288 | bytes 4866048 | tf_op jit(solution)/shard_map/last_grads/pallas_call | solution.py:407
  376.8 12.7 %collective-permute-done.72 = bf16[32,4096]{1,0:T(8,128)(2,1)S(1)} collective-permute-done((bf16[32,4096]{1,0:T(8,128)(2,1)S(1)}, bf16[32,4096]{1,0:T(8,128)(2,1)S(1)}, u32[]{:S(2)}, u32[]{:S(2)}) %collective-permute-start.72) | collective-permute-done | bytes 262176 | tf_op jit(solution)/shard_map/ppermute | solution.py:95
  389.6 9.1 %collective-permute-done.61 = bf16[80,4224]{1,0:T(8,128)(2,1)S(1)} collective-permute-done((bf16[80,4224]{1,0:T(8,128)(2,1)S(1)}, bf16[80,4224]{1,0:T(8,128)(2,1)S(1)}, u32[]{:S(2)}, u32[]{:S(2)}) %collective-permute-start.61) | collective-permute-done | bytes 675872 | tf_op jit(solution)/shard_map/ppermute | solution.py:95
  399.1 17.9 %collective-permute-done.73 = bf16[64,4096]{1,0:T(8,128)(2,1)S(1)} collective-permute-done((bf16[64,4096]{1,0:T(8,128)(2,1)S(1)}, bf16[64,4096]{1,0:T(8,128)(2,1)S(1)}, u32[]{:S(2)}, u32[]{:S(2)}) %collective-permute-start.73) | collective-permute-done | bytes 524320 | tf_op jit(solution)/shard_map/ppermute | solution.py:95
  419.4 2.3 collective-permute-start.74
  421.7 9.8 %collective-permute-done.63 = bf16[32,4224]{1,0:T(8,128)(2,1)S(1)} collective-permute-done((bf16[32,4224]{1,0:T(8,128)(2,1)S(1)}, bf16[32,4224]{1,0:T(8,128)(2,1)S(1)}, u32[]{:S(2)}, u32[]{:S(2)}) %collective-permute-start.63) | collective-permute-done | bytes 270368 | tf_op jit(solution)/shard_map/ppermute | solution.py:95
  437.8 8.4 %unproject.1 = f32[128,1024]{1,0:T(8,128)} custom-call(s32[3]{0:T(128)S(1)} %pad_add_fusion.where_ref.place_ref, bf16[128,1024]{1,0:T(8,128)(2,1)S(1)} %copy-done.10, f32[1,1024]{1,0:T(1,128)S(1)} %bitcast.58, f32[128,1024]{1,0:T(8,128)S(1)} %copy-done.31, bf16[144,4224]{1,0:T(8,128)(2,1)S(1)} %pack.1.back_ref.refs_4_, ...), custom_call_target="tpu_custom_call" | custom-call | flops 1107296256 | bytes 11796480 | tf_op jit(solution)/shard_map/unproject/pallas_call | solution.py:349
  446.3 4.0 last_out.1
  453.8 3.9 last_feed.1
  465.6 2.7 last_in.1
  470.2 5.1 %copy.47 = f32[256,3352]{0,1:T(8,128)} copy(f32[256,3352]{1,0:T(8,128)} %copy-done.7) | data formatting | bytes 6864896
  (422 shorter events, 135.9 us)
Async XLA Ops:
  9.4 26.0 %collective-permute-start.5 = (bf16[128,4224]{1,0:T(8,128)(2,1)}, bf16[128,4224]{1,0:T(8,128)(2,1)}, u32[]{:S(2)}, u32[]{:S(2)}) collective-permute-start(bf16[128,4224]{1,0:T(8,128)(2,1)} %constant_dynamic-slice_fusion.6), channel_id=1, source_target_pairs={{0,16},{8,24},{16,0},{24,8},{1,17},{9,25},{17,1},{25,9},{2,18},{10... | collective-permute-start | bytes 3244040 | tf_op jit(solution)/shard_map/ppermute | solution.py:60
  11.4 27.6 %collective-permute-start.3 = (bf16[128,4224]{1,0:T(8,128)(2,1)}, bf16[128,4224]{1,0:T(8,128)(2,1)}, u32[]{:S(2)}, u32[]{:S(2)}) collective-permute-start(bf16[128,4224]{1,0:T(8,128)(2,1)} %constant_dynamic-slice_fusion.6), channel_id=1, source_target_pairs={{0,8},{8,0},{16,24},{24,16},{1,9},{9,1},{17,25},{25,17},{2,10},{10... | collective-permute-start | bytes 3244040 | tf_op jit(solution)/shard_map/ppermute | solution.py:60
  40.9 21.5 %collective-permute-start.7 = (bf16[64,4224]{1,0:T(8,128)(2,1)}, bf16[64,4224]{1,0:T(8,128)(2,1)}, u32[]{:S(2)}, u32[]{:S(2)}) collective-permute-start(bf16[64,4224]{1,0:T(8,128)(2,1)} %slice.259), channel_id=1, source_target_pairs={{0,16},{8,24},{16,0},{24,8},{1,17},{9,25},{17,1},{25,9},{2,18},{10... | collective-permute-start | bytes 1622024 | tf_op jit(solution)/shard_map/ppermute | solution.py:60
  52.2 18.2 %collective-permute-start.4 = (bf16[128,4224]{1,0:T(8,128)(2,1)}, bf16[128,4224]{1,0:T(8,128)(2,1)S(1)}, u32[]{:S(2)}, u32[]{:S(2)}) collective-permute-start(bf16[128,4224]{1,0:T(8,128)(2,1)} %collective-permute-done.3.refs_0_), channel_id=1, source_target_pairs={{0,1},{1,0},{2,3},{3,2},{4,5},{5,4},{6,7},{7,6},{8,9},{9,8},{10,11... | collective-permute-start | bytes 3244040 | tf_op jit(solution)/shard_map/ppermute | solution.py:43
  52.2 18.2 %collective-permute-start.6 = (bf16[128,4224]{1,0:T(8,128)(2,1)}, bf16[128,4224]{1,0:T(8,128)(2,1)}, u32[]{:S(2)}, u32[]{:S(2)}) collective-permute-start(bf16[128,4224]{1,0:T(8,128)(2,1)} %collective-permute-done.5.refs_2_), channel_id=1, source_target_pairs={{0,1},{1,0},{2,3},{3,2},{4,5},{5,4},{6,7},{7,6},{8,9},{9,8},{10,11... | collective-permute-start | bytes 3244040 | tf_op jit(solution)/shard_map/ppermute | solution.py:43
  61.3 46.9 %collective-permute-start.21 = (bf16[128,8192]{1,0:T(8,128)(2,1)}, bf16[128,8192]{1,0:T(8,128)(2,1)}, u32[]{:S(2)}, u32[]{:S(2)}) collective-permute-start(bf16[128,8192]{1,0:T(8,128)(2,1)} %dynamic-slice_dynamic-update-slice_fusion.2), channel_id=1, source_target_pairs={{0,8},{8,0},{16,24},{24,16},{1,9},{9,1},{17,25},{25,17},{2,10},{10... | collective-permute-start | bytes 6291464 | tf_op jit(solution)/shard_map/ppermute | solution.py:60
  62.5 45.8 %collective-permute-start.22 = (bf16[128,8192]{1,0:T(8,128)(2,1)}, bf16[128,8192]{1,0:T(8,128)(2,1)}, u32[]{:S(2)}, u32[]{:S(2)}) collective-permute-start(bf16[128,8192]{1,0:T(8,128)(2,1)} %dynamic-slice_dynamic-update-slice_fusion.2), channel_id=1, source_target_pairs={{0,16},{8,24},{16,0},{24,8},{1,17},{9,25},{17,1},{25,9},{2,18},{10... | collective-permute-start | bytes 6291464 | tf_op jit(solution)/shard_map/ppermute | solution.py:60
  87.3 29.4 %collective-permute-start.42 = (bf16[128,1024]{1,0:T(8,128)(2,1)}, bf16[128,1024]{1,0:T(8,128)(2,1)S(1)}, u32[]{:S(2)}, u32[]{:S(2)}) collective-permute-start(bf16[128,1024]{1,0:T(8,128)(2,1)} %refs_4_.1), channel_id=1, source_target_pairs={{0,8},{8,0},{16,24},{24,16},{1,9},{9,1},{17,25},{25,17},{2,10},{10... | collective-permute-start | bytes 786440 | tf_op jit(solution)/shard_map/ppermute | solution.py:60
  92.1 15.4 %collective-permute-start.16 = (bf16[4,144,256]{2,1,0:T(8,128)(2,1)S(1)}, bf16[4,144,256]{2,1,0:T(8,128)(2,1)}, u32[]{:S(2)}, u32[]{:S(2)}) collective-permute-start(bf16[4,144,256]{2,1,0:T(8,128)(2,1)S(1)} %pad_maximum_fusion.10.own_ref), channel_id=1, source_target_pairs={{0,1},{1,0},{2,3},{3,2},{4,5},{5,4},{6,7},{7,6},{8,9},{9,8},{10,11... | collective-permute-start | bytes 884744 | tf_op jit(solution)/shard_map/ppermute | solution.py:43
  100.4 24.2 %collective-permute-start.43 = (bf16[128,1024]{1,0:T(8,128)(2,1)}, bf16[128,1024]{1,0:T(8,128)(2,1)}, u32[]{:S(2)}, u32[]{:S(2)}) collective-permute-start(bf16[128,1024]{1,0:T(8,128)(2,1)} %refs_4_.1), channel_id=1, source_target_pairs={{0,16},{8,24},{16,0},{24,8},{1,17},{9,25},{17,1},{25,9},{2,18},{10... | collective-permute-start | bytes 786440 | tf_op jit(solution)/shard_map/ppermute | solution.py:60
  107.5 15.1 %collective-permute-start.12 = (bf16[768,128]{1,0:T(8,128)(2,1)}, bf16[768,128]{1,0:T(8,128)(2,1)}, u32[]{:S(2)}, u32[]{:S(2)}) collective-permute-start(bf16[768,128]{1,0:T(8,128)(2,1)} %constant_dynamic-slice_fusion.4), channel_id=1, source_target_pairs={{0,1},{1,0},{2,3},{3,2},{4,5},{5,4},{6,7},{7,6},{8,9},{9,8},{10,11... | collective-permute-start | bytes 589832 | tf_op jit(solution)/shard_map/ppermute | solution.py:43
  110.6 41.2 %collective-permute-start.25 = (bf16[64,8192]{1,0:T(8,128)(2,1)}, bf16[64,8192]{1,0:T(8,128)(2,1)}, u32[]{:S(2)}, u32[]{:S(2)}) collective-permute-start(bf16[64,8192]{1,0:T(8,128)(2,1)} %slice.222), channel_id=1, source_target_pairs={{0,16},{8,24},{16,0},{24,8},{1,17},{9,25},{17,1},{25,9},{2,18},{10... | collective-permute-start | bytes 3145736 | tf_op jit(solution)/shard_map/ppermute | solution.py:60
  114.1 38.5 %collective-permute-start.27 = (bf16[64,8192]{1,0:T(8,128)(2,1)}, bf16[64,8192]{1,0:T(8,128)(2,1)}, u32[]{:S(2)}, u32[]{:S(2)}) collective-permute-start(bf16[64,8192]{1,0:T(8,128)(2,1)} %slice.223), channel_id=1, source_target_pairs={{0,8},{8,0},{16,24},{24,16},{1,9},{9,1},{17,25},{25,17},{2,10},{10... | collective-permute-start | bytes 3145736 | tf_op jit(solution)/shard_map/ppermute | solution.py:60
  116.7 49.8 %collective-permute-start.23 = (bf16[128,8192]{1,0:T(8,128)(2,1)}, bf16[128,8192]{1,0:T(8,128)(2,1)S(1)}, u32[]{:S(2)}, u32[]{:S(2)}) collective-permute-start(bf16[128,8192]{1,0:T(8,128)(2,1)} %collective-permute-done.21.refs_0_), channel_id=1, source_target_pairs={{0,1},{1,0},{2,3},{3,2},{4,5},{5,4},{6,7},{7,6},{8,9},{9,8},{10,11... | collective-permute-start | bytes 6291464 | tf_op jit(solution)/shard_map/ppermute | solution.py:43
  122.6 45.2 %collective-permute-start.24 = (bf16[128,8192]{1,0:T(8,128)(2,1)}, bf16[128,8192]{1,0:T(8,128)(2,1)S(1)}, u32[]{:S(2)}, u32[]{:S(2)}) collective-permute-start(bf16[128,8192]{1,0:T(8,128)(2,1)} %collective-permute-done.22.refs_2_), channel_id=1, source_target_pairs={{0,1},{1,0},{2,3},{3,2},{4,5},{5,4},{6,7},{7,6},{8,9},{9,8},{10,11... | collective-permute-start | bytes 6291464 | tf_op jit(solution)/shard_map/ppermute | solution.py:43
  139.9 15.4 %collective-permute-start.19 = (bf16[768,128]{1,0:T(8,128)(2,1)S(1)}, bf16[768,128]{1,0:T(8,128)(2,1)S(1)}, u32[]{:S(2)}, u32[]{:S(2)}) collective-permute-start(bf16[768,128]{1,0:T(8,128)(2,1)S(1)} %fusion.2), channel_id=1, source_target_pairs={{0,6},{1,7},{8,14},{9,15},{16,22},{17,23},{24,30},{25,31}} | collective-permute-start | bytes 589832 | tf_op jit(solution)/shard_map/ppermute | solution.py:55
  151.8 16.0 %collective-permute-start.26 = (bf16[64,8192]{1,0:T(8,128)(2,1)}, bf16[64,8192]{1,0:T(8,128)(2,1)S(1)}, u32[]{:S(2)}, u32[]{:S(2)}) collective-permute-start(bf16[64,8192]{1,0:T(8,128)(2,1)} %collective-permute-done.25.refs_4_), channel_id=1, source_target_pairs={{0,1},{1,0},{2,3},{3,2},{4,5},{5,4},{6,7},{7,6},{8,9},{9,8},{10,11... | collective-permute-start | bytes 3145736 | tf_op jit(solution)/shard_map/ppermute | solution.py:43
  152.6 15.2 %collective-permute-start.28 = (bf16[64,8192]{1,0:T(8,128)(2,1)}, bf16[64,8192]{1,0:T(8,128)(2,1)S(1)}, u32[]{:S(2)}, u32[]{:S(2)}) collective-permute-start(bf16[64,8192]{1,0:T(8,128)(2,1)} %collective-permute-done.27.refs_6_), channel_id=1, source_target_pairs={{0,1},{1,0},{2,3},{3,2},{4,5},{5,4},{6,7},{7,6},{8,9},{9,8},{10,11... | collective-permute-start | bytes 3145736 | tf_op jit(solution)/shard_map/ppermute | solution.py:43
  159.2 70.0 %collective-permute-start.44 = (bf16[64,1024]{1,0:T(8,128)(2,1)S(1)}, bf16[64,1024]{1,0:T(8,128)(2,1)S(1)}, u32[]{:S(2)}, u32[]{:S(2)}) collective-permute-start(bf16[64,1024]{1,0:T(8,128)(2,1)S(1)} %slice.280), channel_id=1, source_target_pairs={{0,16},{8,24},{16,0},{24,8},{1,17},{9,25},{17,1},{25,9},{2,18},{10... | collective-permute-start | bytes 393224 | tf_op jit(solution)/shard_map/ppermute | solution.py:60
  166.5 64.1 %collective-permute-start.45 = (bf16[64,1024]{1,0:T(8,128)(2,1)S(1)}, bf16[64,1024]{1,0:T(8,128)(2,1)S(1)}, u32[]{:S(2)}, u32[]{:S(2)}) collective-permute-start(bf16[64,1024]{1,0:T(8,128)(2,1)S(1)} %slice.281), channel_id=1, source_target_pairs={{0,8},{8,0},{16,24},{24,16},{1,9},{9,1},{17,25},{25,17},{2,10},{10... | collective-permute-start | bytes 393224 | tf_op jit(solution)/shard_map/ppermute | solution.py:60
  202.4 16.0 %collective-permute-start.33 = (bf16[768,128]{1,0:T(8,128)(2,1)S(1)}, bf16[768,128]{1,0:T(8,128)(2,1)S(1)}, u32[]{:S(2)}, u32[]{:S(2)}) collective-permute-start(bf16[768,128]{1,0:T(8,128)(2,1)S(1)} %fusion.4), channel_id=1, source_target_pairs={{6,0},{7,1},{14,8},{15,9},{22,16},{23,17},{30,24},{31,25}} | collective-permute-start | bytes 589832 | tf_op jit(solution)/shard_map/ppermute | solution.py:55
  211.6 20.2 %collective-permute-start.39 = (bf16[128,2048]{1,0:T(8,128)(2,1)S(1)}, bf16[128,2048]{1,0:T(8,128)(2,1)S(1)}, u32[]{:S(2)}, u32[]{:S(2)}) collective-permute-start(bf16[128,2048]{1,0:T(8,128)(2,1)S(1)} %get-tuple-element.196), channel_id=1, source_target_pairs={{0,8},{8,0},{16,24},{24,16},{1,9},{9,1},{17,25},{25,17},{2,10},{10... | collective-permute-start | bytes 1572872 | tf_op jit(solution)/shard_map/ppermute | solution.py:60
  212.0 21.2 %collective-permute-start.40 = (bf16[128,2048]{1,0:T(8,128)(2,1)S(1)}, bf16[128,2048]{1,0:T(8,128)(2,1)S(1)}, u32[]{:S(2)}, u32[]{:S(2)}) collective-permute-start(bf16[128,2048]{1,0:T(8,128)(2,1)S(1)} %get-tuple-element.195), channel_id=1, source_target_pairs={{0,16},{8,24},{16,0},{24,8},{1,17},{9,25},{17,1},{25,9},{2,18},{10... | collective-permute-start | bytes 1572872 | tf_op jit(solution)/shard_map/ppermute | solution.py:60
  222.9 19.5 %collective-permute-start.41 = (bf16[128,2048]{1,0:T(8,128)(2,1)S(1)}, bf16[128,2048]{1,0:T(8,128)(2,1)S(1)}, u32[]{:S(2)}, u32[]{:S(2)}) collective-permute-start(bf16[128,2048]{1,0:T(8,128)(2,1)S(1)} %get-tuple-element.194), channel_id=1, source_target_pairs={{0,24},{8,16},{16,8},{24,0},{1,25},{9,17},{17,9},{25,1},{2,26},{10... | collective-permute-start | bytes 1572872 | tf_op jit(solution)/shard_map/ppermute | solution.py:60
  229.3 19.2 %collective-permute-start.36 = (bf16[128,256]{1,0:T(8,128)(2,1)S(1)}, bf16[128,256]{1,0:T(8,128)(2,1)S(1)}, u32[]{:S(2)}, u32[]{:S(2)}) collective-permute-start(bf16[128,256]{1,0:T(8,128)(2,1)S(1)} %get-tuple-element.218), channel_id=1, source_target_pairs={{2,0},{3,1},{4,2},{5,3},{6,4},{7,5},{10,8},{11,9},{12,10},{13,11},... | collective-permute-start | bytes 196616 | tf_op jit(solution)/shard_map/ppermute | solution.py:55
  230.6 17.9 %collective-permute-start.37 = (bf16[128,256]{1,0:T(8,128)(2,1)S(1)}, bf16[128,256]{1,0:T(8,128)(2,1)S(1)}, u32[]{:S(2)}, u32[]{:S(2)}) collective-permute-start(bf16[128,256]{1,0:T(8,128)(2,1)S(1)} %get-tuple-element.217), channel_id=1, source_target_pairs={{4,0},{5,1},{6,2},{7,3},{12,8},{13,9},{14,10},{15,11},{20,16},{21,... | collective-permute-start | bytes 196616 | tf_op jit(solution)/shard_map/ppermute | solution.py:55
  231.9 16.6 %collective-permute-start.38 = (bf16[128,256]{1,0:T(8,128)(2,1)S(1)}, bf16[128,256]{1,0:T(8,128)(2,1)S(1)}, u32[]{:S(2)}, u32[]{:S(2)}) collective-permute-start(bf16[128,256]{1,0:T(8,128)(2,1)S(1)} %get-tuple-element.216), channel_id=1, source_target_pairs={{6,0},{7,1},{14,8},{15,9},{22,16},{23,17},{30,24},{31,25}} | collective-permute-start | bytes 196616 | tf_op jit(solution)/shard_map/ppermute | solution.py:55
  233.2 15.3 %collective-permute-start.35 = (f32[8,1792]{1,0:T(8,128)S(1)}, f32[8,1792]{1,0:T(8,128)S(1)}, u32[]{:S(2)}, u32[]{:S(2)}) collective-permute-start(f32[8,1792]{1,0:T(8,128)S(1)} %get-tuple-element.111), channel_id=1, source_target_pairs={{1,0},{2,1},{3,2},{4,3},{5,4},{6,5},{7,6},{9,8},{10,9},{11,10},{12... | collective-permute-start | bytes 172040 | tf_op jit(solution)/shard_map/ppermute | solution.py:1384
  248.8 24.7 %collective-permute-start.49 = (bf16[128,4096]{1,0:T(8,128)(2,1)}, bf16[128,4096]{1,0:T(8,128)(2,1)}, u32[]{:S(2)}, u32[]{:S(2)}) collective-permute-start(bf16[128,4096]{1,0:T(8,128)(2,1)} %get-tuple-element.119.refs_4_), channel_id=1, source_target_pairs={{0,8},{8,0},{16,24},{24,16},{1,9},{9,1},{17,25},{25,17},{2,10},{10... | collective-permute-start | bytes 3145736 | tf_op jit(solution)/shard_map/ppermute | solution.py:60
  249.1 26.7 %collective-permute-start.50 = (bf16[128,4096]{1,0:T(8,128)(2,1)}, bf16[128,4096]{1,0:T(8,128)(2,1)}, u32[]{:S(2)}, u32[]{:S(2)}) collective-permute-start(bf16[128,4096]{1,0:T(8,128)(2,1)} %get-tuple-element.119.refs_4_), channel_id=1, source_target_pairs={{0,16},{8,24},{16,0},{24,8},{1,17},{9,25},{17,1},{25,9},{2,18},{10... | collective-permute-start | bytes 3145736 | tf_op jit(solution)/shard_map/ppermute | solution.py:60
  254.7 22.9 %collective-permute-start.67 = (bf16[64,4096]{1,0:T(8,128)(2,1)}, bf16[64,4096]{1,0:T(8,128)(2,1)}, u32[]{:S(2)}, u32[]{:S(2)}) collective-permute-start(bf16[64,4096]{1,0:T(8,128)(2,1)} %dynamic-slice_convert_fusion.1), channel_id=1, source_target_pairs={{0,2},{1,3},{2,0},{3,1},{4,6},{5,7},{6,4},{7,5},{8,10},{9,11},{10,... | collective-permute-start | bytes 1572872 | tf_op jit(solution)/shard_map/ppermute | solution.py:95
  256.1 21.2 %collective-permute-start.46 = (bf16[128,512]{1,0:T(8,128)(2,1)}, bf16[128,512]{1,0:T(8,128)(2,1)}, u32[]{:S(2)}, u32[]{:S(2)}) collective-permute-start(bf16[128,512]{1,0:T(8,128)(2,1)} %get-tuple-element.214), channel_id=1, source_target_pairs={{0,8},{8,0},{16,24},{24,16},{1,9},{9,1},{17,25},{25,17},{2,10},{10... | collective-permute-start | bytes 393224 | tf_op jit(solution)/shard_map/ppermute | solution.py:60
  256.4 23.6 %collective-permute-start.47 = (bf16[128,512]{1,0:T(8,128)(2,1)}, bf16[128,512]{1,0:T(8,128)(2,1)S(1)}, u32[]{:S(2)}, u32[]{:S(2)}) collective-permute-start(bf16[128,512]{1,0:T(8,128)(2,1)} %get-tuple-element.213), channel_id=1, source_target_pairs={{0,16},{8,24},{16,0},{24,8},{1,17},{9,25},{17,1},{25,9},{2,18},{10... | collective-permute-start | bytes 393224 | tf_op jit(solution)/shard_map/ppermute | solution.py:60
  273.5 52.3 %collective-permute-start.57 = (bf16[144,4224]{1,0:T(8,128)(2,1)S(1)}, bf16[144,4224]{1,0:T(8,128)(2,1)}, u32[]{:S(2)}, u32[]{:S(2)}) collective-permute-start(bf16[144,4224]{1,0:T(8,128)(2,1)S(1)} %pack.1.back_ref.refs_4_), channel_id=1, source_target_pairs={{0,16},{8,24},{16,0},{24,8},{1,17},{9,25},{17,1},{25,9},{2,18},{10... | collective-permute-start | bytes 3649544 | tf_op jit(solution)/shard_map/ppermute | solution.py:60
  275.8 51.6 %collective-permute-start.56 = (bf16[144,4224]{1,0:T(8,128)(2,1)S(1)}, bf16[144,4224]{1,0:T(8,128)(2,1)}, u32[]{:S(2)}, u32[]{:S(2)}) collective-permute-start(bf16[144,4224]{1,0:T(8,128)(2,1)S(1)} %pack.1.back_ref.refs_4_), channel_id=1, source_target_pairs={{0,8},{8,0},{16,24},{24,16},{1,9},{9,1},{17,25},{25,17},{2,10},{10... | collective-permute-start | bytes 3649544 | tf_op jit(solution)/shard_map/ppermute | solution.py:60
  277.3 38.2 %collective-permute-start.51 = (bf16[64,4096]{1,0:T(8,128)(2,1)S(1)}, bf16[64,4096]{1,0:T(8,128)(2,1)S(1)}, u32[]{:S(2)}, u32[]{:S(2)}) collective-permute-start(bf16[64,4096]{1,0:T(8,128)(2,1)S(1)} %slice.282), channel_id=1, source_target_pairs={{0,16},{8,24},{16,0},{24,8},{1,17},{9,25},{17,1},{25,9},{2,18},{10... | collective-permute-start | bytes 1572872 | tf_op jit(solution)/shard_map/ppermute | solution.py:60
  277.6 37.9 %collective-permute-start.52 = (bf16[64,4096]{1,0:T(8,128)(2,1)S(1)}, bf16[64,4096]{1,0:T(8,128)(2,1)S(1)}, u32[]{:S(2)}, u32[]{:S(2)}) collective-permute-start(bf16[64,4096]{1,0:T(8,128)(2,1)S(1)} %slice.283), channel_id=1, source_target_pairs={{0,8},{8,0},{16,24},{24,16},{1,9},{9,1},{17,25},{25,17},{2,10},{10... | collective-permute-start | bytes 1572872 | tf_op jit(solution)/shard_map/ppermute | solution.py:60
  280.0 35.5 %collective-permute-start.48 = (bf16[128,512]{1,0:T(8,128)(2,1)S(1)}, bf16[128,512]{1,0:T(8,128)(2,1)S(1)}, u32[]{:S(2)}, u32[]{:S(2)}) collective-permute-start(bf16[128,512]{1,0:T(8,128)(2,1)S(1)} %copy-done.79), channel_id=1, source_target_pairs={{0,24},{8,16},{16,8},{24,0},{1,25},{9,17},{17,9},{25,1},{2,26},{10... | collective-permute-start | bytes 393224 | tf_op jit(solution)/shard_map/ppermute | solution.py:60
  327.1 40.4 %collective-permute-start.59 = (bf16[80,4224]{1,0:T(8,128)(2,1)S(1)}, bf16[80,4224]{1,0:T(8,128)(2,1)S(1)}, u32[]{:S(2)}, u32[]{:S(2)}) collective-permute-start(bf16[80,4224]{1,0:T(8,128)(2,1)S(1)} %slice.285), channel_id=1, source_target_pairs={{0,8},{8,0},{16,24},{24,16},{1,9},{9,1},{17,25},{25,17},{2,10},{10... | collective-permute-start | bytes 2027528 | tf_op jit(solution)/shard_map/ppermute | solution.py:60
  328.5 39.0 %collective-permute-start.58 = (bf16[64,4224]{1,0:T(8,128)(2,1)S(1)}, bf16[64,4224]{1,0:T(8,128)(2,1)S(1)}, u32[]{:S(2)}, u32[]{:S(2)}) collective-permute-start(bf16[64,4224]{1,0:T(8,128)(2,1)S(1)} %slice.284), channel_id=1, source_target_pairs={{0,16},{8,24},{16,0},{24,8},{1,17},{9,25},{17,1},{25,9},{2,18},{10... | collective-permute-start | bytes 1622024 | tf_op jit(solution)/shard_map/ppermute | solution.py:60
  335.2 18.2 %collective-permute-start.54 = (bf16[64,4096]{1,0:T(8,128)(2,1)S(1)}, bf16[64,4096]{1,0:T(8,128)(2,1)S(1)}, u32[]{:S(2)}, u32[]{:S(2)}) collective-permute-start(bf16[64,4096]{1,0:T(8,128)(2,1)S(1)} %dynamic-slice_convert_fusion.2), channel_id=1, source_target_pairs={{0,2},{1,3},{2,0},{3,1},{4,6},{5,7},{6,4},{7,5},{8,10},{9,11},{10,... | collective-permute-start | bytes 1572872 | tf_op jit(solution)/shard_map/ppermute | solution.py:95
  353.7 20.1 %collective-permute-start.70 = (bf16[64,4096]{1,0:T(8,128)(2,1)S(1)}, bf16[64,4096]{1,0:T(8,128)(2,1)S(1)}, u32[]{:S(2)}, u32[]{:S(2)}) collective-permute-start(bf16[64,4096]{1,0:T(8,128)(2,1)S(1)} %pad_maximum_fusion.5), channel_id=1, source_target_pairs={{0,2},{1,3},{2,0},{3,1},{4,6},{5,7},{6,4},{7,5},{8,10},{9,11},{10,... | collective-permute-start | bytes 1572872 | tf_op jit(solution)/shard_map/ppermute | solution.py:95
  375.0 71.3 %collective-permute-start.71 = (bf16[128,4096]{1,0:T(8,128)(2,1)}, bf16[128,4096]{1,0:T(8,128)(2,1)}, u32[]{:S(2)}, u32[]{:S(2)}) collective-permute-start(bf16[128,4096]{1,0:T(8,128)(2,1)} %pad_maximum_fusion.1.mine_ref), channel_id=1, source_target_pairs={{0,1},{1,0},{2,3},{3,2},{4,5},{5,4},{6,7},{7,6},{8,9},{9,8},{10,11... | collective-permute-start | bytes 3145736 | tf_op jit(solution)/shard_map/ppermute | solution.py:43
  376.7 22.0 %collective-permute-start.61 = (bf16[80,4224]{1,0:T(8,128)(2,1)S(1)}, bf16[80,4224]{1,0:T(8,128)(2,1)S(1)}, u32[]{:S(2)}, u32[]{:S(2)}) collective-permute-start(bf16[80,4224]{1,0:T(8,128)(2,1)S(1)} %pad_maximum_fusion.3), channel_id=1, source_target_pairs={{0,2},{1,3},{2,0},{3,1},{4,6},{5,7},{6,4},{7,5},{8,10},{9,11},{10,... | collective-permute-start | bytes 2027528 | tf_op jit(solution)/shard_map/ppermute | solution.py:95
  389.5 27.4 %collective-permute-start.73 = (bf16[64,4096]{1,0:T(8,128)(2,1)S(1)}, bf16[64,4096]{1,0:T(8,128)(2,1)S(1)}, u32[]{:S(2)}, u32[]{:S(2)}) collective-permute-start(bf16[64,4096]{1,0:T(8,128)(2,1)S(1)} %pad_maximum_fusion.6), channel_id=1, source_target_pairs={{0,2},{1,3},{2,0},{3,1},{4,6},{5,7},{6,4},{7,5},{8,10},{9,11},{10,... | collective-permute-start | bytes 1572872 | tf_op jit(solution)/shard_map/ppermute | solution.py:95
  399.0 18.2 %collective-permute-start.62 = (bf16[48,4224]{1,0:T(8,128)(2,1)S(1)}, bf16[48,4224]{1,0:T(8,128)(2,1)S(1)}, u32[]{:S(2)}, u32[]{:S(2)}) collective-permute-start(bf16[48,4224]{1,0:T(8,128)(2,1)S(1)} %pad_maximum_fusion.7), channel_id=1, source_target_pairs={{0,4},{1,5},{2,6},{3,7},{4,0},{5,1},{6,2},{7,3},{8,12},{9,13},{10,... | collective-permute-start | bytes 1216520 | tf_op jit(solution)/shard_map/ppermute | solution.py:95
  419.4 33.2 %collective-permute-start.74 = (bf16[128,4096]{1,0:T(8,128)(2,1)}, bf16[128,4096]{1,0:T(8,128)(2,1)}, u32[]{:S(2)}, u32[]{:S(2)}) collective-permute-start(bf16[128,4096]{1,0:T(8,128)(2,1)} %pad_maximum_fusion.2.mine_ref), channel_id=1, source_target_pairs={{0,1},{1,0},{2,3},{3,2},{4,5},{5,4},{6,7},{7,6},{8,9},{9,8},{10,11... | collective-permute-start | bytes 3145736 | tf_op jit(solution)/shard_map/ppermute | solution.py:43
  432.6 25.9 %collective-permute-start.64 = (bf16[64,4224]{1,0:T(8,128)(2,1)}, bf16[64,4224]{1,0:T(8,128)(2,1)}, u32[]{:S(2)}, u32[]{:S(2)}) collective-permute-start(bf16[64,4224]{1,0:T(8,128)(2,1)} %pad_maximum_fusion.4), channel_id=1, source_target_pairs={{0,2},{1,3},{2,0},{3,1},{4,6},{5,7},{6,4},{7,5},{8,10},{9,11},{10,... | collective-permute-start | bytes 1622024 | tf_op jit(solution)/shard_map/ppermute | solution.py:95
  (118 other events, 1228.4 us)

commit v4 on v3

--- a/solution.py
+++ b/solution.py
@@ -139,7 +139,7 @@
     return total
 
 
-def ctx_state(low, decays, chips, core, later):
+def ctx_state(low, decays, chips, chip, core, later):
     half = INNER // 2
     mine = lax.dynamic_slice_in_dim(low, core * half, half, 0).astype(f32)
     others = lax.dynamic_slice_in_dim(low, (1 - core) * half, half, 0)
@@ -147,24 +147,48 @@
     even = jnp.where(core == 0, mine, got)
     odd = jnp.where(core == 0, got, mine)
     dec = lax.dynamic_slice_in_dim(decays, core * (MH // 2), MH // 2, 2)
-    dec = jnp.repeat(dec, MP, axis=2)[..., None]
+    here = lax.dynamic_index_in_dim(dec, chip, 0, False)
+    here = jnp.repeat(here, MP, axis=1)[..., None]
+    block_decay = [dec[c, 0] * dec[c, 1] for c in range(chips)]
     if later:
-        chip_value = even + dec[0, 0] * odd
+        total = even + here[0] * odd
     else:
-        chip_value = odd + dec[0, 1] * even
-    chip_low = chip_value.astype(bf16)
-    sign = -1 if later else 1
-    total = jnp.zeros_like(chip_value)
-    for k in range(chips - 1, 0, -1):
-        arrived = chip_shift(chip_low, sign * k, False).astype(f32)
-        rel = (sign * k) % chips
-        total = arrived + dec[rel, 0] * dec[rel, 1] * total
+        total = odd + here[1] * even
+    before = jnp.zeros_like(total)
+    reach = jnp.ones((MH // 2,), f32)
+    bit = 1
+
+    def wide(vec):
+        return jnp.repeat(vec, MP)[:, None]
+
+    while bit < chips:
+        if later or bit == 1:
+            arrived = chip_swap(total.astype(bf16), bit).astype(f32)
+        else:
+            arrived = chip_swap(jnp.concatenate(two(total), axis=0), bit).astype(f32)
+            arrived = arrived[:half] + arrived[half:]
+        upper = (chip & bit) != 0
+        takes = jnp.logical_not(upper) if later else upper
+        mine_at, other_at = chip // bit, (chip // bit) ^ 1
+        table = jnp.stack(block_decay)
+        mine_decay = lax.dynamic_index_in_dim(table, mine_at, 0, False)
+        other_decay = lax.dynamic_index_in_dim(table, other_at, 0, False)
+        before = before + jnp.where(takes, wide(reach) * arrived, 0.0)
+        reach = jnp.where(takes, reach * other_decay, reach)
+        if 2 * bit < chips:
+            total = jnp.where(
+                takes, wide(mine_decay) * arrived + total, wide(other_decay) * total + arrived
+            )
+            block_decay = [
+                block_decay[2 * i] * block_decay[2 * i + 1] for i in range(len(block_decay) // 2)
+            ]
+        bit *= 2
     if later:
-        for_odd = total
-        for_even = odd + dec[0, 1] * total
+        for_odd = before
+        for_even = odd + here[1] * before
     else:
-        for_even = total
-        for_odd = even + dec[0, 0] * total
+        for_even = before
+        for_odd = even + here[0] * before
     keep = jnp.where(core == 0, for_even, for_odd).astype(bf16)
     give = jnp.where(core == 0, for_odd, for_even).astype(bf16)
     back = swap_core(give)
@@ -720,19 +744,29 @@
     is0 = where_ref[1] == 0
     hr = mine_ref.shape[0]
     total = [jnp.zeros((hr, 1), f32), jnp.zeros((hr, 1), f32)]
+
+    def added(i, grad, here, cols):
+        total[i] = total[i] + jnp.sum(
+            grad * weight_ref[here, cols].astype(f32), axis=1, keepdims=True
+        )
+
     at = 0
-    for ref in (q_ref, k_ref, v_ref, mix_ref):
-        size = ref.shape[1]
-        for start in range(0, size, 512):
-            step = min(512, size - start)
-            cols = slice(at + start, at + start + step)
-            for i, grad in enumerate(halves_in_order(is0, mine_ref, other_ref, cols)):
-                here = slice(i * hr, (i + 1) * hr)
-                ref[here, start : start + step] = grad
-                total[i] = total[i] + jnp.sum(
-                    grad * weight_ref[here, cols].astype(f32), axis=1, keepdims=True
-                )
-        at += size
+    for ref in (q_ref, k_ref, v_ref):
+        cols = slice(at, at + ref.shape[1])
+        for i, grad in enumerate(halves_in_order(is0, mine_ref, other_ref, cols)):
+            here = slice(i * hr, (i + 1) * hr)
+            ref[here, :] = grad
+            added(i, grad, here, cols)
+        at += ref.shape[1]
+    mixed, part = mix_ref.shape[0], 128
+    for start in range(0, mixed, part):
+        size = min(part, mixed - start)
+        cols = slice(at + start, at + start + part)
+        turned = []
+        for i, grad in enumerate(halves_in_order(is0, mine_ref, other_ref, cols)):
+            added(i, grad, slice(i * hr, (i + 1) * hr), cols)
+            turned.append(jnp.transpose(grad)[:size])
+        mix_ref[start : start + size, :] = jnp.concatenate(turned, axis=1)
     for i in range(2):
         here = slice(i * hr, (i + 1) * hr)
         gin_ref[here, :] = total[i] / gain_ref[here, :].astype(f32)
@@ -741,10 +775,10 @@
 def last_in(where, mine, other, weight, gain, mixed):
     vm = pl.BlockSpec(memory_space=pltpu.VMEM)
     rows = 2 * mine.shape[0]
-    sizes = (QW, KW, KW, mixed, 1)
+    shapes = ((rows, QW), (rows, KW), (rows, KW), (mixed, rows), (rows, 1))
     return pl.pallas_call(
         last_in_kernel,
-        out_shape=tuple(jax.ShapeDtypeStruct((rows, size), f32) for size in sizes),
+        out_shape=tuple(jax.ShapeDtypeStruct(shape, f32) for shape in shapes),
         in_specs=[pl.BlockSpec(memory_space=pltpu.SMEM)] + [vm] * 4,
         out_specs=[vm] * 5,
         compiler_params=pltpu.CompilerParams(vmem_limit_bytes=40 * 2**20),
@@ -1276,11 +1310,26 @@
     chip, core = ctx // 2, ctx % 2
     ff = w_gate.shape[1]
 
+    used = QW + 2 * KW + w_mixin.shape[1]
+    wide = -(-used // 128) * 128
+    cut = width // (4 * seqs)
+    cut = cut if cut % 16 == 0 else 0
+    in_parts = [w_query, key_weight, value_weight, w_mixin]
+
+    def joined(parts):
+        blank = jnp.zeros((parts[0].shape[0], wide - used), bf16)
+        return jnp.concatenate([*parts, blank], axis=1)
+
+    in_half = joined(lax.optimization_barrier([take_half(part, core) for part in in_parts]))
+    near = first_phase(in_half)
     sizes = (gain_input.size, gain_feed.size, conv_bias.size, gain_mixer.size, conv_taps.size)
     small = jnp.concatenate(
         [gain_input, gain_feed, conv_bias, gain_mixer, conv_taps.reshape(-1)]
     )
     small = [small] + [seq_swap(small, k) for k in range(1, seqs)]
+    near, small, in_parts = lax.optimization_barrier((near, small, in_parts))
+    w_in = second_phase(near, cut)
+    in_loc = joined(in_parts)
     bit = 1
     while bit < seqs:
         flip = (place & bit) != 0
@@ -1298,13 +1347,6 @@
     gmix = pieces[3].reshape(-1)
     taps = pieces[4].reshape(seqs, KC, -1).transpose(1, 0, 2).reshape(KC, -1)
 
-    used = QW + 2 * KW + w_mixin.shape[1]
-    wide = -(-used // 128) * 128
-    blank = jnp.zeros((w_mixin.shape[0], wide - used), bf16)
-    in_loc = jnp.concatenate([w_query, key_weight, value_weight, w_mixin, blank], axis=1)
-    cut = width // (4 * seqs)
-    cut = cut if cut % 16 == 0 else 0
-    w_in = gather_pieces(take_half(in_loc, core), cut)
     out_loc = jnp.concatenate([w_mixout, w_attnout], axis=0)
     half_out = take_half(out_loc, core)
     half_dn = take_half(w_down, core)
@@ -1353,11 +1395,19 @@
     decays = jnp.stack(
         [jnp.where(core == 0, dec_own, dec_sib), jnp.where(core == 0, dec_sib, dec_own)], axis=1
     )
+    by_chip = jnp.arange(chips, dtype=jnp.int32)
+    picked = (chip - by_chip) % chips
+    decays = jnp.stack(
+        [
+            sum(jnp.where(picked[c] == k, decays[k], 0.0) for k in range(chips))
+            for c in range(chips)
+        ]
+    )
 
     act, out_zero, local_state, c_state, exp_cum = ssm_forward(
         conv_low, edge, raw_step, taps, cbias[None, :], offset, rates, skip_wide
     )
-    start_state = ctx_state(local_state, decays, chips, core, False)
+    start_state = ctx_state(local_state, decays, chips, chip, core, False)
     cots = [cotangent] + [p[2] for p in gather_pieces(cotangent, rows // 2)]
     queries, near = lax.optimization_barrier((queries, near))
     rest_far = second_phase(near, cut)
@@ -1369,14 +1419,18 @@
         gmix[None, :], gfeed[None, :], (w_gate, w_up, w_mixout, w_attnout, w_down), w_rest, seqs,
     )
     msgs1 = [msg1[0]] + [seq_swap(msg1[k], k) for k in range(1, seqs)]
+    d_att, d_gu, msg2, msgs1 = lax.optimization_barrier((d_att, d_gu, msg2, msgs1))
+    near = first_phase(d_gu)
     msgs2 = [msg2[0]] + [seq_swap(msg2[k], k) for k in range(1, seqs)]
 
-    later_grad = ctx_state(d_start, decays, chips, core, True)
+    later_grad = ctx_state(d_start, decays, chips, chip, core, True)
     d_q, d_kv, d_kv_sib = attend_back(
         where, queries, kv_own, kv_sib, top, total, d_att, cosine, sine
     )
     d_kv = d_kv + swap_core(d_kv_sib).astype(f32)
     arrived = [chip_shift(d_kv[k].astype(bf16), -k, False) for k in range(1, chips)]
+    later_grad, near = lax.optimization_barrier((later_grad, near))
+    rights2 = [d_gu] + [p[2] for p in second_phase(near, rows // 2)]
     d_conv, d_edge, d_raw, extra = ssm_backward(
         conv_low, edge, raw_step, taps, offset, rates, skip_wide, act,
         d_ssm, d_c, d_cum, later_grad, start_state, wide,
@@ -1386,26 +1440,28 @@
         d_q, d_kv[0], cosine, sine, d_gate_z, d_conv, edge_back, d_raw, extra, arrived
     )
     keep1, give1 = grads(grads_kernel, "out_grads", where, msgs1, cots, hr, 4 * width)
-    back_msg, keep1, give1 = lax.optimization_barrier((back_msg, keep1, give1))
+    back_msg, rights2, msgs2, give1 = lax.optimization_barrier((back_msg, rights2, msgs2, give1))
     total1, unused = sum_halves(keep1, swap_core(give1), chips, chip, None)
-    rights2 = [d_gu] + [p[2] for p in gather_pieces(d_gu, rows // 2)]
     keep2, give2 = grads(feed_grads_kernel, "feed_grads", where, msgs2, rights2, hr, 2 * ff)
     total2, unused = sum_halves(keep2, swap_core(give2), chips, chip, None)
+    mine1 = spread_halves(total1, chips, chip)
     backs = [back_msg] + [p[2] for p in gather_pieces(back_msg, rows // 2)]
-    backs[0], total2 = lax.optimization_barrier((backs[0], total2))
+    backs[0], total2, mine1 = lax.optimization_barrier((backs[0], total2, mine1))
     keep3, give3, small = last_grads(where, msgs2, backs, hr, rows // 2)
-    mine1 = spread_halves(total1, chips, chip)
     mine2 = spread_halves(total2, chips, chip)
     total3, small_sum = sum_halves(keep3, swap_core(give3), chips, chip, small)
     grad_tokens = unproject(where, tokens, gin[None, :], grad_res, back_msg, in_loc, w_in)
+    sums_out = last_out(
+        where, mine1, swap_core(mine1), w_mixout, gain_mixer[:, None], QW // seqs
+    )
+    total3, mine2, grad_tokens, sums_out = lax.optimization_barrier(
+        (total3, mine2, grad_tokens, sums_out)
+    )
+    sum_mix, sum_att, sum_dn, grad_gmix = sums_out
     mine3 = spread_halves(total3, chips, chip)
-
-    sum_mix, sum_att, sum_dn, grad_gmix = last_out(
-        where, mine1, swap_core(mine1), w_mixout, gain_mixer[:, None], QW // seqs
-    )
-    sum_gate, sum_up, grad_gfeed = last_feed(
-        where, mine2, swap_core(mine2), w_gate, w_up, gain_feed[:, None]
-    )
+    sums_feed = last_feed(where, mine2, swap_core(mine2), w_gate, w_up, gain_feed[:, None])
+    mine3, sums_feed = lax.optimization_barrier((mine3, sums_feed))
+    sum_gate, sum_up, grad_gfeed = sums_feed
     sum_q, sum_k, sum_v, sum_mixin, grad_gin = last_in(
         where, mine3, swap_core(mine3), in_loc, gain_input[:, None], used - mix0
     )
@@ -1423,7 +1479,7 @@
         sum_q,
         sum_k,
         sum_v,
-        sum_mixin,
+        sum_mixin.T,
         own_share(small_taps),
         own_share(small_sum[2, :CONVW]),
         heads[:MH],

time: 485 us -> 516 us (1.064)
  waiting for transfers between devices: 187 us -> 227 us
  starting transfers between devices: 105 us -> 83.7 us
  between operations: 2.68 us -> 13.2 us
    ppermute x12 -> x16, waiting for transfers between devices: 81.1 us -> 132 us  [chip_swap(): return lax.ppermute(value, 'ctx', [(i, i ^ 2 * bit) for i in range(count)])]
    ppermute x12 -> x6, starting transfers between devices: 32.9 us -> 7.66 us  [chip_shift(): return lax.ppermute(value, 'ctx', pairs)]
    ppermute x12 -> x6, waiting for transfers between devices: 23.4 us -> 0.02 us  [chip_shift(): return lax.ppermute(value, 'ctx', pairs)]
    ppermute x12 -> x16, starting transfers between devices: 4.17 us -> 23.8 us  [chip_swap(): return lax.ppermute(value, 'ctx', [(i, i ^ 2 * bit) for i in range(count)])]
    ppermute x29, waiting for transfers between devices: 77.9 us -> 91.8 us  [seq_swap(): return lax.ppermute(value, 'seq', [(i, i ^ k) for i in range(count)])]
    ppermute x20, starting transfers between devices: 28.2 us -> 15.9 us  [swap_core(): return lax.ppermute(value, 'ctx', [(i, i ^ 1) for i in range(count)])]
    unnamed x192 -> x256, local copies, waits for them, and re-layouts: 37.6 us -> 35 us
  transfers between devices with their start and end apart: 75 -> 73, of which waited for: 25 -> 27; matrix products, arithmetic and copies ran while one was open for 13% -> 12% of each run, Pallas kernels for 16% -> 9%
where the time goes in v4:
time: 516 us; the launch traced here: 509 us
  waiting for transfers between devices  227 us (44%)
  starting transfers between devices  83.7 us (16%)
  Pallas kernels  80.6 us (16%)
  local copies, waits for them, and re-layouts  74.8 us (14%)
  other arithmetic  30.3 us (6%)
  between operations  13.2 us (3%)
    ppermute x16, waiting for transfers between devices, chip_swap(): return lax.ppermute(value, 'ctx', [(i, i ^ 2 * bit) for i in range(count)])  132 us
    ppermute x29, waiting for transfers between devices, seq_swap(): return lax.ppermute(value, 'seq', [(i, i ^ k) for i in range(count)])  91.8 us
    unnamed x256, local copies, waits for them, and re-layouts  35 us
    ppermute x29, starting transfers between devices, seq_swap(): return lax.ppermute(value, 'seq', [(i, i ^ k) for i in range(count)])  25.5 us
    ppermute x16, starting transfers between devices, chip_swap(): return lax.ppermute(value, 'ctx', [(i, i ^ 2 * bit) for i in range(count)])  23.8 us
    pallas_call x1, Pallas kernels, middle(): pl.pallas_call(functools.partial(middle_kernel, seqs, [p[:3] for p in pie...  20.7 us
    ppermute x20, starting transfers between devices, swap_core(): return lax.ppermute(value, 'ctx', [(i, i ^ 1) for i in range(count)])  15.9 us
  transfers between devices with their start and end apart: 73, of which 27 were waited for; matrix products, arithmetic and copies ran while one was open for 12% of the time, Pallas kernels for 9%

profile of v4, /device:TPU:1, one launch (start us, length us, event | category | flops | bytes accessed | tf_op | source)
XLA Modules:
  0.0 509.2 jit_solution(3777702198194599316)
XLA Ops:
  3.7 3.2 concatenate.48
  10.7 2.3 collective-permute-start.4
  16.2 16.9 %collective-permute-done.2 = bf16[3136]{0:T(1024)(128)(2,1)S(1)} collective-permute-done((bf16[3136]{0:T(1024)(128)(2,1)S(1)}, bf16[3136]{0:T(1024)(128)(2,1)S(1)}, u32[]{:S(2)}, u32[]{:S(2)}) %collective-permute-start.2) | collective-permute-done | bytes 6304 | tf_op jit(solution)/shard_map/ppermute | solution.py:60
  46.2 7.7 %collective-permute-done.9.refs_6_ = bf16[64,4224]{1,0:T(8,128)(2,1)} collective-permute-done((bf16[64,4224]{1,0:T(8,128)(2,1)}, bf16[64,4224]{1,0:T(8,128)(2,1)}, u32[]{:S(2)}, u32[]{:S(2)}) %collective-permute-start.9) | collective-permute-done | bytes 540704 | tf_op jit(solution)/shard_map/ppermute | solution.py:60
  57.1 2.4 copy.43
  60.9 3.6 concatenate.50.local_ref.weight_ref
  66.4 7.7 %project.1 = (bf16[128,1024]{1,0:T(8,128)(2,1)S(1)}, bf16[128,512]{1,0:T(8,128)(2,1)S(1)}, bf16[144,256]{1,0:T(8,128)(2,1)}, f32[128,1536]{1,0:T(8,128)S(1)}, bf...) custom-call(s32[3]{0:T(128)S(1)} %pad_add_fusion.where_ref.place_ref, bf16[128,1024]{1,0:T(8,128)(2,1)S(1)} %copy-done.9, ...), custom_call_target="tpu_custom_call" | custom-call | flops 1107296256 | bytes 11796480 | tf_op jit(solution)/shard_map/project/pallas_call | solution.py:318
  77.8 3.3 collective-permute-start.15
  98.9 5.1 %collective-permute-start.11 = (bf16[16,1792]{1,0:T(8,128)(2,1)S(1)}, bf16[16,1792]{1,0:T(8,128)(2,1)S(1)}, u32[]{:S(2)}, u32[]{:S(2)}) collective-permute-start(bf16[16,1792]{1,0:T(8,128)(2,1)S(1)} %slice.277), channel_id=1, source_target_pairs={{0,1},{1,2},{2,3},{3,4},{4,5},{5,6},{6,7},{8,9},{9,10},{10,11},{11... | collective-permute-start | bytes 172040 | tf_op jit(solution)/shard_map/ppermute | solution.py:1388
  115.0 2.3 collective-permute-start.17
  117.4 22.0 %collective-permute-done.20.refs_0_ = bf16[128,8192]{1,0:T(8,128)(2,1)} collective-permute-done((bf16[128,8192]{1,0:T(8,128)(2,1)}, bf16[128,8192]{1,0:T(8,128)(2,1)}, u32[]{:S(2)}, u32[]{:S(2)}) %collective-permute-start.20) | collective-permute-done | bytes 2097184 | tf_op jit(solution)/shard_map/ppermute | solution.py:60
  139.6 2.3 slice.308
  143.1 2.3 slice.309
  146.2 2.6 collective-permute-start.22
  154.1 16.9 %collective-permute-done.18 = bf16[1536,128]{1,0:T(8,128)(2,1)} collective-permute-done((bf16[1536,128]{1,0:T(8,128)(2,1)}, bf16[1536,128]{1,0:T(8,128)(2,1)}, u32[]{:S(2)}, u32[]{:S(2)}) %collective-permute-start.18) | collective-permute-done | bytes 393248 | tf_op jit(solution)/shard_map/ppermute | solution.py:95
  179.8 4.8 attend.1
  186.0 20.7 %middle.1 = (bf16[128,1024]{1,0:T(8,128)(2,1)}, bf16[4,128,2048]{2,1,0:T(8,128)(2,1)}, bf16[4,128,512]{2,1,0:T(8,128)(2,1)}, bf16[128,4096]{1,0:T(8,128)(2,1)}, ...) custom-call(s32[3]{0:T(128)S(1)} %pad_add_fusion.where_ref.place_ref, ...), custom_call_target="tpu_custom_call" | custom-call | flops 4294967296 | bytes 25165824 | tf_op jit(solution)/shard_map/middle/pallas_call | solution.py:651
  210.8 3.0 slice_bitcast_fusion
  219.1 24.9 %collective-permute-done.47.refs_5_ = bf16[128,1024]{1,0:T(8,128)(2,1)} collective-permute-done((bf16[128,1024]{1,0:T(8,128)(2,1)}, bf16[128,1024]{1,0:T(8,128)(2,1)}, u32[]{:S(2)}, u32[]{:S(2)}) %collective-permute-start.47) | collective-permute-done | bytes 262176 | tf_op jit(solution)/shard_map/ppermute | solution.py:60
  244.0 3.0 collective-permute-start.34
  253.3 3.0 collective-permute-done.34
  264.5 6.2 %attend_back.1 = (bf16[128,512]{1,0:T(8,128)(2,1)S(1)}, f32[4,128,256]{2,1,0:T(8,128)S(1)}, bf16[4,128,256]{2,1,0:T(8,128)(2,1)S(1)}) custom-call(s32[3]{0:T(128)S(1)} %pad_add_fusion.where_ref.place_ref, bf16[128,512]{1,0:T(8,128)(2,1)S(1)} %copy-done.68, bf16[4,144,256]{2,1,0:T(8,128)(2,1)S(1)} %copy-done.53, ...), custom_call_target="tpu_custom_call" | custom-call | flops 671088640 | bytes 1179648 | tf_op jit(solution)/shard_map/attend_back/pallas_call | solution.py:1224
  272.5 4.3 collective-permute-done.36.refs_5_
  280.2 5.5 %ssm_backward.1 = (f32[128,1792]{1,0:T(8,128)S(1)}, f32[8,1792]{1,0:T(8,128)S(1)}, f32[128,128]{1,0:T(8,128)S(1)}, bf16[16,4224]{1,0:T(8,128)(2,1)S(1)}) custom-call(bf16[128,1792]{1,0:T(8,128)(2,1)S(1)} %copy-done.34, bf16[16,1792]{1,0:T(8,128)(2,1)S(1)} %copy-done.65, f32[128,128]{1,0:T(8,128)S(1)} %copy-done.59, f32[4,1792]{1,0:T(4,128)S(1)} %reshape.195.taps_ref, ...), custom_call_target="tpu_custom_call" | custom-call | flops 805306368 | bytes 8388608 | tf_op jit(solution)/shard_map/ssm_backward/pallas_call | solution.py:1077
  288.3 5.8 %collective-permute-start.38 = (f32[8,1792]{1,0:T(8,128)S(1)}, f32[8,1792]{1,0:T(8,128)S(1)}, u32[]{:S(2)}, u32[]{:S(2)}) collective-permute-start(f32[8,1792]{1,0:T(8,128)S(1)} %get-tuple-element.174), channel_id=1, source_target_pairs={{1,0},{2,1},{3,2},{4,3},{5,4},{6,5},{7,6},{9,8},{10,9},{11,10},{12... | collective-permute-start | bytes 172040 | tf_op jit(solution)/shard_map/ppermute | solution.py:1438
  294.1 5.5 %out_grads.1 = (f32[128,4096]{1,0:T(8,128)S(1)}, bf16[128,4096]{1,0:T(8,128)(2,1)}) custom-call(s32[3]{0:T(128)S(1)} %pad_add_fusion.where_ref.place_ref, bf16[128,2048]{1,0:T(8,128)(2,1)S(1)} %copy-done.49, bf16[128,2048]{1,0:T(8,128)(2,1)} %collective-permute-done.28.refs_1_, bf16[128,2048]{1,0:T(8,128)(2,1)} %collective-permute-done.29.refs_2_, ...), custom_call_target="tpu_custom_call" | custom-call | flops 1073741824 | bytes 6291456 | tf_op jit(solution)/shard_map/out_grads/pallas_call | solution.py:719
  303.8 2.7 collective-permute-done.44.refs_1_
  307.1 2.3 collective-permute-done.45.refs_2_
  322.8 3.3 feed_grads.1
  331.1 10.1 %collective-permute-done.60.refs_6_ = bf16[144,4224]{1,0:T(8,128)(2,1)S(1)} collective-permute-done((bf16[144,4224]{1,0:T(8,128)(2,1)S(1)}, bf16[144,4224]{1,0:T(8,128)(2,1)S(1)}, u32[]{:S(2)}, u32[]{:S(2)}) %collective-permute-start.60) | collective-permute-done | bytes 1216544 | tf_op jit(solution)/shard_map/ppermute | solution.py:60
  343.0 3.4 collective-permute-start.56
  346.4 12.8 %collective-permute-done.52 = bf16[64,4096]{1,0:T(8,128)(2,1)S(1)} collective-permute-done((bf16[64,4096]{1,0:T(8,128)(2,1)S(1)}, bf16[64,4096]{1,0:T(8,128)(2,1)S(1)}, u32[]{:S(2)}, u32[]{:S(2)}) %collective-permute-start.52) | collective-permute-done | bytes 524320 | tf_op jit(solution)/shard_map/ppermute | solution.py:95
  359.4 2.8 collective-permute-start.57
  362.3 16.8 %collective-permute-done.57 = bf16[32,4096]{1,0:T(8,128)(2,1)S(1)} collective-permute-done((bf16[32,4096]{1,0:T(8,128)(2,1)S(1)}, bf16[32,4096]{1,0:T(8,128)(2,1)S(1)}, u32[]{:S(2)}, u32[]{:S(2)}) %collective-permute-start.57) | collective-permute-done | bytes 262176 | tf_op jit(solution)/shard_map/ppermute | solution.py:95
  380.8 4.0 collective-permute-done.53
  384.9 12.1 %collective-permute-done.58 = bf16[64,4096]{1,0:T(8,128)(2,1)S(1)} collective-permute-done((bf16[64,4096]{1,0:T(8,128)(2,1)S(1)}, bf16[64,4096]{1,0:T(8,128)(2,1)S(1)}, u32[]{:S(2)}, u32[]{:S(2)}) %collective-permute-start.58) | collective-permute-done | bytes 524320 | tf_op jit(solution)/shard_map/ppermute | solution.py:95
  399.0 8.6 %unproject.1 = f32[128,1024]{1,0:T(8,128)} custom-call(s32[3]{0:T(128)S(1)} %pad_add_fusion.where_ref.place_ref, bf16[128,1024]{1,0:T(8,128)(2,1)S(1)} %copy-done.10, f32[1,1024]{1,0:T(1,128)S(1)} %bitcast.92, f32[128,1024]{1,0:T(8,128)S(1)} %copy-done.35, bf16[144,4224]{1,0:T(8,128)(2,1)S(1)} %pack.1.refs_4_.back_ref, ...), custom_call_target="tpu_custom_call" | custom-call | flops 1107296256 | bytes 11796480 | tf_op jit(solution)/shard_map/unproject/pallas_call | solution.py:373
  407.6 4.5 last_grads.1
  413.1 2.3 collective-permute-start.67
  415.9 2.3 collective-permute-start.64
  418.1 9.2 %collective-permute-done.67 = bf16[64,4096]{1,0:T(8,128)(2,1)S(1)} collective-permute-done((bf16[64,4096]{1,0:T(8,128)(2,1)S(1)}, bf16[64,4096]{1,0:T(8,128)(2,1)S(1)}, u32[]{:S(2)}, u32[]{:S(2)}) %collective-permute-start.67) | collective-permute-done | bytes 524320 | tf_op jit(solution)/shard_map/ppermute | solution.py:95
  427.5 14.3 %collective-permute-done.64 = bf16[80,4224]{1,0:T(8,128)(2,1)S(1)} collective-permute-done((bf16[80,4224]{1,0:T(8,128)(2,1)S(1)}, bf16[80,4224]{1,0:T(8,128)(2,1)S(1)}, u32[]{:S(2)}, u32[]{:S(2)}) %collective-permute-start.64) | collective-permute-done | bytes 675872 | tf_op jit(solution)/shard_map/ppermute | solution.py:95
  443.2 2.9 last_out.1
  446.1 16.0 %collective-permute-done.65 = bf16[48,4224]{1,0:T(8,128)(2,1)S(1)} collective-permute-done((bf16[48,4224]{1,0:T(8,128)(2,1)S(1)}, bf16[48,4224]{1,0:T(8,128)(2,1)S(1)}, u32[]{:S(2)}, u32[]{:S(2)}) %collective-permute-start.65) | collective-permute-done | bytes 405536 | tf_op jit(solution)/shard_map/ppermute | solution.py:95
  462.2 14.5 %collective-permute-done.69 = bf16[32,4224]{1,0:T(8,128)(2,1)S(1)} collective-permute-done((bf16[32,4224]{1,0:T(8,128)(2,1)S(1)}, bf16[32,4224]{1,0:T(8,128)(2,1)S(1)}, u32[]{:S(2)}, u32[]{:S(2)}) %collective-permute-start.69) | collective-permute-done | bytes 270368 | tf_op jit(solution)/shard_map/ppermute | solution.py:95
  477.7 12.6 %collective-permute-done.70 = bf16[64,4224]{1,0:T(8,128)(2,1)} collective-permute-done((bf16[64,4224]{1,0:T(8,128)(2,1)S(1)}, bf16[64,4224]{1,0:T(8,128)(2,1)}, u32[]{:S(2)}, u32[]{:S(2)}) %collective-permute-start.70) | collective-permute-done | bytes 540704 | tf_op jit(solution)/shard_map/ppermute | solution.py:95
  491.7 4.0 last_feed.1
  503.6 4.7 last_in.1
  (510 shorter events, 142.7 us)
Async XLA Ops:
  7.0 27.0 %collective-permute-start = (bf16[128,4224]{1,0:T(8,128)(2,1)}, bf16[128,4224]{1,0:T(8,128)(2,1)}, u32[]{:S(2)}, u32[]{:S(2)}) collective-permute-start(bf16[128,4224]{1,0:T(8,128)(2,1)} %concatenate.48), channel_id=1, source_target_pairs={{0,8},{8,0},{16,24},{24,16},{1,9},{9,1},{17,25},{25,17},{2,10},{10... | collective-permute-start | bytes 3244040 | tf_op jit(solution)/shard_map/ppermute | solution.py:60
  9.0 24.9 %collective-permute-start.1 = (bf16[128,4224]{1,0:T(8,128)(2,1)}, bf16[128,4224]{1,0:T(8,128)(2,1)}, u32[]{:S(2)}, u32[]{:S(2)}) collective-permute-start(bf16[128,4224]{1,0:T(8,128)(2,1)} %concatenate.48), channel_id=1, source_target_pairs={{0,16},{8,24},{16,0},{24,8},{1,17},{9,25},{17,1},{25,9},{2,18},{10... | collective-permute-start | bytes 3244040 | tf_op jit(solution)/shard_map/ppermute | solution.py:60
  10.4 22.6 %collective-permute-start.2 = (bf16[3136]{0:T(1024)(128)(2,1)S(1)}, bf16[3136]{0:T(1024)(128)(2,1)S(1)}, u32[]{:S(2)}, u32[]{:S(2)}) collective-permute-start(bf16[3136]{0:T(1024)(128)(2,1)S(1)} %concatenate.49), channel_id=1, source_target_pairs={{0,8},{8,0},{16,24},{24,16},{1,9},{9,1},{17,25},{25,17},{2,10},{10... | collective-permute-start | bytes 18824 | tf_op jit(solution)/shard_map/ppermute | solution.py:60
  10.7 23.2 %collective-permute-start.3 = (bf16[3136]{0:T(1024)(128)(2,1)S(1)}, bf16[3136]{0:T(1024)(128)(2,1)S(1)}, u32[]{:S(2)}, u32[]{:S(2)}) collective-permute-start(bf16[3136]{0:T(1024)(128)(2,1)S(1)} %concatenate.49), channel_id=1, source_target_pairs={{0,16},{8,24},{16,0},{24,8},{1,17},{9,25},{17,1},{25,9},{2,18},{10... | collective-permute-start | bytes 18824 | tf_op jit(solution)/shard_map/ppermute | solution.py:60
  10.7 23.2 %collective-permute-start.4 = (bf16[3136]{0:T(1024)(128)(2,1)S(1)}, bf16[3136]{0:T(1024)(128)(2,1)S(1)}, u32[]{:S(2)}, u32[]{:S(2)}) collective-permute-start(bf16[3136]{0:T(1024)(128)(2,1)S(1)} %concatenate.49), channel_id=1, source_target_pairs={{0,24},{8,16},{16,8},{24,0},{1,25},{9,17},{17,9},{25,1},{2,26},{10... | collective-permute-start | bytes 18824 | tf_op jit(solution)/shard_map/ppermute | solution.py:60
  36.4 28.2 %collective-permute-start.5 = (bf16[128,4224]{1,0:T(8,128)(2,1)}, bf16[128,4224]{1,0:T(8,128)(2,1)S(1)}, u32[]{:S(2)}, u32[]{:S(2)}) collective-permute-start(bf16[128,4224]{1,0:T(8,128)(2,1)} %collective-permute-done.refs_0_), channel_id=1, source_target_pairs={{0,1},{1,0},{2,3},{3,2},{4,5},{5,4},{6,7},{7,6},{8,9},{9,8},{10,11... | collective-permute-start | bytes 3244040 | tf_op jit(solution)/shard_map/ppermute | solution.py:43
  40.2 24.4 %collective-permute-start.6 = (bf16[128,4224]{1,0:T(8,128)(2,1)}, bf16[128,4224]{1,0:T(8,128)(2,1)}, u32[]{:S(2)}, u32[]{:S(2)}) collective-permute-start(bf16[128,4224]{1,0:T(8,128)(2,1)} %collective-permute-done.1.refs_2_), channel_id=1, source_target_pairs={{0,1},{1,0},{2,3},{3,2},{4,5},{5,4},{6,7},{7,6},{8,9},{9,8},{10,11... | collective-permute-start | bytes 3244040 | tf_op jit(solution)/shard_map/ppermute | solution.py:43
  77.8 16.7 %collective-permute-start.15 = (bf16[144,256]{1,0:T(8,128)(2,1)}, bf16[144,256]{1,0:T(8,128)(2,1)S(1)}, u32[]{:S(2)}, u32[]{:S(2)}) collective-permute-start(bf16[144,256]{1,0:T(8,128)(2,1)} %get-tuple-element.147), channel_id=1, source_target_pairs={{0,6},{1,7},{2,0},{3,1},{4,2},{5,3},{6,4},{7,5},{8,14},{9,15},{10,... | collective-permute-start | bytes 221192 | tf_op jit(solution)/shard_map/ppermute | solution.py:55
  92.7 46.7 %collective-permute-start.20 = (bf16[128,8192]{1,0:T(8,128)(2,1)}, bf16[128,8192]{1,0:T(8,128)(2,1)}, u32[]{:S(2)}, u32[]{:S(2)}) collective-permute-start(bf16[128,8192]{1,0:T(8,128)(2,1)} %dynamic-slice_dynamic-update-slice_fusion.2), channel_id=1, source_target_pairs={{0,8},{8,0},{16,24},{24,16},{1,9},{9,1},{17,25},{25,17},{2,10},{10... | collective-permute-start | bytes 6291464 | tf_op jit(solution)/shard_map/ppermute | solution.py:60
  93.3 46.3 %collective-permute-start.21 = (bf16[128,8192]{1,0:T(8,128)(2,1)}, bf16[128,8192]{1,0:T(8,128)(2,1)}, u32[]{:S(2)}, u32[]{:S(2)}) collective-permute-start(bf16[128,8192]{1,0:T(8,128)(2,1)} %dynamic-slice_dynamic-update-slice_fusion.2), channel_id=1, source_target_pairs={{0,16},{8,24},{16,0},{24,8},{1,17},{9,25},{17,1},{25,9},{2,18},{10... | collective-permute-start | bytes 6291464 | tf_op jit(solution)/shard_map/ppermute | solution.py:60
  95.5 16.0 %collective-permute-start.16 = (bf16[4,144,256]{2,1,0:T(8,128)(2,1)S(1)}, bf16[4,144,256]{2,1,0:T(8,128)(2,1)}, u32[]{:S(2)}, u32[]{:S(2)}) collective-permute-start(bf16[4,144,256]{2,1,0:T(8,128)(2,1)S(1)} %pad_maximum_fusion.11.own_ref), channel_id=1, source_target_pairs={{0,1},{1,0},{2,3},{3,2},{4,5},{5,4},{6,7},{7,6},{8,9},{9,8},{10,11... | collective-permute-start | bytes 884744 | tf_op jit(solution)/shard_map/ppermute | solution.py:43
  115.0 34.0 %collective-permute-start.17 = (bf16[768,128]{1,0:T(8,128)(2,1)}, bf16[768,128]{1,0:T(8,128)(2,1)}, u32[]{:S(2)}, u32[]{:S(2)}) collective-permute-start(bf16[768,128]{1,0:T(8,128)(2,1)} %fusion.13), channel_id=1, source_target_pairs={{0,2},{1,3},{2,0},{3,1},{4,6},{5,7},{6,4},{7,5},{8,10},{9,11},{10,... | collective-permute-start | bytes 589832 | tf_op jit(solution)/shard_map/ppermute | solution.py:95
  141.8 30.3 %collective-permute-start.24 = (bf16[64,8192]{1,0:T(8,128)(2,1)}, bf16[64,8192]{1,0:T(8,128)(2,1)}, u32[]{:S(2)}, u32[]{:S(2)}) collective-permute-start(bf16[64,8192]{1,0:T(8,128)(2,1)} %slice.308), channel_id=1, source_target_pairs={{0,16},{8,24},{16,0},{24,8},{1,17},{9,25},{17,1},{25,9},{2,18},{10... | collective-permute-start | bytes 3145736 | tf_op jit(solution)/shard_map/ppermute | solution.py:60
  145.3 28.2 %collective-permute-start.26 = (bf16[64,8192]{1,0:T(8,128)(2,1)}, bf16[64,8192]{1,0:T(8,128)(2,1)}, u32[]{:S(2)}, u32[]{:S(2)}) collective-permute-start(bf16[64,8192]{1,0:T(8,128)(2,1)} %slice.309), channel_id=1, source_target_pairs={{0,8},{8,0},{16,24},{24,16},{1,9},{9,1},{17,25},{25,17},{2,10},{10... | collective-permute-start | bytes 3145736 | tf_op jit(solution)/shard_map/ppermute | solution.py:60
  146.2 38.5 %collective-permute-start.22 = (bf16[128,8192]{1,0:T(8,128)(2,1)}, bf16[128,8192]{1,0:T(8,128)(2,1)}, u32[]{:S(2)}, u32[]{:S(2)}) collective-permute-start(bf16[128,8192]{1,0:T(8,128)(2,1)} %collective-permute-done.20.refs_0_), channel_id=1, source_target_pairs={{0,1},{1,0},{2,3},{3,2},{4,5},{5,4},{6,7},{7,6},{8,9},{9,8},{10,11... | collective-permute-start | bytes 6291464 | tf_op jit(solution)/shard_map/ppermute | solution.py:43
  148.7 35.9 %collective-permute-start.23 = (bf16[128,8192]{1,0:T(8,128)(2,1)}, bf16[128,8192]{1,0:T(8,128)(2,1)}, u32[]{:S(2)}, u32[]{:S(2)}) collective-permute-start(bf16[128,8192]{1,0:T(8,128)(2,1)} %collective-permute-done.21.refs_2_), channel_id=1, source_target_pairs={{0,1},{1,0},{2,3},{3,2},{4,5},{5,4},{6,7},{7,6},{8,9},{9,8},{10,11... | collective-permute-start | bytes 6291464 | tf_op jit(solution)/shard_map/ppermute | solution.py:43
  151.2 19.8 %collective-permute-start.18 = (bf16[1536,128]{1,0:T(8,128)(2,1)}, bf16[1536,128]{1,0:T(8,128)(2,1)}, u32[]{:S(2)}, u32[]{:S(2)}) collective-permute-start(bf16[1536,128]{1,0:T(8,128)(2,1)} %pad_maximum_fusion.8), channel_id=1, source_target_pairs={{0,4},{1,5},{2,6},{3,7},{4,0},{5,1},{6,2},{7,3},{8,12},{9,13},{10,... | collective-permute-start | bytes 1179656 | tf_op jit(solution)/shard_map/ppermute | solution.py:95
  213.8 37.4 %collective-permute-start.28 = (bf16[128,2048]{1,0:T(8,128)(2,1)}, bf16[128,2048]{1,0:T(8,128)(2,1)}, u32[]{:S(2)}, u32[]{:S(2)}) collective-permute-start(bf16[128,2048]{1,0:T(8,128)(2,1)} %get-tuple-element.247), channel_id=1, source_target_pairs={{0,8},{8,0},{16,24},{24,16},{1,9},{9,1},{17,25},{25,17},{2,10},{10... | collective-permute-start | bytes 1572872 | tf_op jit(solution)/shard_map/ppermute | solution.py:60
  215.1 36.6 %collective-permute-start.29 = (bf16[128,2048]{1,0:T(8,128)(2,1)}, bf16[128,2048]{1,0:T(8,128)(2,1)}, u32[]{:S(2)}, u32[]{:S(2)}) collective-permute-start(bf16[128,2048]{1,0:T(8,128)(2,1)} %get-tuple-element.246), channel_id=1, source_target_pairs={{0,16},{8,24},{16,0},{24,8},{1,17},{9,25},{17,1},{25,9},{2,18},{10... | collective-permute-start | bytes 1572872 | tf_op jit(solution)/shard_map/ppermute | solution.py:60
  215.3 36.4 %collective-permute-start.30 = (bf16[128,2048]{1,0:T(8,128)(2,1)}, bf16[128,2048]{1,0:T(8,128)(2,1)}, u32[]{:S(2)}, u32[]{:S(2)}) collective-permute-start(bf16[128,2048]{1,0:T(8,128)(2,1)} %get-tuple-element.245), channel_id=1, source_target_pairs={{0,24},{8,16},{16,8},{24,0},{1,25},{9,17},{17,9},{25,1},{2,26},{10... | collective-permute-start | bytes 1572872 | tf_op jit(solution)/shard_map/ppermute | solution.py:60
  216.5 27.4 %collective-permute-start.47 = (bf16[128,1024]{1,0:T(8,128)(2,1)}, bf16[128,1024]{1,0:T(8,128)(2,1)}, u32[]{:S(2)}, u32[]{:S(2)}) collective-permute-start(bf16[128,1024]{1,0:T(8,128)(2,1)} %refs_4_.1), channel_id=1, source_target_pairs={{0,8},{8,0},{16,24},{24,16},{1,9},{9,1},{17,25},{25,17},{2,10},{10... | collective-permute-start | bytes 786440 | tf_op jit(solution)/shard_map/ppermute | solution.py:60
  217.8 30.8 %collective-permute-start.48 = (bf16[128,1024]{1,0:T(8,128)(2,1)}, bf16[128,1024]{1,0:T(8,128)(2,1)}, u32[]{:S(2)}, u32[]{:S(2)}) collective-permute-start(bf16[128,1024]{1,0:T(8,128)(2,1)} %refs_4_.1), channel_id=1, source_target_pairs={{0,16},{8,24},{16,0},{24,8},{1,17},{9,25},{17,1},{25,9},{2,18},{10... | collective-permute-start | bytes 786440 | tf_op jit(solution)/shard_map/ppermute | solution.py:60
  248.5 37.1 %collective-permute-start.49 = (bf16[64,1024]{1,0:T(8,128)(2,1)}, bf16[64,1024]{1,0:T(8,128)(2,1)}, u32[]{:S(2)}, u32[]{:S(2)}) collective-permute-start(bf16[64,1024]{1,0:T(8,128)(2,1)} %slice.364), channel_id=1, source_target_pairs={{0,16},{8,24},{16,0},{24,8},{1,17},{9,25},{17,1},{25,9},{2,18},{10... | collective-permute-start | bytes 393224 | tf_op jit(solution)/shard_map/ppermute | solution.py:60
  251.2 35.8 %collective-permute-start.50 = (bf16[64,1024]{1,0:T(8,128)(2,1)}, bf16[64,1024]{1,0:T(8,128)(2,1)S(1)}, u32[]{:S(2)}, u32[]{:S(2)}) collective-permute-start(bf16[64,1024]{1,0:T(8,128)(2,1)} %slice.365), channel_id=1, source_target_pairs={{0,8},{8,0},{16,24},{24,16},{1,9},{9,1},{17,25},{25,17},{2,10},{10... | collective-permute-start | bytes 393224 | tf_op jit(solution)/shard_map/ppermute | solution.py:60
  251.8 25.0 %collective-permute-start.36 = (bf16[128,4096]{1,0:T(8,128)(2,1)S(1)}, bf16[128,4096]{1,0:T(8,128)(2,1)S(1)}, u32[]{:S(2)}, u32[]{:S(2)}) collective-permute-start(bf16[128,4096]{1,0:T(8,128)(2,1)S(1)} %copy-done.19), channel_id=1, source_target_pairs={{0,8},{8,0},{16,24},{24,16},{1,9},{9,1},{17,25},{25,17},{2,10},{10... | collective-permute-start | bytes 3145736 | tf_op jit(solution)/shard_map/ppermute | solution.py:60
  252.8 24.0 %collective-permute-start.37 = (bf16[128,4096]{1,0:T(8,128)(2,1)S(1)}, bf16[128,4096]{1,0:T(8,128)(2,1)S(1)}, u32[]{:S(2)}, u32[]{:S(2)}) collective-permute-start(bf16[128,4096]{1,0:T(8,128)(2,1)S(1)} %copy-done.19), channel_id=1, source_target_pairs={{0,16},{8,24},{16,0},{24,8},{1,17},{9,25},{17,1},{25,9},{2,18},{10... | collective-permute-start | bytes 3145736 | tf_op jit(solution)/shard_map/ppermute | solution.py:60
  276.9 33.9 %collective-permute-start.42 = (bf16[64,4096]{1,0:T(8,128)(2,1)S(1)}, bf16[64,4096]{1,0:T(8,128)(2,1)S(1)}, u32[]{:S(2)}, u32[]{:S(2)}) collective-permute-start(bf16[64,4096]{1,0:T(8,128)(2,1)S(1)} %slice.318), channel_id=1, source_target_pairs={{0,16},{8,24},{16,0},{24,8},{1,17},{9,25},{17,1},{25,9},{2,18},{10... | collective-permute-start | bytes 1572872 | tf_op jit(solution)/shard_map/ppermute | solution.py:60
  277.5 34.0 %collective-permute-start.43 = (bf16[64,4096]{1,0:T(8,128)(2,1)S(1)}, bf16[64,4096]{1,0:T(8,128)(2,1)S(1)}, u32[]{:S(2)}, u32[]{:S(2)}) collective-permute-start(bf16[64,4096]{1,0:T(8,128)(2,1)S(1)} %slice.319), channel_id=1, source_target_pairs={{0,8},{8,0},{16,24},{24,16},{1,9},{9,1},{17,25},{25,17},{2,10},{10... | collective-permute-start | bytes 1572872 | tf_op jit(solution)/shard_map/ppermute | solution.py:60
  285.7 15.2 %collective-permute-start.40 = (bf16[128,256]{1,0:T(8,128)(2,1)S(1)}, bf16[128,256]{1,0:T(8,128)(2,1)S(1)}, u32[]{:S(2)}, u32[]{:S(2)}) collective-permute-start(bf16[128,256]{1,0:T(8,128)(2,1)S(1)} %get-tuple-element.268), channel_id=1, source_target_pairs={{4,0},{5,1},{6,2},{7,3},{12,8},{13,9},{14,10},{15,11},{20,16},{21,... | collective-permute-start | bytes 196616 | tf_op jit(solution)/shard_map/ppermute | solution.py:55
  287.0 14.2 %collective-permute-start.41 = (bf16[128,256]{1,0:T(8,128)(2,1)S(1)}, bf16[128,256]{1,0:T(8,128)(2,1)S(1)}, u32[]{:S(2)}, u32[]{:S(2)}) collective-permute-start(bf16[128,256]{1,0:T(8,128)(2,1)S(1)} %get-tuple-element.267), channel_id=1, source_target_pairs={{6,0},{7,1},{14,8},{15,9},{22,16},{23,17},{30,24},{31,25}} | collective-permute-start | bytes 196616 | tf_op jit(solution)/shard_map/ppermute | solution.py:55
  312.3 14.4 %collective-permute-start.54 = (bf16[128,4096]{1,0:T(8,128)(2,1)}, bf16[128,4096]{1,0:T(8,128)(2,1)}, u32[]{:S(2)}, u32[]{:S(2)}) collective-permute-start(bf16[128,4096]{1,0:T(8,128)(2,1)} %get-tuple-element.198), channel_id=1, source_target_pairs={{0,1},{1,0},{2,3},{3,2},{4,5},{5,4},{6,7},{7,6},{8,9},{9,8},{10,11... | collective-permute-start | bytes 3145736 | tf_op jit(solution)/shard_map/ppermute | solution.py:43
  312.8 28.4 %collective-permute-start.60 = (bf16[144,4224]{1,0:T(8,128)(2,1)S(1)}, bf16[144,4224]{1,0:T(8,128)(2,1)S(1)}, u32[]{:S(2)}, u32[]{:S(2)}) collective-permute-start(bf16[144,4224]{1,0:T(8,128)(2,1)S(1)} %pack.1.refs_4_.back_ref), channel_id=1, source_target_pairs={{0,16},{8,24},{16,0},{24,8},{1,17},{9,25},{17,1},{25,9},{2,18},{10... | collective-permute-start | bytes 3649544 | tf_op jit(solution)/shard_map/ppermute | solution.py:60
  313.7 28.8 %collective-permute-start.59 = (bf16[144,4224]{1,0:T(8,128)(2,1)S(1)}, bf16[144,4224]{1,0:T(8,128)(2,1)S(1)}, u32[]{:S(2)}, u32[]{:S(2)}) collective-permute-start(bf16[144,4224]{1,0:T(8,128)(2,1)S(1)} %pack.1.refs_4_.back_ref), channel_id=1, source_target_pairs={{0,8},{8,0},{16,24},{24,16},{1,9},{9,1},{17,25},{25,17},{2,10},{10... | collective-permute-start | bytes 3649544 | tf_op jit(solution)/shard_map/ppermute | solution.py:60
  328.3 14.6 %collective-permute-start.55 = (bf16[64,4096]{1,0:T(8,128)(2,1)S(1)}, bf16[64,4096]{1,0:T(8,128)(2,1)S(1)}, u32[]{:S(2)}, u32[]{:S(2)}) collective-permute-start(bf16[64,4096]{1,0:T(8,128)(2,1)S(1)} %dynamic-slice_convert_fusion.1), channel_id=1, source_target_pairs={{0,2},{1,3},{2,0},{3,1},{4,6},{5,7},{6,4},{7,5},{8,10},{9,11},{10,... | collective-permute-start | bytes 1572872 | tf_op jit(solution)/shard_map/ppermute | solution.py:95
  330.4 28.8 %collective-permute-start.52 = (bf16[64,4096]{1,0:T(8,128)(2,1)S(1)}, bf16[64,4096]{1,0:T(8,128)(2,1)S(1)}, u32[]{:S(2)}, u32[]{:S(2)}) collective-permute-start(bf16[64,4096]{1,0:T(8,128)(2,1)S(1)} %dynamic-slice_convert_fusion.2), channel_id=1, source_target_pairs={{0,2},{1,3},{2,0},{3,1},{4,6},{5,7},{6,4},{7,5},{8,10},{9,11},{10,... | collective-permute-start | bytes 1572872 | tf_op jit(solution)/shard_map/ppermute | solution.py:95
  341.3 66.3 %collective-permute-start.62 = (bf16[80,4224]{1,0:T(8,128)(2,1)S(1)}, bf16[80,4224]{1,0:T(8,128)(2,1)S(1)}, u32[]{:S(2)}, u32[]{:S(2)}) collective-permute-start(bf16[80,4224]{1,0:T(8,128)(2,1)S(1)} %slice.367), channel_id=1, source_target_pairs={{0,8},{8,0},{16,24},{24,16},{1,9},{9,1},{17,25},{25,17},{2,10},{10... | collective-permute-start | bytes 2027528 | tf_op jit(solution)/shard_map/ppermute | solution.py:60
  342.6 65.0 %collective-permute-start.61 = (bf16[64,4224]{1,0:T(8,128)(2,1)S(1)}, bf16[64,4224]{1,0:T(8,128)(2,1)S(1)}, u32[]{:S(2)}, u32[]{:S(2)}) collective-permute-start(bf16[64,4224]{1,0:T(8,128)(2,1)S(1)} %slice.366), channel_id=1, source_target_pairs={{0,16},{8,24},{16,0},{24,8},{1,17},{9,25},{17,1},{25,9},{2,18},{10... | collective-permute-start | bytes 1622024 | tf_op jit(solution)/shard_map/ppermute | solution.py:60
  343.0 16.3 %collective-permute-start.56 = (bf16[32,4096]{1,0:T(8,128)(2,1)S(1)}, bf16[32,4096]{1,0:T(8,128)(2,1)S(1)}, u32[]{:S(2)}, u32[]{:S(2)}) collective-permute-start(bf16[32,4096]{1,0:T(8,128)(2,1)S(1)} %dynamic-slice_convert_fusion.4), channel_id=1, source_target_pairs={{0,4},{1,5},{2,6},{3,7},{4,0},{5,1},{6,2},{7,3},{8,12},{9,13},{10,... | collective-permute-start | bytes 786440 | tf_op jit(solution)/shard_map/ppermute | solution.py:95
  359.4 19.8 %collective-permute-start.57 = (bf16[32,4096]{1,0:T(8,128)(2,1)S(1)}, bf16[32,4096]{1,0:T(8,128)(2,1)S(1)}, u32[]{:S(2)}, u32[]{:S(2)}) collective-permute-start(bf16[32,4096]{1,0:T(8,128)(2,1)S(1)} %add_convert_fusion.1), channel_id=1, source_target_pairs={{0,4},{1,5},{2,6},{3,7},{4,0},{5,1},{6,2},{7,3},{8,12},{9,13},{10,... | collective-permute-start | bytes 786440 | tf_op jit(solution)/shard_map/ppermute | solution.py:95
  362.2 22.6 %collective-permute-start.53 = (bf16[32,4096]{1,0:T(8,128)(2,1)S(1)}, bf16[32,4096]{1,0:T(8,128)(2,1)S(1)}, u32[]{:S(2)}, u32[]{:S(2)}) collective-permute-start(bf16[32,4096]{1,0:T(8,128)(2,1)S(1)} %dynamic-slice_convert_fusion.5), channel_id=1, source_target_pairs={{0,4},{1,5},{2,6},{3,7},{4,0},{5,1},{6,2},{7,3},{8,12},{9,13},{10,... | collective-permute-start | bytes 786440 | tf_op jit(solution)/shard_map/ppermute | solution.py:95
  379.2 17.8 %collective-permute-start.58 = (bf16[64,4096]{1,0:T(8,128)(2,1)S(1)}, bf16[64,4096]{1,0:T(8,128)(2,1)S(1)}, u32[]{:S(2)}, u32[]{:S(2)}) collective-permute-start(bf16[64,4096]{1,0:T(8,128)(2,1)S(1)} %pad_maximum_fusion.5), channel_id=1, source_target_pairs={{0,2},{1,3},{2,0},{3,1},{4,6},{5,7},{6,4},{7,5},{8,10},{9,11},{10,... | collective-permute-start | bytes 1572872 | tf_op jit(solution)/shard_map/ppermute | solution.py:95
  397.4 15.7 %collective-permute-start.66 = (bf16[32,4096]{1,0:T(8,128)(2,1)S(1)}, bf16[32,4096]{1,0:T(8,128)(2,1)S(1)}, u32[]{:S(2)}, u32[]{:S(2)}) collective-permute-start(bf16[32,4096]{1,0:T(8,128)(2,1)S(1)} %add_convert_fusion.2), channel_id=1, source_target_pairs={{0,4},{1,5},{2,6},{3,7},{4,0},{5,1},{6,2},{7,3},{8,12},{9,13},{10,... | collective-permute-start | bytes 786440 | tf_op jit(solution)/shard_map/ppermute | solution.py:95
  412.9 30.3 %collective-permute-start.68 = (bf16[128,4096]{1,0:T(8,128)(2,1)S(1)}, bf16[128,4096]{1,0:T(8,128)(2,1)S(1)}, u32[]{:S(2)}, u32[]{:S(2)}) collective-permute-start(bf16[128,4096]{1,0:T(8,128)(2,1)S(1)} %pad_maximum_fusion.1.mine_ref), channel_id=1, source_target_pairs={{0,1},{1,0},{2,3},{3,2},{4,5},{5,4},{6,7},{7,6},{8,9},{9,8},{10,11... | collective-permute-start | bytes 3145736 | tf_op jit(solution)/shard_map/ppermute | solution.py:43
  413.1 14.2 %collective-permute-start.67 = (bf16[64,4096]{1,0:T(8,128)(2,1)S(1)}, bf16[64,4096]{1,0:T(8,128)(2,1)S(1)}, u32[]{:S(2)}, u32[]{:S(2)}) collective-permute-start(bf16[64,4096]{1,0:T(8,128)(2,1)S(1)} %pad_maximum_fusion.6), channel_id=1, source_target_pairs={{0,2},{1,3},{2,0},{3,1},{4,6},{5,7},{6,4},{7,5},{8,10},{9,11},{10,... | collective-permute-start | bytes 1572872 | tf_op jit(solution)/shard_map/ppermute | solution.py:95
  415.9 25.9 %collective-permute-start.64 = (bf16[80,4224]{1,0:T(8,128)(2,1)S(1)}, bf16[80,4224]{1,0:T(8,128)(2,1)S(1)}, u32[]{:S(2)}, u32[]{:S(2)}) collective-permute-start(bf16[80,4224]{1,0:T(8,128)(2,1)S(1)} %pad_maximum_fusion.3), channel_id=1, source_target_pairs={{0,2},{1,3},{2,0},{3,1},{4,6},{5,7},{6,4},{7,5},{8,10},{9,11},{10,... | collective-permute-start | bytes 2027528 | tf_op jit(solution)/shard_map/ppermute | solution.py:95
  442.1 20.0 %collective-permute-start.65 = (bf16[48,4224]{1,0:T(8,128)(2,1)S(1)}, bf16[48,4224]{1,0:T(8,128)(2,1)S(1)}, u32[]{:S(2)}, u32[]{:S(2)}) collective-permute-start(bf16[48,4224]{1,0:T(8,128)(2,1)S(1)} %pad_maximum_fusion.7), channel_id=1, source_target_pairs={{0,4},{1,5},{2,6},{3,7},{4,0},{5,1},{6,2},{7,3},{8,12},{9,13},{10,... | collective-permute-start | bytes 1216520 | tf_op jit(solution)/shard_map/ppermute | solution.py:95
  462.2 14.5 %collective-permute-start.69 = (bf16[32,4224]{1,0:T(8,128)(2,1)S(1)}, bf16[32,4224]{1,0:T(8,128)(2,1)S(1)}, u32[]{:S(2)}, u32[]{:S(2)}) collective-permute-start(bf16[32,4224]{1,0:T(8,128)(2,1)S(1)} %add_convert_fusion), channel_id=1, source_target_pairs={{0,4},{1,5},{2,6},{3,7},{4,0},{5,1},{6,2},{7,3},{8,12},{9,13},{10,... | collective-permute-start | bytes 811016 | tf_op jit(solution)/shard_map/ppermute | solution.py:95
  477.2 14.5 %collective-permute-start.71 = (bf16[128,4096]{1,0:T(8,128)(2,1)}, bf16[128,4096]{1,0:T(8,128)(2,1)S(1)}, u32[]{:S(2)}, u32[]{:S(2)}) collective-permute-start(bf16[128,4096]{1,0:T(8,128)(2,1)} %pad_maximum_fusion.2.mine_ref), channel_id=1, source_target_pairs={{0,1},{1,0},{2,3},{3,2},{4,5},{5,4},{6,7},{7,6},{8,9},{9,8},{10,11... | collective-permute-start | bytes 3145736 | tf_op jit(solution)/shard_map/ppermute | solution.py:43
  (149 other events, 1564.6 us)
